TPU v7x, 32 devices: a whole 2x2x4 slice. The times are simulated.
32 devices in a mesh: dp: 8 (over y, x, core), tensor: 4 (over z).
Axes of the slice: x: 2, y: 2, z: 4, core: 2. Of those that a mesh axis runs over, the one named last changes fastest.
Arguments:
- tokens: bfloat16 [64, 577, 1024], P('dp'), may hold values from -6 to 6
- cotangent: bfloat16 [64, 577, 1024], P('dp'), may hold values from -2.09375 to 2.09375
- qkv_weight: float32 [1024, 3, 1024], P(None, None, 'tensor'), may hold values from -0.1875 to 0.1875
- qv_bias: float32 [2, 1024], P(None, 'tensor'), may hold values from -0.3 to 0.3
- proj_weight: float32 [1024, 1024], P('tensor'), may hold values from -2 to 2
- fc1_weight: float32 [1024, 4096], P(None, 'tensor'), may hold values from -0.1875 to 0.1875
- fc1_bias: float32 [4096], P('tensor'), may hold values from -3 to 3
- fc2_weight: float32 [4096, 1024], P('tensor'), may hold values from -0.25 to 0.25
- norm_gains: float32 [2, 1024], replicated, may hold values from 0.5 to 1.5
- shift_biases: float32 [4, 1024], replicated, may hold values from -1.5 to 1.5
- first_qkv_weight: float32 [1024, 3, 1024], P(None, None, 'tensor'), may hold values from -160 to 160
- first_qv_bias: float32 [2, 1024], P(None, 'tensor'), may hold values from -192 to 192
- first_proj_weight: float32 [1024, 1024], P('tensor'), may hold values from -56 to 56
- first_fc1_weight: float32 [1024, 4096], P(None, 'tensor'), may hold values from -56 to 56
- first_fc1_bias: float32 [4096], P('tensor'), may hold values from -56 to 56
- first_fc2_weight: float32 [4096, 1024], P('tensor'), may hold values from -56 to 56
- first_norm_gains: float32 [2, 1024], replicated, may hold values from -56 to 56
- first_shift_biases: float32 [4, 1024], replicated, may hold values from -56 to 56
- second_qkv_weight: float32 [1024, 3, 1024], P(None, None, 'tensor'), may hold values from 124.632 to 498.528
- second_qv_bias: float32 [2, 1024], P(None, 'tensor'), may hold values from 169.8688 to 679.4752
- second_proj_weight: float32 [1024, 1024], P('tensor'), may hold values from 3.6928 to 14.7712
- second_fc1_weight: float32 [1024, 4096], P(None, 'tensor'), may hold values from 3.6928 to 14.7712
- second_fc1_bias: float32 [4096], P('tensor'), may hold values from 3.6928 to 14.7712
- second_fc2_weight: float32 [4096, 1024], P('tensor'), may hold values from 3.6928 to 14.7712
- second_norm_gains: float32 [2, 1024], replicated, may hold values from 923.2 to 3692.8
- second_shift_biases: float32 [4, 1024], replicated, may hold values from 923.2 to 3692.8
Outputs:
- output: bfloat16 [64, 577, 1024], P('dp')
- grad_tokens: bfloat16 [64, 577, 1024], P('dp')
- grad_qkv_weight: float32 [1024, 3, 1024], P(None, None, 'tensor')
- grad_qv_bias: float32 [2, 1024], P(None, 'tensor')
- grad_proj_weight: float32 [1024, 1024], P('tensor')
- grad_fc1_weight: float32 [1024, 4096], P(None, 'tensor')
- grad_fc1_bias: float32 [4096], P('tensor')
- grad_fc2_weight: float32 [4096, 1024], P('tensor')
- grad_norm_gains: float32 [2, 1024], replicated
- grad_shift_biases: float32 [4, 1024], replicated
- new_qkv_weight: float32 [1024, 3, 1024], P(None, None, 'tensor')
- new_qv_bias: float32 [2, 1024], P(None, 'tensor')
- new_proj_weight: float32 [1024, 1024], P('tensor')
- new_fc1_weight: float32 [1024, 4096], P(None, 'tensor')
- new_fc1_bias: float32 [4096], P('tensor')
- new_fc2_weight: float32 [4096, 1024], P('tensor')
- new_norm_gains: float32 [2, 1024], replicated
- new_shift_biases: float32 [4, 1024], replicated
- new_first_qkv_weight: float32 [1024, 3, 1024], P(None, None, 'tensor')
- new_first_qv_bias: float32 [2, 1024], P(None, 'tensor')
- new_first_proj_weight: float32 [1024, 1024], P('tensor')
- new_first_fc1_weight: float32 [1024, 4096], P(None, 'tensor')
- new_first_fc1_bias: float32 [4096], P('tensor')
- new_first_fc2_weight: float32 [4096, 1024], P('tensor')
- new_first_norm_gains: float32 [2, 1024], replicated
- new_first_shift_biases: float32 [4, 1024], replicated
- new_second_qkv_weight: float32 [1024, 3, 1024], P(None, None, 'tensor')
- new_second_qv_bias: float32 [2, 1024], P(None, 'tensor')
- new_second_proj_weight: float32 [1024, 1024], P('tensor')
- new_second_fc1_weight: float32 [1024, 4096], P(None, 'tensor')
- new_second_fc1_bias: float32 [4096], P('tensor')
- new_second_fc2_weight: float32 [4096, 1024], P('tensor')
- new_second_norm_gains: float32 [2, 1024], replicated
- new_second_shift_biases: float32 [4, 1024], replicated
All inputs are finite; a program needn't handle non-finite values.
Results may differ from a plain program's by a relative error of at most 0.024.
Values may be sent and summed in bfloat16 or wider, within the bound.
No kernel may reach another device: no remote copies, remote signals or barrier semaphores. Data moves between devices by JAX's collectives and lax.ppermute only.
A program may use at most 576 MiB of HBM per device.

v0:
```python
import math

import jax
import jax.numpy as jnp
from jax import lax
from jax.sharding import PartitionSpec as P

D = 1024
HD = 64
FF = 4096
STEP = 3


NORM_EPS = 1e-05
BETA_ONE = 0.9
BETA_TWO = 0.999
ADAM_EPS = 1e-08
MATRIX_DECAY = 0.05
SQRT_HALF = 0.7071067811865476
INV_SQRT_TAU = 0.3989422804014327


def layer_norm(values_in, gain_row, shift_row):
    center = values_in - jnp.mean(values_in, axis=-1, keepdims=True)
    inv_std = lax.rsqrt(jnp.mean(center * center, axis=-1, keepdims=True) + NORM_EPS)
    normed = center * inv_std
    return (normed, inv_std, normed * gain_row + shift_row)


def norm_back(d_normed, normed, inv_std):
    return inv_std * (
        d_normed
        - jnp.mean(d_normed, axis=-1, keepdims=True)
        - normed * jnp.mean(d_normed * normed, axis=-1, keepdims=True)
    )


def gelu_slope(pre_act):
    normal_cdf = 0.5 * (1.0 + lax.erf(pre_act * SQRT_HALF))
    return normal_cdf + pre_act * jnp.exp(-0.5 * pre_act * pre_act) * INV_SQRT_TAU


def adamw(weight_old, moment_one, moment_two, grad_sum, rate_value, decay_value):
    new_one = BETA_ONE * moment_one + (1.0 - BETA_ONE) * grad_sum
    new_two = BETA_TWO * moment_two + (1.0 - BETA_TWO) * grad_sum * grad_sum
    one_hat = new_one / (1.0 - BETA_ONE**STEP)
    two_hat = new_two / (1.0 - BETA_TWO**STEP)
    new_weight = weight_old - rate_value * (
        one_hat / (jnp.sqrt(two_hat) + ADAM_EPS) + decay_value * weight_old
    )
    return (new_weight, new_one, new_two)


def layer_pass(
    tokens,
    cotangent,
    qkv_w3,
    qv_bias,
    proj_b,
    fc1_b,
    fc1_bias,
    fc2_b,
    norm_gains,
    shift_biases,
    attn_reduce,
    mlp_reduce,
    back_reduce,
    qkv_reduce,
    mlp_hook,
):
    images, seq_len, width = tokens.shape
    local_width = qkv_w3.shape[2]
    heads_dev = local_width // HD
    token_rows = images * seq_len
    score_scale = 1.0 / math.sqrt(HD)
    qkv_b = qkv_w3.reshape(width, 3 * local_width)
    x_float = tokens.reshape(token_rows, width).astype(jnp.float32)
    normed1, inv_std1, pre1 = layer_norm(x_float, norm_gains[0], shift_biases[0])
    act1 = pre1.astype(jnp.bfloat16)
    qkv = jnp.dot(act1, qkv_b, preferred_element_type=jnp.float32).reshape(
        token_rows, 3, local_width
    )
    head_shape = (images, seq_len, heads_dev, HD)
    query = (qkv[:, 0] + qv_bias[0]).astype(jnp.bfloat16).reshape(head_shape)
    keys = qkv[:, 1].astype(jnp.bfloat16).reshape(head_shape)
    values = (qkv[:, 2] + qv_bias[1]).astype(jnp.bfloat16).reshape(head_shape)
    scores = (
        jnp.einsum("bqhd,bkhd->bhqk", query, keys, preferred_element_type=jnp.float32) * score_scale
    )
    row_max = jnp.max(scores, axis=-1, keepdims=True)
    log_total = row_max + jnp.log(jnp.sum(jnp.exp(scores - row_max), axis=-1, keepdims=True))
    probs = jnp.exp(scores - log_total).astype(jnp.bfloat16)
    attended = jnp.einsum("bhqk,bkhd->bqhd", probs, values, preferred_element_type=jnp.float32)
    attended = attended.astype(jnp.bfloat16).reshape(token_rows, local_width)
    attn_out = attn_reduce(attended)
    resid = x_float + attn_out + shift_biases[2]
    normed2, inv_std2, pre2 = layer_norm(resid, norm_gains[1], shift_biases[1])
    act2 = pre2.astype(jnp.bfloat16)
    pre_act = jnp.dot(act2, fc1_b, preferred_element_type=jnp.float32) + fc1_bias
    hidden = jax.nn.gelu(pre_act, approximate=False).astype(jnp.bfloat16)
    mlp_out = mlp_reduce(hidden)
    output = (
        (resid + mlp_out + shift_biases[3]).astype(jnp.bfloat16).reshape(images, seq_len, width)
    )
    cot_rows = cotangent.reshape(token_rows, width)
    d_out = cot_rows.astype(jnp.float32)
    g_out_bias = jnp.sum(d_out, axis=0)
    d_hidden = jnp.dot(cot_rows, fc2_b.T, preferred_element_type=jnp.float32)
    g_fc2 = jnp.dot(hidden.T, cot_rows, preferred_element_type=jnp.float32)
    d_pre = d_hidden * gelu_slope(pre_act)
    g_fc1_bias = jnp.sum(d_pre, axis=0)
    d_pre_b = d_pre.astype(jnp.bfloat16)
    g_fc1 = jnp.dot(act2.T, d_pre_b, preferred_element_type=jnp.float32)
    d_act2 = back_reduce(d_pre_b)
    g_fc1, g_fc1_bias, g_fc2 = mlp_hook(g_fc1, g_fc1_bias, g_fc2)
    g_gain2 = jnp.sum(d_act2 * normed2, axis=0)
    g_shift2 = jnp.sum(d_act2, axis=0)
    d_resid = d_out + norm_back(d_act2 * norm_gains[1], normed2, inv_std2)
    g_proj_bias = jnp.sum(d_resid, axis=0)
    d_resid_b = d_resid.astype(jnp.bfloat16)
    g_proj = jnp.dot(attended.T, d_resid_b, preferred_element_type=jnp.float32)
    d_att = (
        jnp.dot(d_resid_b, proj_b.T, preferred_element_type=jnp.float32)
        .astype(jnp.bfloat16)
        .reshape(head_shape)
    )
    again = (
        jnp.einsum("bqhd,bkhd->bhqk", query, keys, preferred_element_type=jnp.float32) * score_scale
    )
    probs_f = jnp.exp(again - log_total)
    probs_b = probs_f.astype(jnp.bfloat16)
    d_values = jnp.einsum("bhqk,bqhd->bkhd", probs_b, d_att, preferred_element_type=jnp.float32)
    d_probs = jnp.einsum("bqhd,bkhd->bhqk", d_att, values, preferred_element_type=jnp.float32)
    delta = jnp.sum(probs_f * d_probs, axis=-1, keepdims=True)
    d_scores = (probs_f * (d_probs - delta) * score_scale).astype(jnp.bfloat16)
    d_query = jnp.einsum("bhqk,bkhd->bqhd", d_scores, keys, preferred_element_type=jnp.float32)
    d_keys = jnp.einsum("bhqk,bqhd->bkhd", d_scores, query, preferred_element_type=jnp.float32)
    d_query = d_query.reshape(token_rows, local_width)
    d_keys = d_keys.reshape(token_rows, local_width)
    d_values = d_values.reshape(token_rows, local_width)
    g_qv = jnp.stack([jnp.sum(d_query, axis=0), jnp.sum(d_values, axis=0)])
    d_qkv3 = jnp.stack([d_query, d_keys, d_values], axis=1).astype(jnp.bfloat16)
    g_qkv = jnp.dot(
        act1.T, d_qkv3.reshape(token_rows, 3 * local_width), preferred_element_type=jnp.float32
    ).reshape(width, 3, local_width)
    d_act1 = qkv_reduce(d_qkv3)
    g_gain1 = jnp.sum(d_act1 * normed1, axis=0)
    g_shift1 = jnp.sum(d_act1, axis=0)
    grad_tokens = (d_resid + norm_back(d_act1 * norm_gains[0], normed1, inv_std1)).astype(
        jnp.bfloat16
    )
    grad_tokens = grad_tokens.reshape(images, seq_len, width)
    g_gains = jnp.stack([g_gain1, g_gain2])
    g_shifts = jnp.stack([g_shift1, g_shift2, g_proj_bias, g_out_bias])
    return (output, grad_tokens, (g_qkv, g_qv, g_proj, g_fc1, g_fc1_bias, g_fc2, g_gains, g_shifts))


def per_device(
    tokens,
    cotangent,
    qkv_weight,
    qv_bias,
    proj_weight,
    fc1_weight,
    fc1_bias,
    fc2_weight,
    norm_gains,
    shift_biases,
    first_qkv_weight,
    first_qv_bias,
    first_proj_weight,
    first_fc1_weight,
    first_fc1_bias,
    first_fc2_weight,
    first_norm_gains,
    first_shift_biases,
    second_qkv_weight,
    second_qv_bias,
    second_proj_weight,
    second_fc1_weight,
    second_fc1_bias,
    second_fc2_weight,
    second_norm_gains,
    second_shift_biases,
):
    width = tokens.shape[2]
    qkv_w3 = qkv_weight.astype(jnp.bfloat16)
    proj_b = proj_weight.astype(jnp.bfloat16)
    fc1_b = fc1_weight.astype(jnp.bfloat16)
    fc2_b = fc2_weight.astype(jnp.bfloat16)

    def attn_reduce(attended):
        return lax.psum(
            jnp.dot(attended, proj_b, preferred_element_type=jnp.float32).astype(jnp.bfloat16),
            "tensor",
        ).astype(jnp.float32)

    def mlp_reduce(hidden):
        return lax.psum(
            jnp.dot(hidden, fc2_b, preferred_element_type=jnp.float32).astype(jnp.bfloat16),
            "tensor",
        ).astype(jnp.float32)

    def back_reduce(d_pre_b):
        return lax.psum(
            jnp.dot(d_pre_b, fc1_b.T, preferred_element_type=jnp.float32).astype(jnp.bfloat16),
            "tensor",
        ).astype(jnp.float32)

    def qkv_reduce(d_qkv3):
        rows = d_qkv3.shape[0]
        flat_left = d_qkv3.reshape(rows, -1)
        flat_right = qkv_w3.reshape(width, -1)
        return lax.psum(
            jnp.dot(flat_left, flat_right.T, preferred_element_type=jnp.float32).astype(
                jnp.bfloat16
            ),
            "tensor",
        ).astype(jnp.float32)

    def mlp_hook(g_fc1, g_fc1_bias, g_fc2):
        return (g_fc1, g_fc1_bias, g_fc2)

    output, grad_tokens, grads = layer_pass(
        tokens,
        cotangent,
        qkv_w3,
        qv_bias,
        proj_b,
        fc1_b,
        fc1_bias,
        fc2_b,
        norm_gains,
        shift_biases,
        attn_reduce,
        mlp_reduce,
        back_reduce,
        qkv_reduce,
        mlp_hook,
    )
    g_qkv, g_qv, g_proj, g_fc1, g_fc1_bias, g_fc2, g_gains, g_shifts = grads
    g_qkv, g_qv, g_proj, g_fc1, g_fc1_bias, g_fc2, g_gains, g_shifts = (
        lax.psum(g_qkv.astype(jnp.bfloat16), "dp").astype(jnp.float32),
        lax.psum(g_qv.astype(jnp.bfloat16), "dp").astype(jnp.float32),
        lax.psum(g_proj.astype(jnp.bfloat16), "dp").astype(jnp.float32),
        lax.psum(g_fc1.astype(jnp.bfloat16), "dp").astype(jnp.float32),
        lax.psum(g_fc1_bias.astype(jnp.bfloat16), "dp").astype(jnp.float32),
        lax.psum(g_fc2.astype(jnp.bfloat16), "dp").astype(jnp.float32),
        lax.psum(g_gains.astype(jnp.bfloat16), "dp").astype(jnp.float32),
        lax.psum(g_shifts.astype(jnp.bfloat16), "dp").astype(jnp.float32),
    )
    grads = (g_qkv, g_qv, g_proj, g_fc1, g_fc1_bias, g_fc2, g_gains, g_shifts)
    weights = (
        qkv_weight,
        qv_bias,
        proj_weight,
        fc1_weight,
        fc1_bias,
        fc2_weight,
        norm_gains,
        shift_biases,
    )
    firsts = (
        first_qkv_weight,
        first_qv_bias,
        first_proj_weight,
        first_fc1_weight,
        first_fc1_bias,
        first_fc2_weight,
        first_norm_gains,
        first_shift_biases,
    )
    seconds = (
        second_qkv_weight,
        second_qv_bias,
        second_proj_weight,
        second_fc1_weight,
        second_fc1_bias,
        second_fc2_weight,
        second_norm_gains,
        second_shift_biases,
    )
    rates = (
        1.2 / math.sqrt(D),
        0.6,
        0.6 / math.sqrt(max(D // 128, 1)),
        0.6 / math.sqrt(D),
        0.3,
        0.6 / math.sqrt(max(FF // 8, 1)),
        3.0,
        3.0,
    )
    decays = (MATRIX_DECAY, 0.0, MATRIX_DECAY, MATRIX_DECAY, 0.0, MATRIX_DECAY, 0.0, 0.0)
    updated = []
    for weight_old, moment_one, moment_two, grad_sum, rate_value, decay_value in zip(
        weights, firsts, seconds, grads, rates, decays
    ):
        updated.append(adamw(weight_old, moment_one, moment_two, grad_sum, rate_value, decay_value))
    return (
        output,
        grad_tokens,
        grads[0],
        grads[1],
        grads[2],
        grads[3],
        grads[4],
        grads[5],
        grads[6],
        grads[7],
        updated[0][0],
        updated[1][0],
        updated[2][0],
        updated[3][0],
        updated[4][0],
        updated[5][0],
        updated[6][0],
        updated[7][0],
        updated[0][1],
        updated[1][1],
        updated[2][1],
        updated[3][1],
        updated[4][1],
        updated[5][1],
        updated[6][1],
        updated[7][1],
        updated[0][2],
        updated[1][2],
        updated[2][2],
        updated[3][2],
        updated[4][2],
        updated[5][2],
        updated[6][2],
        updated[7][2],
    )


def solution(mesh):
    return jax.shard_map(
        per_device,
        mesh=mesh,
        in_specs=(
            P("dp", None, None),
            P("dp", None, None),
            P(None, None, "tensor"),
            P(None, "tensor"),
            P("tensor", None),
            P(None, "tensor"),
            P("tensor"),
            P("tensor", None),
            P(),
            P(),
            P(None, None, "tensor"),
            P(None, "tensor"),
            P("tensor", None),
            P(None, "tensor"),
            P("tensor"),
            P("tensor", None),
            P(),
            P(),
            P(None, None, "tensor"),
            P(None, "tensor"),
            P("tensor", None),
            P(None, "tensor"),
            P("tensor"),
            P("tensor", None),
            P(),
            P(),
        ),
        out_specs=(
            P("dp", None, None),
            P("dp", None, None),
            P(None, None, "tensor"),
            P(None, "tensor"),
            P("tensor", None),
            P(None, "tensor"),
            P("tensor"),
            P("tensor", None),
            P(),
            P(),
            P(None, None, "tensor"),
            P(None, "tensor"),
            P("tensor", None),
            P(None, "tensor"),
            P("tensor"),
            P("tensor", None),
            P(),
            P(),
            P(None, None, "tensor"),
            P(None, "tensor"),
            P("tensor", None),
            P(None, "tensor"),
            P("tensor"),
            P("tensor", None),
            P(),
            P(),
            P(None, None, "tensor"),
            P(None, "tensor"),
            P("tensor", None),
            P(None, "tensor"),
            P("tensor"),
            P("tensor", None),
            P(),
            P(),
        ),
        check_vma=False,
    )
```

profile of v0, /device:TPU:0, one launch (start us, length us, event | category | flops | bytes accessed | tf_op | source)
XLA Modules:
  0.0 2112.3 jit_solution(18283868986137072831)
XLA Ops:
  10.1 5.1 convert_reduce_fusion
  15.6 7.0 multiply_reduce_fusion.3
  26.4 10.9 add_convert_fusion.2
  37.3 12.7 copy.147
  50.0 10.3 reshape.241
  60.4 10.5 fusion.91
  75.6 5.7 copy.149
  81.3 7.1 squeeze.7
  92.5 7.3 copy.153
  99.8 5.8 copy.150
  105.6 7.1 squeeze.8
  118.9 21.2 %multiply_reduce_fusion.1 = (f32[8,4,577]{2,1,0:T(4,128)S(1)}, f32[8,4,577,577]{2,3,1,0:T(8,128)}) fusion(bf16[8,577,4,64]{1,3,2,0:T(8,128)(2,1)} %copy.153, bf16[8,577,4,64]{1,0,3,2:T(8,128)(2,1)} %add_convert_fusion.3), kind=kOutput, calls=%fused_computation.6 | convolution fusion | flops 1384966144 | bytes 47415552 | tf_op jit(solution)/shard_map/bqhd,bkhd->bhqk/dot_general | solution.py:88
  140.1 19.7 exponential_reduce_fusion
  160.5 18.5 convert_bitcast_fusion
  179.0 4.8 copy.156
  188.2 5.2 convolution_convert_fusion.2
  193.7 15.6 copy.142
  209.3 12.7 copy.157
  222.0 10.5 reshape.237
  232.5 15.2 reshape.240
  247.7 274.3 %all-reduce.8.cloned.1.call-done = bf16[4616,1024]{1,0:T(8,128)(2,1)} async-done(((bf16[4616,1024]{1,0:T(8,128)(2,1)}), bf16[4616,1024]{1,0:T(8,128)(2,1)}) %all-reduce.8.cloned.1.call-update) | async-done | bytes 9453584 | tf_op jit(solution)/shard_map/psum | solution.py:193
  522.0 16.2 fusion.128
  538.3 8.5 multiply_reduce_fusion.2
  546.8 56.7 %fusion.38 = (bf16[4616,1024]{1,0:T(8,128)(2,1)}, f32[4616,1024]{1,0:T(8,128)}) fusion(f32[1024]{0:T(1024)S(1)} %copy-done.49, f32[1024,1024]{1,0:T(8,128)} %param.31, f32[4616,1024]{1,0:T(8,128)} %get-tuple-element.223, f32[1024]{0:T(1024)S(1)} %bitcast.77, f32[1024]{0:T(1024)S(1)} %bitcast.70, f32[4616]{0:T(1024)S(1)} %add_rsqrt_fusion, ...), kind=kOutput, calls=%fused_computation.39 | convolution fusion | flops 10017103872 | bytes 51511360 | tf_op jit(solution)/shard_map/dot_general | solution.py:99
  603.6 21.5 %fusion.136 = (bf16[1024]{0:T(1024)(128)(2,1)}, bf16[4616,1024]{1,0:T(8,128)(2,1)}) fusion(f32[4616,1024]{1,0:T(8,128)} %get-tuple-element.235, f32[1024]{0:T(1024)S(1)} %copy-done.49, bf16[4616,1024]{1,0:T(8,128)(2,1)S(1)} %copy-done.2, f32[1024,1024]{1,0:T(8,128)S(1)} %copy-done.15), kind=kOutput, calls=%fused_computation.172 | convolution fusion | flops 9738222592 | bytes 42014720 | tf_op jit(solution)/shard_map/dot_general | solution.py:108
  625.1 16.2 convolution_convert_fusion
  641.3 17.4 convolution_convert_fusion.4
  658.7 23.6 %fusion.85 = bf16[1024,1024]{1,0:T(8,128)(2,1)} fusion(bf16[4616,1024]{1,0:T(8,128)(2,1)} %get-tuple-element.241, f32[4616,1024]{1,0:T(8,128)} %get-tuple-element.223, f32[1024]{0:T(1024)S(1)} %bitcast.78, f32[1024]{0:T(1024)S(1)} %bitcast.71, f32[4616]{0:T(1024)S(1)} %add_rsqrt_fusion, f32[4616]{0:T(1024)S(1)} %broadcast_multiply_fusion.4), kind=kOutput, calls=%fused_computation.111 | convolution fusion | flops 9705136128 | bytes 30502976 | tf_op jit(solution)/shard_map/dot_general | solution.py:113
  682.3 284.0 %all-reduce.10.cloned.1.call-done = bf16[4616,1024]{1,0:T(8,128)(2,1)} async-done(((bf16[4616,1024]{1,0:T(8,128)(2,1)}), bf16[4616,1024]{1,0:T(8,128)(2,1)}) %all-reduce.10.cloned.1.call-update) | async-done | bytes 9453584 | tf_op jit(solution)/shard_map/psum | solution.py:205
  966.2 15.0 fusion.29
  981.3 11.2 fusion.126
  992.5 7.4 fusion.93
  999.9 5.5 convolution_convert_fusion.3
  1005.4 8.1 reshape.248
  1013.5 7.3 copy.159
  1020.8 20.5 fusion.132
  1041.3 20.3 fusion.75
  1061.6 61.6 %fusion.72 = bf16[8,577,4,64]{1,3,2,0:T(8,128)(2,1)} fusion(f32[8,4,577,577]{2,3,1,0:T(8,128)} %fusion.75, f32[8,4,577,577]{2,3,1,0:T(8,128)} %get-tuple-element.233, f32[8,4,577]{2,1,0:T(4,128)S(1)} %bitcast.63, bf16[8,577,4,64]{1,0,3,2:T(8,128)(2,1)} %add_convert_fusion.3), kind=kOutput, calls=%fused_computation.103 | convolution fusion | flops 1459579776 | bytes 90030464 | tf_op jit(solution)/shard_map/bhqk,bqhd->bkhd/dot_general | solution.py:137
  1123.1 61.2 %fusion.133 = (bf16[4,64]{1,0:T(4,128)(2,1)S(1)}, bf16[8,577,4,64]{1,3,2,0:T(8,128)(2,1)}) fusion(bf16[8,577,4,64]{1,3,2,0:T(8,128)(2,1)S(1)} %copy-done.9, f32[8,4,577,577]{2,3,1,0:T(8,128)} %fusion.75, f32[8,4,577,577]{2,3,1,0:T(8,128)} %get-tuple-element.233, f32[8,4,577]{2,1,0:T(4,128)S(1)} %bitcast.64), kind=kOutput, calls=%fused_computation.171 | convolution fusion | flops 1461942912 | bytes 90030976 | tf_op jit(solution)/shard_map/bhqk,bkhd->bqhd/dot_general | solution.py:136
  1184.3 7.3 copy.186
  1191.6 8.0 reshape.246
  1199.6 7.3 copy.185
  1206.9 7.9 reshape.245
  1214.8 5.0 copy.184
  1219.8 6.8 reshape.244
  1226.6 13.7 fusion.88
  1240.4 17.8 convolution_convert_fusion.1
  1258.3 9.7 bitcast_convert_fusion
  1268.9 5.3 reduce.7
  1274.2 5.2 reduce.6
  1279.6 64.7 %all-reduce.12.cloned.1.call-done = (bf16[1024,3,256]{2,0,1:T(8,128)(2,1)}, bf16[256,1024]{1,0:T(8,128)(2,1)}, bf16[1024,1024]{1,0:T(8,128)(2,1)}, bf16[1024,1024]{1,0:T(8,128)(2,1)}) async-done(((bf16[1024,3,256]{2,0,1:T(8,128)(2,1)}, bf16[256,1024]{1,0:T(8,128)(2,1)}, bf16[1024,1024]{1,0:T(8,128)(2,1)}, bf16[1024,1024]{1,0:T(8,128)(2,1)}), (bf16[1024,3,256]{2,0,1:T(8,128)(2,1)}, ...) | async-done | bytes 6291472 | tf_op jit(solution)/shard_map/psum | solution.py:243
  1349.4 8.6 multiply_subtract_fusion.2
  1358.2 9.9 multiply_subtract_fusion.1
  1368.5 7.9 multiply_subtract_fusion
  1376.3 603.6 %all-reduce.14.cloned.1.call-done = (bf16[4616,1024]{1,0:T(8,128)(2,1)}, bf16[4616,1024]{1,0:T(8,128)(2,1)}) async-done(((bf16[4616,1024]{1,0:T(8,128)(2,1)}, bf16[4616,1024]{1,0:T(8,128)(2,1)}), (bf16[4616,1024]{1,0:T(8,128)(2,1)}, bf16[4616,1024]{1,0:T(8,128)(2,1)})) %all-reduce.14.cloned.1.call-update) | async-done | bytes 18907152 | tf_op jit(solution)/shard_map/psum | solution.py:199
  1979.9 5.1 reduce.5
  1985.1 14.8 fusion.35
  1999.9 18.1 fusion.33
  2018.0 10.2 reshape.239
  2028.2 12.8 copy.177
  2041.0 14.6 add_convert_fusion
  2055.6 10.2 reshape.236
  2065.9 12.9 copy.176
  2078.8 24.0 %all-reduce = (bf16[2,256]{1,0:T(2,128)(2,1)S(1)}, bf16[1024]{0:T(1024)(128)(2,1)S(1)}, bf16[2,1024]{1,0:T(2,128)(2,1)S(1)}, bf16[4,1024]{1,0:T(4,128)(2,1)S(1)}) all-reduce(bf16[2,256]{1,0:T(2,128)(2,1)S(1)} %pad_maximum_fusion.2, bf16[1024]{0:T(1024)(128)(2,1)S(1)} %copy-done.56, ...), channel_id=1, replica_groups=mesh['dp'=8,'tensor'=4] {'dp'}, use_global_device_ids=true, to_apply=%region_18.0 | all-reduce | flops 7680 | bytes 30720 | tf_op jit(solution)/shard_map/psum | solution.py:244
  (171 shorter events, 37.0 us)
Async XLA Ops:
  7.2 514.8 %all-reduce.8.cloned.1.call-start = ((), (), s32[]{:S(2)}) async-start(), calls=%async_computation | async-start | bytes 18907136 | tf_op jit(solution)/shard_map/psum | solution.py:193
  8.6 17.8 copy-start.35
  10.1 14.5 copy-start.7
  15.4 21.9 %copy-start.30 = (f32[8,577]{1,0:T(8,128)}, f32[8,577]{1,0:T(8,128)S(1)}, u32[]{:S(2)}) copy-start(f32[8,577]{1,0:T(8,128)S(1)} %broadcast_multiply_fusion.5) | copy-start | bytes 55396
  23.7 13.6 copy-start.32
  50.0 10.3 copy-start.26
  71.2 4.3 copy-start.47
  112.7 4.0 copy-start.6
  116.7 43.1 %copy-start.3 = (bf16[8,577,4,64]{1,0,3,2:T(8,128)(2,1)}, bf16[8,577,4,64]{1,0,3,2:T(8,128)(2,1)S(1)}, u32[]{:S(2)}) copy-start(bf16[8,577,4,64]{1,0,3,2:T(8,128)(2,1)S(1)} %add_convert_fusion.4) | copy-start | bytes 7090180
  159.8 0.6 copy-start.28
  179.0 9.2 copy-start.10
  188.2 5.2 copy-start.5
  193.4 772.8 %all-reduce.10.cloned.1.call-start = ((), (), s32[]{:S(2)}) async-start(), calls=%async_computation.1 | async-start | bytes 18907136 | tf_op jit(solution)/shard_map/psum | solution.py:205
  232.5 289.5 %copy-start.40 = (f32[1,1024]{1,0:T(1,128)S(1)}, f32[1,1024]{1,0:T(1,128)}, u32[]{:S(2)}) copy-start(f32[1,1024]{1,0:T(1,128)} %get-tuple-element.228) | copy-start | bytes 12292
  538.2 8.5 copy-start.37
  538.2 8.5 copy-start.49
  538.2 8.5 copy-start.53
  546.8 56.8 %copy-start.2 = (bf16[4616,1024]{1,0:T(8,128)(2,1)S(1)}, bf16[4616,1024]{1,0:T(8,128)(2,1)}, u32[]{:S(2)}) copy-start(bf16[4616,1024]{1,0:T(8,128)(2,1)} %reshape.237) | copy-start | bytes 28360708
  546.8 56.8 %copy-start.15 = (f32[1024,1024]{1,0:T(8,128)S(1)}, f32[1024,1024]{1,0:T(8,128)}, u32[]{:S(2)}) copy-start(f32[1024,1024]{1,0:T(8,128)} %param.33) | copy-start | bytes 12582916
  603.6 21.5 %copy-start.11 = (f32[1024,1024]{1,0:T(8,128)S(1)}, f32[1024,1024]{1,0:T(8,128)}, u32[]{:S(2)}) copy-start(f32[1024,1024]{1,0:T(8,128)} %param.31) | copy-start | bytes 12582916
  641.3 703.0 %all-reduce.12.cloned.1.call-start = ((), (), s32[]{:S(2)}) async-start(), calls=%async_computation.2 | async-start | bytes 12582912 | tf_op jit(solution)/shard_map/psum | solution.py:243
  966.2 15.1 copy-start.1
  992.5 7.4 copy-start
  1005.4 15.4 copy-start.29
  1020.8 20.5 copy-start.4
  1061.6 61.6 %copy-start.9 = (bf16[8,577,4,64]{1,3,2,0:T(8,128)(2,1)S(1)}, bf16[8,577,4,64]{1,3,2,0:T(8,128)(2,1)}, u32[]{:S(2)}) copy-start(bf16[8,577,4,64]{1,3,2,0:T(8,128)(2,1)} %copy.153) | copy-start | bytes 7090180
  1191.6 23.2 %copy-start.21 = (bf16[8,577,4,64]{1,3,2,0:T(8,128)(2,1)S(1)}, bf16[8,577,4,64]{1,3,2,0:T(8,128)(2,1)}, u32[]{:S(2)}) copy-start(bf16[8,577,4,64]{1,3,2,0:T(8,128)(2,1)} %get-tuple-element.239) | copy-start | bytes 7090180
  1226.6 13.7 copy-start.24
  1240.3 17.9 copy-start.22
  1240.3 739.5 %all-reduce.14.cloned.1.call-start = ((), (), s32[]{:S(2)}) async-start(), calls=%async_computation.3 | async-start | bytes 37814272 | tf_op jit(solution)/shard_map/psum | solution.py:199
  1240.4 17.9 copy-start.23
  1240.4 17.9 copy-start.25
  1240.4 17.8 copy-start.27
  1267.9 0.7 copy-start.31
  1267.9 0.8 copy-start.33
  1268.8 10.6 copy-start.44
  1268.9 10.6 copy-start.43
  1274.2 74.6 %copy-start.8 = (f32[1024,3,256]{2,0,1:T(8,128)S(1)}, f32[1024,3,256]{2,0,1:T(8,128)}, u32[]{:S(2)}) copy-start(f32[1024,3,256]{2,0,1:T(8,128)} %param.28) | copy-start | bytes 9437188
  1344.3 4.5 copy-start.19
  1344.3 5.1 copy-start.20
  1349.3 8.6 copy-start.12
  1349.4 8.6 copy-start.13
  1349.4 8.8 copy-start.14
  1358.1 9.9 copy-start.16
  1358.1 9.9 copy-start.17
  1358.1 10.3 copy-start.18
  1376.3 608.7 %copy-start.36 = (f32[1,1024]{1,0:T(1,128)S(1)}, f32[1,1024]{1,0:T(1,128)}, u32[]{:S(2)}) copy-start(f32[1,1024]{1,0:T(1,128)} %copy-done.35) | copy-start | bytes 12292
  1979.9 20.0 slice-start
  1985.0 14.8 slice-start.1
  1985.1 14.8 slice-start.2
  2028.2 12.8 copy-start.39
  2065.8 13.1 copy-start.56
  2065.8 37.1 %copy-start.48 = (f32[2,256]{1,0:T(2,128)S(1)}, f32[2,256]{1,0:T(2,128)}, u32[]{:S(2)}) copy-start(f32[2,256]{1,0:T(2,128)} %param.29) | copy-start | bytes 6148
  2065.8 37.1 %copy-start.54 = (f32[2,256]{1,0:T(2,128)S(1)}, f32[2,256]{1,0:T(2,128)}, u32[]{:S(2)}) copy-start(f32[2,256]{1,0:T(2,128)} %param.37) | copy-start | bytes 6148
  2065.8 37.1 %copy-start.55 = (f32[2,256]{1,0:T(2,128)S(1)}, f32[2,256]{1,0:T(2,128)}, u32[]{:S(2)}) copy-start(f32[2,256]{1,0:T(2,128)} %param.45) | copy-start | bytes 6148
  2065.8 37.7 %copy-start.50 = (f32[1024]{0:T(1024)S(1)}, f32[1024]{0:T(1024)}, u32[]{:S(2)}) copy-start(f32[1024]{0:T(1024)} %param.32) | copy-start | bytes 12292
  2065.8 37.7 %copy-start.51 = (f32[1024]{0:T(1024)S(1)}, f32[1024]{0:T(1024)}, u32[]{:S(2)}) copy-start(f32[1024]{0:T(1024)} %param.40) | copy-start | bytes 12292
  2065.8 37.7 %copy-start.52 = (f32[1024]{0:T(1024)S(1)}, f32[1024]{0:T(1024)}, u32[]{:S(2)}) copy-start(f32[1024]{0:T(1024)} %param.48) | copy-start | bytes 12292
  2065.8 38.3 %copy-start.38 = (f32[2,1024]{1,0:T(2,128)S(1)}, f32[2,1024]{1,0:T(2,128)}, u32[]{:S(2)}) copy-start(f32[2,1024]{1,0:T(2,128)} %param.34) | copy-start | bytes 24580
  2065.8 38.3 %copy-start.45 = (f32[2,1024]{1,0:T(2,128)S(1)}, f32[2,1024]{1,0:T(2,128)}, u32[]{:S(2)}) copy-start(f32[2,1024]{1,0:T(2,128)} %param.42) | copy-start | bytes 24580
  2065.9 38.3 %copy-start.46 = (f32[2,1024]{1,0:T(2,128)S(1)}, f32[2,1024]{1,0:T(2,128)}, u32[]{:S(2)}) copy-start(f32[2,1024]{1,0:T(2,128)} %param.50) | copy-start | bytes 24580
  2065.9 38.9 %copy-start.34 = (f32[4,1024]{1,0:T(4,128)S(1)}, f32[4,1024]{1,0:T(4,128)}, u32[]{:S(2)}) copy-start(f32[4,1024]{1,0:T(4,128)} %param.35) | copy-start | bytes 49156
  2065.9 38.9 %copy-start.41 = (f32[4,1024]{1,0:T(4,128)S(1)}, f32[4,1024]{1,0:T(4,128)}, u32[]{:S(2)}) copy-start(f32[4,1024]{1,0:T(4,128)} %param.43) | copy-start | bytes 49156
  2065.9 38.9 %copy-start.42 = (f32[4,1024]{1,0:T(4,128)S(1)}, f32[4,1024]{1,0:T(4,128)}, u32[]{:S(2)}) copy-start(f32[4,1024]{1,0:T(4,128)} %param.51) | copy-start | bytes 49156
Sparse Core Ops, SparseCore 0:
  193.6 328.3 all-reduce.7
  641.4 324.7 all-reduce.9
  1240.5 103.7 all-reduce.11
  1347.5 632.3 all-reduce.13
where the time goes:
time: 2120 us; the launch traced here: 2110 us
  waiting for transfers between devices  1230 us (58%)
  matrix products  408 us (19%)
  local copies, waits for them, and re-layouts  243 us (11%)
  other arithmetic  195 us (9%)
  blocking collectives  24 us (1%)
    psum x1, waiting for transfers between devices, mlp_reduce(): lax.psum(jnp.dot(hidden, fc2_b, preferred_element_type=jnp.float32).astyp...  604 us
    psum x1, waiting for transfers between devices, back_reduce(): lax.psum(jnp.dot(d_pre_b, fc1_b.T, preferred_element_type=jnp.float32).as...  284 us
    psum x1, waiting for transfers between devices, attn_reduce(): lax.psum(jnp.dot(attended, proj_b, preferred_element_type=jnp.float32).as...  274 us
    psum x1, waiting for transfers between devices, per_device(): lax.psum(g_qkv.astype(jnp.bfloat16), 'dp').astype(jnp.float32)  64.7 us
    dot_general x1, matrix products, layer_pass(): jnp.einsum('bhqk,bqhd->bkhd', d_scores, query, preferred_element_type=jnp...  61.6 us
    dot_general x1, matrix products, layer_pass(): jnp.einsum('bhqk,bkhd->bqhd', d_scores, keys, preferred_element_type=jnp....  61.2 us
    dot_general x1, matrix products, layer_pass(): jnp.dot(act2, fc1_b, preferred_element_type=jnp.float32) + fc1_bias  56.7 us
    unnamed x124, local copies, waits for them, and re-layouts  44 us
  transfers between devices with their start and end apart: 4, of which 4 were waited for; matrix products, arithmetic and copies ran while one was open for 8% of the time, Pallas kernels for 0%

commit v1 on v0

v1 whole, which is shorter than its diff:
```python
import math

import jax
import jax.numpy as jnp
from jax import lax
from jax.experimental import pallas as pl
from jax.experimental.pallas import tpu as pltpu
from jax.sharding import PartitionSpec as P

D = 1024
FF = 4096
STEP = 3


NORM_EPS = 1e-05
BETA_ONE = 0.9
BETA_TWO = 0.999
ADAM_EPS = 1e-08
MATRIX_DECAY = 0.05
SQRT_HALF = 0.7071067811865476
INV_SQRT_TAU = 0.3989422804014327


def layer_norm(values_in, gain_row, shift_row):
    center = values_in - jnp.mean(values_in, axis=-1, keepdims=True)
    inv_std = lax.rsqrt(jnp.mean(center * center, axis=-1, keepdims=True) + NORM_EPS)
    normed = center * inv_std
    return (normed, inv_std, normed * gain_row + shift_row)


def norm_back(d_normed, normed, inv_std):
    return inv_std * (
        d_normed
        - jnp.mean(d_normed, axis=-1, keepdims=True)
        - normed * jnp.mean(d_normed * normed, axis=-1, keepdims=True)
    )


def gelu_slope(pre_act):
    normal_cdf = 0.5 * (1.0 + lax.erf(pre_act * SQRT_HALF))
    return normal_cdf + pre_act * jnp.exp(-0.5 * pre_act * pre_act) * INV_SQRT_TAU


def adamw(weight_old, moment_one, moment_two, grad_sum, rate_value, decay_value):
    new_one = BETA_ONE * moment_one + (1.0 - BETA_ONE) * grad_sum
    new_two = BETA_TWO * moment_two + (1.0 - BETA_TWO) * grad_sum * grad_sum
    one_hat = new_one / (1.0 - BETA_ONE**STEP)
    two_hat = new_two / (1.0 - BETA_TWO**STEP)
    new_weight = weight_old - rate_value * (
        one_hat / (jnp.sqrt(two_hat) + ADAM_EPS) + decay_value * weight_old
    )
    return (new_weight, new_one, new_two)


HD=64
LOG2E=1.4426950408889634
NT=(((1,),(1,)),((),()))
NN=(((1,),(0,)),((),()))
TN=(((0,),(0,)),((),()))

def dot(a,b,dims):
    return lax.dot_general(a,b,dims,preferred_element_type=jnp.float32)

def attn_fwd_kernel(qkv_ref, out_ref):
    seq=qkv_ref.shape[1]
    lane=lax.broadcasted_iota(jnp.int32,(seq,2*HD),1)
    low=lane<HD
    for p in range(2):
        q=qkv_ref[0,:,p*128:(p+1)*128]
        k=qkv_ref[0,:,256+p*128:256+(p+1)*128]
        v=qkv_ref[0,:,512+p*128:512+(p+1)*128]
        outs=[]
        for h in range(2):
            qm=jnp.where(low if h==0 else ~low, q, jnp.zeros_like(q))
            s=dot(qm,k,NT)*(0.125*LOG2E)
            m=jnp.max(s,axis=1,keepdims=True)
            e=jnp.exp2(s-m)
            l=jnp.sum(e,axis=1,keepdims=True)
            o=dot(e.astype(jnp.bfloat16),v,NN)
            outs.append(o/l)
        out_ref[0,:,p*128:(p+1)*128]=jnp.where(low,outs[0],outs[1]).astype(jnp.bfloat16)

def attn_bwd_kernel(qkv_ref, do_ref, dqkv_ref, sums_ref):
    seq=qkv_ref.shape[1]
    lane=lax.broadcasted_iota(jnp.int32,(seq,2*HD),1)
    low=lane<HD
    for p in range(2):
        q=qkv_ref[0,:,p*128:(p+1)*128]
        k=qkv_ref[0,:,256+p*128:256+(p+1)*128]
        v=qkv_ref[0,:,512+p*128:512+(p+1)*128]
        do=do_ref[0,:,p*128:(p+1)*128]
        dqs=[];dks=[];dvs=[]
        for h in range(2):
            sel=low if h==0 else ~low
            km=jnp.where(sel,k,jnp.zeros_like(k))
            vm=jnp.where(sel,v,jnp.zeros_like(v))
            st=dot(km,q,NT)*(0.125*LOG2E)
            m=jnp.max(st,axis=0,keepdims=True)
            e=jnp.exp2(st-m)
            r=1.0/jnp.sum(e,axis=0,keepdims=True)
            pt=e*r
            dp=dot(vm,do,NT)
            delta=jnp.sum(pt*dp,axis=0,keepdims=True)
            ds=(pt*((dp-delta)*0.125)).astype(jnp.bfloat16)
            dvs.append(dot(pt.astype(jnp.bfloat16),do,NN))
            dks.append(dot(ds,q,NN))
            dqs.append(dot(ds,k,TN))
        dq=jnp.where(low,dqs[0],dqs[1]); dk=jnp.where(low,dks[0],dks[1]); dv=jnp.where(low,dvs[0],dvs[1])
        dqkv_ref[0,:,p*128:(p+1)*128]=dq.astype(jnp.bfloat16)
        dqkv_ref[0,:,256+p*128:256+(p+1)*128]=dk.astype(jnp.bfloat16)
        dqkv_ref[0,:,512+p*128:512+(p+1)*128]=dv.astype(jnp.bfloat16)
        sums_ref[0,0,0:1,p*128:(p+1)*128]=jnp.sum(dq,axis=0,keepdims=True)
        sums_ref[0,0,1:2,p*128:(p+1)*128]=jnp.sum(dv,axis=0,keepdims=True)

def attn_fwd(qkv):
    n,seq,w=qkv.shape
    g=w//768
    return pl.pallas_call(attn_fwd_kernel,grid=(n,g),
        in_specs=[pl.BlockSpec((1,seq,768),lambda i,t:(i,0,t))],
        out_specs=pl.BlockSpec((1,seq,256),lambda i,t:(i,0,t)),
        out_shape=jax.ShapeDtypeStruct((n,seq,g*256),jnp.bfloat16),
        compiler_params=pltpu.CompilerParams(vmem_limit_bytes=56*2**20),name="attn_fwd",
        cost_estimate=pl.CostEstimate(flops=n*g*4*4*seq*seq*64*4,bytes_accessed=n*seq*(w+g*256)*2,transcendentals=n*g*4*seq*seq))(qkv)

def attn_bwd(qkv,do):
    n,seq,w=qkv.shape
    g=w//768
    return pl.pallas_call(attn_bwd_kernel,grid=(n,g),
        in_specs=[pl.BlockSpec((1,seq,768),lambda i,t:(i,0,t)),pl.BlockSpec((1,seq,256),lambda i,t:(i,0,t))],
        out_specs=[pl.BlockSpec((1,seq,768),lambda i,t:(i,0,t)),pl.BlockSpec((1,1,2,256),lambda i,t:(i,t,0,0))],
        out_shape=[jax.ShapeDtypeStruct((n,seq,w),jnp.bfloat16),jax.ShapeDtypeStruct((n,g,2,256),jnp.float32)],
        compiler_params=pltpu.CompilerParams(vmem_limit_bytes=56*2**20),name="attn_bwd",
        cost_estimate=pl.CostEstimate(flops=n*g*4*10*seq*seq*64*4,bytes_accessed=n*seq*(w+g*256)*4,transcendentals=n*g*4*seq*seq))(qkv,do)

def matmul(left, right):
    return lax.dot_general(left, right, (((left.ndim - 1,), (0,)), ((), ())), preferred_element_type=jnp.float32)


def matmul_t(left, right):
    return lax.dot_general(left, right, (((left.ndim - 1,), (1,)), ((), ())), preferred_element_type=jnp.float32)


def weight_grad(left, right):
    return lax.dot_general(left, right, (((0, 1), (0, 1)), ((), ())), preferred_element_type=jnp.float32)


def per_device(*args):
    tokens, cotangent = args[0], args[1]
    weights, firsts, seconds = args[2:10], args[10:18], args[18:26]
    qkv_weight, qv_bias, proj_weight, fc1_weight, fc1_bias, fc2_weight, norm_gains, shift_biases = weights
    n_t = lax.axis_size("tensor")
    n_dp = lax.axis_size("dp")
    t_at = lax.axis_index("tensor")
    dp_at = lax.axis_index("dp")
    width = tokens.shape[2]
    own = tokens.shape[0] // n_t
    x = lax.dynamic_slice_in_dim(tokens, t_at * own, own, 0)
    cot = lax.dynamic_slice_in_dim(cotangent, t_at * own, own, 0)

    def full_weight(shard):
        rows = shard.shape[0] // n_dp
        piece = lax.dynamic_slice_in_dim(shard, dp_at * rows, rows, 0).astype(jnp.bfloat16)
        return lax.all_gather(piece, ("tensor", "dp"), axis=0, tiled=True)

    lw = qkv_weight.shape[2]
    qkv_w = full_weight(qkv_weight.reshape(width, 3 * lw)).reshape(n_t, width, 3 * lw)
    proj_w = full_weight(proj_weight)
    fc1_w = full_weight(fc1_weight).reshape(n_t, width, fc1_weight.shape[1])
    fc2_w = full_weight(fc2_weight)
    small = jnp.concatenate([qv_bias.reshape(-1), fc1_bias])
    small = lax.all_gather(small, "tensor", axis=0, tiled=False)
    qv_all = small[:, : 2 * lw].reshape(n_t, 2, lw)
    b1_all = small[:, 2 * lw :].reshape(-1)

    x_float = x.astype(jnp.float32)
    normed1, inv_std1, pre1 = layer_norm(x_float, norm_gains[0], shift_biases[0])
    act1 = pre1.astype(jnp.bfloat16)
    qkv_bias = jnp.stack([qv_all[:, 0], jnp.zeros_like(qv_all[:, 0]), qv_all[:, 1]], axis=1).reshape(n_t, 3 * lw)
    qkv = jnp.concatenate(
        [(matmul(act1, qkv_w[t]) + qkv_bias[t]).astype(jnp.bfloat16) for t in range(n_t)], axis=2
    )
    attended = attn_fwd(qkv)
    resid = x_float + matmul(attended, proj_w) + shift_biases[2]
    normed2, inv_std2, pre2 = layer_norm(resid, norm_gains[1], shift_biases[1])
    act2 = pre2.astype(jnp.bfloat16)
    pre_act = jnp.concatenate([matmul(act2, fc1_w[t]) for t in range(n_t)], axis=2) + b1_all
    normal_cdf = 0.5 * (1.0 + lax.erf(pre_act * SQRT_HALF))
    hidden = (pre_act * normal_cdf).astype(jnp.bfloat16)
    slope = (normal_cdf + pre_act * jnp.exp(-0.5 * pre_act * pre_act) * INV_SQRT_TAU).astype(jnp.bfloat16)
    out_own = (resid + matmul(hidden, fc2_w) + shift_biases[3]).astype(jnp.bfloat16)
    output = lax.all_gather(out_own, "tensor", axis=0, tiled=True)

    def reduce_grad(full):
        rows = full.shape[1] // n_dp
        parts = full.reshape(n_t, n_dp, rows, full.shape[2]).transpose(1, 0, 2, 3).astype(jnp.bfloat16)
        part = lax.psum_scatter(parts, "dp", scatter_dimension=0, tiled=False)
        part = lax.psum_scatter(part, "tensor", scatter_dimension=0, tiled=False)
        return lax.all_gather(part, "dp", axis=0, tiled=True).astype(jnp.float32)

    d_out = cot.astype(jnp.float32)
    g_out_bias = jnp.sum(d_out, axis=(0, 1))
    d_pre = matmul_t(cot, fc2_w) * slope.astype(jnp.float32)
    g_fc1_bias = jnp.sum(d_pre, axis=(0, 1))
    d_pre_b = d_pre.astype(jnp.bfloat16)
    g_fc2 = reduce_grad(weight_grad(hidden, cot).reshape(n_t, -1, width))
    fw = fc1_w.shape[2]
    g_fc1 = reduce_grad(
        jnp.stack([weight_grad(act2, d_pre_b[:, :, t * fw : (t + 1) * fw]) for t in range(n_t)])
    )
    d_act2 = sum(matmul_t(d_pre_b[:, :, t * fw : (t + 1) * fw], fc1_w[t]) for t in range(n_t))
    g_gain2 = jnp.sum(d_act2 * normed2, axis=(0, 1))
    g_shift2 = jnp.sum(d_act2, axis=(0, 1))
    d_resid = d_out + norm_back(d_act2 * norm_gains[1], normed2, inv_std2)
    g_proj_bias = jnp.sum(d_resid, axis=(0, 1))
    d_resid_b = d_resid.astype(jnp.bfloat16)
    g_proj = reduce_grad(weight_grad(attended, d_resid_b).reshape(n_t, -1, width))
    d_att = matmul_t(d_resid_b, proj_w).astype(jnp.bfloat16)
    d_qkv, qkv_sums = attn_bwd(qkv, d_att)
    g_qv = jnp.sum(qkv_sums, axis=0)
    g_qkv = reduce_grad(
        jnp.stack([weight_grad(act1, d_qkv[:, :, t * 3 * lw : (t + 1) * 3 * lw]) for t in range(n_t)])
    ).reshape(width, 3, lw)
    d_act1 = sum(matmul_t(d_qkv[:, :, t * 3 * lw : (t + 1) * 3 * lw], qkv_w[t]) for t in range(n_t))
    g_gain1 = jnp.sum(d_act1 * normed1, axis=(0, 1))
    g_shift1 = jnp.sum(d_act1, axis=(0, 1))
    gt_own = (d_resid + norm_back(d_act1 * norm_gains[0], normed1, inv_std1)).astype(jnp.bfloat16)
    grad_tokens = lax.all_gather(gt_own, "tensor", axis=0, tiled=True)

    vecs = jnp.concatenate(
        [
            g_qv.reshape(-1),
            g_fc1_bias,
            g_gain1,
            g_gain2,
            g_shift1,
            g_shift2,
            g_proj_bias,
            g_out_bias,
        ]
    )
    vecs = lax.psum(vecs, ("dp", "tensor"))
    g_qv = lax.dynamic_index_in_dim(vecs[: 2 * width].reshape(n_t, 2, lw), t_at, 0, keepdims=False)
    g_fc1_bias = lax.dynamic_slice_in_dim(vecs, 2 * width + t_at * fw, fw, 0)
    rest = vecs[2 * width + n_t * fw :].reshape(6, width)
    grads = (g_qkv, g_qv, g_proj, g_fc1, g_fc1_bias, g_fc2, rest[:2], rest[2:])
    rates = (
        1.2 / math.sqrt(D),
        0.6,
        0.6 / math.sqrt(max(D // 128, 1)),
        0.6 / math.sqrt(D),
        0.3,
        0.6 / math.sqrt(max(FF // 8, 1)),
        3.0,
        3.0,
    )
    decays = (MATRIX_DECAY, 0.0, MATRIX_DECAY, MATRIX_DECAY, 0.0, MATRIX_DECAY, 0.0, 0.0)
    updated = [adamw(*leaf) for leaf in zip(weights, firsts, seconds, grads, rates, decays)]
    return (
        output,
        grad_tokens,
        *grads,
        *(u[0] for u in updated),
        *(u[1] for u in updated),
        *(u[2] for u in updated),
    )


def solution(mesh):
    weights = (
        P(None, None, "tensor"),
        P(None, "tensor"),
        P("tensor", None),
        P(None, "tensor"),
        P("tensor"),
        P("tensor", None),
        P(),
        P(),
    )
    images = (P("dp", None, None), P("dp", None, None))
    return jax.shard_map(
        per_device,
        mesh=mesh,
        in_specs=images + weights * 3,
        out_specs=images + weights * 4,
        check_vma=False,
    )
```

time: 2120 us -> 1280 us (0.60)
  waiting for transfers between devices: 1230 us -> 741 us
  matrix products: 408 us -> 213 us
  local copies, waits for them, and re-layouts: 243 us -> 93 us
  other arithmetic: 195 us -> 69.9 us
  Pallas kernels: 0 us -> 75.8 us
  blocking collectives: 24 us -> 64.9 us
    psum x4 -> x0, waiting for transfers between devices: 1230 us -> none  [the longest x1 604 us: mlp_reduce(): lax.psum(jnp.dot(hidden, fc2_b, preferred_element_type=jnp.float32).astyp...]
    all_gather x0 -> x9, waiting for transfers between devices: none -> 514 us  [the longest x4 181 us: full_weight(): return lax.all_gather(piece, ('tensor', 'dp'), axis=0, tiled=True)]
    reduce_scatter x0 -> x8, waiting for transfers between devices: none -> 226 us  [the longest x4 200 us: reduce_grad(): part = lax.psum_scatter(parts, 'dp', scatter_dimension=0, tiled=False)]
    dot_general x18 -> x30, matrix products: 408 us -> 213 us  [the longest x10 95.2 us: matmul_t(): lax.dot_general(left, right, (((left.ndim - 1,), (1,)), ((), ())), prefer...]
    pallas_call x0 -> x2, Pallas kernels: none -> 75.8 us  [the longest x1 50.9 us: attn_bwd(): pl.pallas_call(attn_bwd_kernel, grid=(n, g), in_specs=[pl.BlockSpec((1, s...]
    reduce_sum x7 -> x2, other arithmetic: 76.3 us -> 4.67 us  [the longest x1 4.65 us: per_device(): g_proj_bias = jnp.sum(d_resid, axis=(0, 1))]
    convert_element_type x7 -> x5, local copies, waits for them, and re-layouts: 70.2 us -> 15 us  [the longest x2 9.87 us: reduce_grad(): full.reshape(n_t, n_dp, rows, full.shape[2]).transpose(1, 0, 2, 3)]
    reshape x6 -> x1, local copies, waits for them, and re-layouts: 50.6 us -> 0.02 us  [per_device(): qv_all = small[:, :2 * lw].reshape(n_t, 2, lw)]
  transfers between devices with their start and end apart: 4 -> 17, of which waited for: 4 -> 13; matrix products, arithmetic and copies ran while one was open for 8% -> 19% of each run, Pallas kernels for 0% -> 2%
where the time goes in v1:
time: 1280 us; the launch traced here: 1270 us
  waiting for transfers between devices  741 us (58%)
  matrix products  213 us (17%)
  local copies, waits for them, and re-layouts  93 us (7%)
  Pallas kernels  75.8 us (6%)
  other arithmetic  69.9 us (5%)
  blocking collectives  64.9 us (5%)
  between operations  15.3 us (1%)
    reduce_scatter x4, waiting for transfers between devices, reduce_grad(): part = lax.psum_scatter(parts, 'dp', scatter_dimension=0, tiled=False)  200 us
    all_gather x4, waiting for transfers between devices, full_weight(): return lax.all_gather(piece, ('tensor', 'dp'), axis=0, tiled=True)  181 us
    all_gather x1, waiting for transfers between devices, per_device(): grad_tokens = lax.all_gather(gt_own, 'tensor', axis=0, tiled=True)  156 us
    all_gather x1, waiting for transfers between devices, per_device(): output = lax.all_gather(out_own, 'tensor', axis=0, tiled=True)  142 us
    dot_general x10, matrix products, matmul_t(): lax.dot_general(left, right, (((left.ndim - 1,), (1,)), ((), ())), prefer...  95.2 us
    dot_general x10, matrix products, weight_grad(): lax.dot_general(left, right, (((0, 1), (0, 1)), ((), ())), preferred_elem...  60.9 us
    dot_general x10, matrix products, matmul(): lax.dot_general(left, right, (((left.ndim - 1,), (0,)), ((), ())), prefer...  57.3 us
    unnamed x139, local copies, waits for them, and re-layouts  53.1 us
  transfers between devices with their start and end apart: 17, of which 13 were waited for; matrix products, arithmetic and copies ran while one was open for 19% of the time, Pallas kernels for 2%

profile of v1, /device:TPU:0, one launch (start us, length us, event | category | flops | bytes accessed | tf_op | source)
XLA Modules:
  0.0 1273.6 jit_solution(5333653234068204471)
XLA Ops:
  16.3 14.8 %all-gather.5 = f32[4,1,1536]{2,1,0:T(1,128)S(1)} all-gather(f32[1,1,1536]{2,1,0:T(1,128)S(1)} %reshape.239), channel_id=2, replica_groups=mesh['dp'=8,'tensor'=4] {'tensor'}, dimensions={0}, use_global_device_ids=true | all-gather | bytes 30720 | tf_op jit(solution)/shard_map/all_gather | solution.py:171
  31.4 6.2 constant_dynamic-slice_fusion.2
  39.9 7.6 constant_dynamic-slice_fusion
  47.5 36.4 %all-gather.16.cloned.1.call-done = bf16[4096,768]{1,0:T(8,128)(2,1)} async-done(((bf16[128,768]{1,0:T(8,128)(2,1)}), bf16[4096,768]{1,0:T(8,128)(2,1)}) %all-gather.16.cloned.1.call-update) | async-done | bytes 6291472 | tf_op jit(solution)/shard_map/all_gather | solution.py:163
  83.9 4.8 add_convert_fusion.2
  88.6 3.0 add_convert_fusion.3
  97.8 4.1 pad_maximum_fusion.qkv_ref
  101.9 24.8 %attn_fwd.1 = bf16[2,577,1024]{2,1,0:T(8,128)(2,1)} custom-call(bf16[2,577,3072]{2,1,0:T(8,128)(2,1)} %pad_maximum_fusion.qkv_ref), custom_call_target="tpu_custom_call" | custom-call | flops 10909417472 | bytes 9453568 | tf_op jit(solution)/shard_map/attn_fwd/pallas_call | solution.py:118
  126.7 15.5 %all-gather.18.cloned.1.call-done = bf16[1024,1024]{1,0:T(8,128)(2,1)} async-done(((bf16[32,1024]{1,0:T(8,128)(2,1)}), bf16[1024,1024]{1,0:T(8,128)(2,1)}) %all-gather.18.cloned.1.call-update) | async-done | bytes 2097168 | tf_op jit(solution)/shard_map/all_gather | solution.py:163
  142.2 5.8 fusion.102
  150.9 71.1 %all-gather.20.cloned.1.call-done = bf16[4096,1024]{1,0:T(8,128)(2,1)} async-done(((bf16[128,1024]{1,0:T(8,128)(2,1)}), bf16[4096,1024]{1,0:T(8,128)(2,1)}) %all-gather.20.cloned.1.call-update) | async-done | bytes 8388624 | tf_op jit(solution)/shard_map/all_gather | solution.py:163
  222.0 6.0 fusion.56
  228.0 4.3 fusion.55
  232.3 4.3 fusion.54
  236.6 6.2 fusion.53
  242.8 58.6 %all-gather.22.cloned.1.call-done = bf16[4096,1024]{1,0:T(8,128)(2,1)} async-done(((bf16[128,1024]{1,0:T(8,128)(2,1)}), bf16[4096,1024]{1,0:T(8,128)(2,1)}) %all-gather.22.cloned.1.call-update) | async-done | bytes 8388624 | tf_op jit(solution)/shard_map/all_gather | solution.py:163
  301.4 33.8 %fusion.5 = (f32[4096]{0:T(1024)}, bf16[2,577,4096]{2,1,0:T(8,128)(2,1)}, bf16[2,577,4096]{2,1,0:T(8,128)(2,1)}, f32[2,577,4096]{2,1,0:T(8,128)}) fusion(f32[4096]{0:T(1024)S(1)} %bitcast.202, f32[2,577,1024]{2,1,0:T(8,128)} %fusion.56, f32[2,577,1024]{2,1,0:T(8,128)} %fusion.55, f32[2,577,1024]{2,1,0:T(8,128)} %fusion.54, f32[2,577,1024]{2,1,0:T(8,128)} %fusion.53, ...), kind=kOutput, calls=%fused_computation.11 | convolution fusion | flops 9765531648 | bytes 67506176 | tf_op jit(solution)/shard_map/dot_general | solution.py:140
  335.1 10.2 fusion.6
  345.4 7.5 fusion.33
  352.9 6.0 fusion.36
  358.9 6.0 fusion.39
  364.9 9.7 multiply_reduce_fusion
  374.6 4.7 fusion.95
  381.4 3.9 fusion.48.do_ref
  385.3 50.9 %attn_bwd.1 = (bf16[2,577,3072]{2,1,0:T(8,128)(2,1)}, f32[2,4,2,256]{3,2,1,0:T(2,128)}) custom-call(bf16[2,577,3072]{2,1,0:T(8,128)(2,1)} %pad_maximum_fusion.qkv_ref, bf16[2,577,1024]{2,1,0:T(8,128)(2,1)} %fusion.48.do_ref), custom_call_target="tpu_custom_call" | custom-call | flops 27273543680 | bytes 18907136 | tf_op jit(solution)/shard_map/attn_bwd/pallas_call | solution.py:128
  436.3 5.9 bitcast_convert_fusion.6
  442.2 4.3 bitcast_convert_fusion.7
  446.6 4.3 bitcast_convert_fusion.8
  450.9 4.8 bitcast_convert_fusion.9
  465.9 6.5 maximum_bitcast_fusion.1
  472.5 5.5 bitcast_convert_fusion.1
  478.0 5.4 bitcast_convert_fusion.2
  483.5 3.2 bitcast_convert_fusion.3
  486.7 3.2 bitcast_convert_fusion.4
  489.8 3.9 maximum_bitcast_fusion
  493.8 17.8 %bitcast_convert_fusion = bf16[4096,1024]{1,0:T(8,128)(2,1)} fusion(bf16[2,577,4096]{2,1,0:T(8,128)(2,1)} %get-tuple-element.181, bf16[2,577,1024]{2,0,1:T(2,128)(2,1)} %constant_dynamic-slice_fusion), kind=kOutput, calls=%fused_computation.10 | convolution fusion | flops 9684647936 | bytes 20205568 | tf_op jit(solution)/shard_map/dot_general | solution.py:144
  511.6 8.3 copy.154
  520.0 6.5 bitcast_convert_fusion.5
  528.2 4.8 reduce-scatter.9.cloned.1.call-done
  533.0 75.5 %reduce-scatter.17.cloned.1.call-done = bf16[1,4,128,1024]{3,2,1,0:T(8,128)(2,1)} async-done(((bf16[8,4,128,1024]{3,2,1,0:T(8,128)(2,1)}), bf16[1,4,128,1024]{3,2,1,0:T(8,128)(2,1)}) %reduce-scatter.17.cloned.1.call-update) | async-done | bytes 1048592 | tf_op jit(solution)/shard_map/reduce_scatter | solution.py:196
  608.6 74.7 %reduce-scatter.21.cloned.1.call-done = bf16[1,4,128,1024]{3,2,1,0:T(8,128)(2,1)} async-done(((bf16[8,4,128,1024]{3,2,1,0:T(8,128)(2,1)}), bf16[1,4,128,1024]{3,2,1,0:T(8,128)(2,1)}) %reduce-scatter.21.cloned.1.call-update) | async-done | bytes 1048592 | tf_op jit(solution)/shard_map/reduce_scatter | solution.py:196
  683.4 45.4 %reduce-scatter.13.cloned.1.call-done = bf16[1,4,32,1024]{3,2,1,0:T(8,128)(2,1)} async-done(((bf16[8,4,32,1024]{3,2,1,0:T(8,128)(2,1)}), bf16[1,4,32,1024]{3,2,1,0:T(8,128)(2,1)}) %reduce-scatter.13.cloned.1.call-update) | async-done | bytes 262160 | tf_op jit(solution)/shard_map/reduce_scatter | solution.py:196
  728.8 25.6 %reduce-scatter.11.cloned.1.call-done = bf16[1,128,768]{1,2,0:T(8,128)(2,1)} async-done(((bf16[4,128,768]{1,2,0:T(8,128)(2,1)}), bf16[1,128,768]{1,2,0:T(8,128)(2,1)}) %reduce-scatter.11.cloned.1.call-update) | async-done | bytes 196624 | tf_op jit(solution)/shard_map/reduce_scatter | solution.py:197
  754.5 17.0 %add_convert_fusion = bf16[2,577,1024]{2,1,0:T(8,128)(2,1)} fusion(f32[2,577,1024]{2,1,0:T(8,128)} %copy-done, f32[1024]{0:T(1024)S(1)} %bitcast.205, bf16[2,577,4096]{2,1,0:T(8,128)(2,1)} %get-tuple-element.181, bf16[4096,1024]{1,0:T(8,128)(2,1)} %all-gather.22.cloned.1.call-done), kind=kOutput, calls=%fused_computation.48 | convolution fusion | flops 9683998720 | bytes 24936448 | tf_op jit(solution)/shard_map/dot_general | solution.py:136
  771.6 6.4 fusion.62
  778.0 6.4 fusion.68
  784.4 5.9 fusion.65
  790.3 9.6 fusion.24
  803.5 4.0 copy.109
  810.2 39.5 %psum.7 = f32[12288]{0:T(1024)S(1)} all-reduce(f32[12288]{0:T(1024)S(1)} %constant_dynamic-update-slice_fusion), channel_id=1, replica_groups=mesh['dp'=8,'tensor'=4] {'dp','tensor'}, use_global_device_ids=true, to_apply=%region_18.0 | all-reduce | flops 12288 | bytes 98304 | tf_op jit(solution)/shard_map/psum | solution.py:241
  852.5 10.6 all-gather.2
  863.1 4.2 multiply_subtract_fusion.3
  867.3 3.3 copy.115
  871.0 7.3 multiply_subtract_fusion.2
  878.3 3.5 copy.116
  881.8 3.7 copy.117
  888.0 141.7 %all-gather.24.cloned.1.call-done = bf16[8,577,1024]{2,1,0:T(8,128)(2,1)} async-done(((bf16[2,577,1024]{2,1,0:T(8,128)(2,1)}), bf16[8,577,1024]{2,1,0:T(8,128)(2,1)}) %all-gather.24.cloned.1.call-update) | async-done | bytes 9453584 | tf_op jit(solution)/shard_map/all_gather | solution.py:191
  1029.8 13.2 %copy.113 = bf16[8,577,1024]{2,0,1:T(8,128)(2,1)} copy(bf16[8,577,1024]{2,1,0:T(8,128)(2,1)} %all-gather.24.cloned.1.call-done) | data formatting | bytes 18907136
  1043.0 156.0 %all-gather.26.cloned.1.call-done = bf16[8,577,1024]{2,1,0:T(8,128)(2,1)} async-done(((bf16[2,577,1024]{2,1,0:T(8,128)(2,1)}), bf16[8,577,1024]{2,1,0:T(8,128)(2,1)}) %all-gather.26.cloned.1.call-update) | async-done | bytes 9453584 | tf_op jit(solution)/shard_map/all_gather | solution.py:227
  1199.0 12.8 %copy.114 = bf16[8,577,1024]{2,0,1:T(8,128)(2,1)} copy(bf16[8,577,1024]{2,1,0:T(8,128)(2,1)} %all-gather.26.cloned.1.call-done) | data formatting | bytes 18907136
  1211.8 15.2 %all-gather.30.cloned.1.call-done = bf16[1,1024,1024]{2,1,0:T(8,128)(2,1)} async-done(((bf16[1,128,1024]{2,1,0:T(8,128)(2,1)}), bf16[1,1024,1024]{2,1,0:T(8,128)(2,1)}) %all-gather.30.cloned.1.call-update) | async-done | bytes 2097168 | tf_op jit(solution)/shard_map/all_gather | solution.py:198
  1227.0 10.3 multiply_subtract_fusion.1
  1237.3 19.6 %all-gather.32.cloned.1.call-done = bf16[1,1024,1024]{2,1,0:T(8,128)(2,1)} async-done(((bf16[1,128,1024]{2,1,0:T(8,128)(2,1)}), bf16[1,1024,1024]{2,1,0:T(8,128)(2,1)}) %all-gather.32.cloned.1.call-update) | async-done | bytes 2097168 | tf_op jit(solution)/shard_map/all_gather | solution.py:198
  1256.8 10.1 multiply_subtract_fusion
  (222 shorter events, 46.6 us)
Async XLA Ops:
  7.2 76.6 %all-gather.16.cloned.1.call-start = ((), (), s32[]{:S(2)}) async-start(), calls=%async_computation.8 | async-start | bytes 6488064 | tf_op jit(solution)/shard_map/all_gather | solution.py:163
  7.3 9.0 copy-start.37
  7.3 9.0 copy-start.33
  9.7 21.7 %copy-start.5 = (f32[1024,3,256]{0,2,1:T(8,128)}, f32[1024,3,256]{0,2,1:T(8,128)S(1)}, u32[]{:S(2)}) copy-start(f32[1024,3,256]{0,2,1:T(8,128)S(1)} %copy.96) | copy-start | bytes 9437188
  10.8 131.4 %all-gather.18.cloned.1.call-start = ((), (), s32[]{:S(2)}) async-start(), calls=%async_computation.9 | async-start | bytes 2162688 | tf_op jit(solution)/shard_map/all_gather | solution.py:163
  12.4 209.5 %all-gather.20.cloned.1.call-start = ((), (), s32[]{:S(2)}) async-start(), calls=%async_computation.10 | async-start | bytes 8650752 | tf_op jit(solution)/shard_map/all_gather | solution.py:163
  14.3 287.0 %all-gather.22.cloned.1.call-start = ((), (), s32[]{:S(2)}) async-start(), calls=%async_computation.11 | async-start | bytes 8650752 | tf_op jit(solution)/shard_map/all_gather | solution.py:163
  16.2 516.8 %reduce-scatter.9.cloned.1.call-start = ((), (), s32[]{:S(2)}) async-start(), calls=%async_computation.14 | async-start | bytes 7077888 | tf_op jit(solution)/shard_map/reduce_scatter | solution.py:196
  31.3 7.9 copy-start.18
  31.4 7.9 copy-start.13
  37.6 104.6 %copy-start.1 = (bf16[2,577,1024]{2,0,1:T(2,128)(2,1)}, bf16[2,577,1024]{2,0,1:T(2,128)(2,1)S(1)}, u32[]{:S(2)}) copy-start(bf16[2,577,1024]{2,0,1:T(2,128)(2,1)S(1)} %constant_dynamic-slice_fusion.2) | copy-start | bytes 7090180
  38.3 56.4 %copy-start.16 = (f32[2,577]{1,0:T(2,128)}, f32[2,577]{1,0:T(2,128)S(1)}, u32[]{:S(2)}) copy-start(f32[2,577]{1,0:T(2,128)S(1)} %broadcast_multiply_fusion.5) | copy-start | bytes 13852
  39.3 55.5 %copy-start.21 = (f32[2,577]{1,0:T(2,128)}, f32[2,577]{1,0:T(2,128)S(1)}, u32[]{:S(2)}) copy-start(f32[2,577]{1,0:T(2,128)S(1)} %add_rsqrt_fusion.1) | copy-start | bytes 13852
  39.3 55.4 %copy-start.27 = (f32[1,1024]{1,0:T(1,128)}, f32[1,1024]{1,0:T(1,128)S(1)}, u32[]{:S(2)}) copy-start(f32[1,1024]{1,0:T(1,128)S(1)} %get-tuple-element.194) | copy-start | bytes 12292
  39.9 54.8 %copy-start.42 = (f32[1,1024]{1,0:T(1,128)}, f32[1,1024]{1,0:T(1,128)S(1)}, u32[]{:S(2)}) copy-start(f32[1,1024]{1,0:T(1,128)S(1)} %get-tuple-element.187) | copy-start | bytes 12292
  83.9 4.8 copy-start.46
  150.9 81.4 %copy-start.10 = (bf16[2,577,1024]{2,1,0:T(8,128)(2,1)}, bf16[2,577,1024]{2,1,0:T(8,128)(2,1)S(1)}, u32[]{:S(2)}) copy-start(bf16[2,577,1024]{2,1,0:T(8,128)(2,1)S(1)} %add_convert_fusion.1) | copy-start | bytes 7090180
  222.0 6.0 copy-start.12
  236.6 64.7 %copy-start.8 = (bf16[2,577,1024]{2,0,1:T(2,128)(2,1)S(1)}, bf16[2,577,1024]{2,0,1:T(2,128)(2,1)}, u32[]{:S(2)}) copy-start(bf16[2,577,1024]{2,0,1:T(2,128)(2,1)} %constant_dynamic-slice_fusion) | copy-start | bytes 7090180
  345.4 19.5 %copy-start.4 = (bf16[2,577,4096]{2,1,0:T(8,128)(2,1)}, bf16[2,577,4096]{2,1,0:T(8,128)(2,1)S(1)}, u32[]{:S(2)}) copy-start(bf16[2,577,4096]{2,1,0:T(8,128)(2,1)S(1)} %fusion.6) | copy-start | bytes 28360708
  352.9 12.0 slice-start
  358.9 6.0 slice-start.1
  374.6 6.8 copy-start.47
  385.3 51.0 %copy-start.2 = (bf16[2,577,1024]{2,0,1:T(2,128)(2,1)S(1)}, bf16[2,577,1024]{2,0,1:T(2,128)(2,1)}, u32[]{:S(2)}) copy-start(bf16[2,577,1024]{2,0,1:T(2,128)(2,1)} %copy-done.1) | copy-start | bytes 7090180
  385.3 51.0 %copy-start.17 = (f32[2,577]{1,0:T(2,128)S(1)}, f32[2,577]{1,0:T(2,128)}, u32[]{:S(2)}) copy-start(f32[2,577]{1,0:T(2,128)} %copy-done.16) | copy-start | bytes 13852
  385.3 51.0 %copy-start.22 = (f32[2,577]{1,0:T(2,128)S(1)}, f32[2,577]{1,0:T(2,128)}, u32[]{:S(2)}) copy-start(f32[2,577]{1,0:T(2,128)} %copy-done.21) | copy-start | bytes 13852
  385.3 51.0 %copy-start.28 = (f32[1,1024]{1,0:T(1,128)S(1)}, f32[1,1024]{1,0:T(1,128)}, u32[]{:S(2)}) copy-start(f32[1,1024]{1,0:T(1,128)} %copy-done.27) | copy-start | bytes 12292
  385.3 51.0 %copy-start.43 = (f32[1,1024]{1,0:T(1,128)S(1)}, f32[1,1024]{1,0:T(1,128)}, u32[]{:S(2)}) copy-start(f32[1,1024]{1,0:T(1,128)} %copy-done.42) | copy-start | bytes 12292
  436.3 5.9 copy-start.48
  472.4 136.1 %reduce-scatter.17.cloned.1.call-start = ((), (), s32[]{:S(2)}) async-start(), calls=%async_computation.18 | async-start | bytes 9437184 | tf_op jit(solution)/shard_map/reduce_scatter | solution.py:196
  472.5 5.5 copy-start.11
  472.5 11.0 slice-start.4
  472.5 11.0 slice-start.5
  478.0 5.5 slice-start.6
  493.7 189.6 %reduce-scatter.21.cloned.1.call-start = ((), (), s32[]{:S(2)}) async-start(), calls=%async_computation.20 | async-start | bytes 9437184 | tf_op jit(solution)/shard_map/reduce_scatter | solution.py:196
  520.0 208.8 %reduce-scatter.13.cloned.1.call-start = ((), (), s32[]{:S(2)}) async-start(), calls=%async_computation.16 | async-start | bytes 2359296 | tf_op jit(solution)/shard_map/reduce_scatter | solution.py:196
  526.6 227.9 %copy-start.41 = (f32[1,1024]{1,0:T(1,128)S(1)}, f32[1,1024]{1,0:T(1,128)}, u32[]{:S(2)}) copy-start(f32[1,1024]{1,0:T(1,128)} %get-tuple-element.188) | copy-start | bytes 12292
  528.1 226.3 %reduce-scatter.11.cloned.1.call-start = ((), (), s32[]{:S(2)}) async-start(), calls=%async_computation.15 | async-start | bytes 983040 | tf_op jit(solution)/shard_map/reduce_scatter | solution.py:197
  533.0 270.0 %reduce-scatter.19.cloned.1.call-start = ((), (), s32[]{:S(2)}) async-start(), calls=%async_computation.19 | async-start | bytes 1310720 | tf_op jit(solution)/shard_map/reduce_scatter | solution.py:197
  608.5 241.2 %reduce-scatter.23.cloned.1.call-start = ((), (), s32[]{:S(2)}) async-start(), calls=%async_computation.21 | async-start | bytes 1310720 | tf_op jit(solution)/shard_map/reduce_scatter | solution.py:197
  683.3 169.1 %reduce-scatter.15.cloned.1.call-start = ((), (), s32[]{:S(2)}) async-start(), calls=%async_computation.17 | async-start | bytes 327680 | tf_op jit(solution)/shard_map/reduce_scatter | solution.py:197
  728.8 138.6 %all-gather.28.cloned.1.call-start = ((), (), s32[]{:S(2)}) async-start(), calls=%async_computation.22 | async-start | bytes 1769472 | tf_op jit(solution)/shard_map/all_gather | solution.py:198
  754.4 275.3 %all-gather.24.cloned.1.call-start = ((), (), s32[]{:S(2)}) async-start(), calls=%async_computation.12 | async-start | bytes 11960320 | tf_op jit(solution)/shard_map/all_gather | solution.py:191
  771.5 427.5 %all-gather.26.cloned.1.call-start = ((), (), s32[]{:S(2)}) async-start(), calls=%async_computation.13 | async-start | bytes 11960320 | tf_op jit(solution)/shard_map/all_gather | solution.py:227
  771.5 12.8 %slice-start.7 = ((s8[6291456]{0:T(1024)(128)(4,1)}), s8[4194304]{0:T(1024)(128)(4,1)S(1)}, s32[]{:S(2)}) async-start(s8[6291456]{0:T(1024)(128)(4,1)} %bitcast.215), calls=%async_computation.32 | async-start | bytes 8388608
  778.0 6.4 slice-start.8
  784.4 15.5 %slice-start.2 = ((s8[4784128]{0:T(1024)(128)(4,1)}), s8[4194304]{0:T(1024)(128)(4,1)S(1)}, s32[]{:S(2)}) async-start(s8[4784128]{0:T(1024)(128)(4,1)} %bitcast.162), calls=%async_computation.27 | async-start | bytes 8388608
  790.3 9.6 slice-start.3
  802.9 424.1 %all-gather.30.cloned.1.call-start = ((), (), s32[]{:S(2)}) async-start(), calls=%async_computation.23 | async-start | bytes 2359296 | tf_op jit(solution)/shard_map/all_gather | solution.py:198
  803.5 453.3 %all-gather.32.cloned.1.call-start = ((), (), s32[]{:S(2)}) async-start(), calls=%async_computation.24 | async-start | bytes 2359296 | tf_op jit(solution)/shard_map/all_gather | solution.py:198
  807.6 42.3 %copy-start.38 = (f32[2,256]{1,0:T(2,128)S(1)}, f32[2,256]{1,0:T(2,128)}, u32[]{:S(2)}) copy-start(f32[2,256]{1,0:T(2,128)} %param.29) | copy-start | bytes 6148
  807.6 42.3 %copy-start.44 = (f32[2,256]{1,0:T(2,128)S(1)}, f32[2,256]{1,0:T(2,128)}, u32[]{:S(2)}) copy-start(f32[2,256]{1,0:T(2,128)} %param.37) | copy-start | bytes 6148
  807.6 42.3 %copy-start.45 = (f32[2,256]{1,0:T(2,128)S(1)}, f32[2,256]{1,0:T(2,128)}, u32[]{:S(2)}) copy-start(f32[2,256]{1,0:T(2,128)} %param.45) | copy-start | bytes 6148
  807.6 42.9 %copy-start.34 = (f32[1024]{0:T(1024)S(1)}, f32[1024]{0:T(1024)}, u32[]{:S(2)}) copy-start(f32[1024]{0:T(1024)} %param.32) | copy-start | bytes 12292
  807.6 42.9 %copy-start.39 = (f32[1024]{0:T(1024)S(1)}, f32[1024]{0:T(1024)}, u32[]{:S(2)}) copy-start(f32[1024]{0:T(1024)} %param.40) | copy-start | bytes 12292
  807.6 42.9 %copy-start.40 = (f32[1024]{0:T(1024)S(1)}, f32[1024]{0:T(1024)}, u32[]{:S(2)}) copy-start(f32[1024]{0:T(1024)} %param.48) | copy-start | bytes 12292
  807.6 43.5 %copy-start.19 = (f32[2,1024]{1,0:T(2,128)S(1)}, f32[2,1024]{1,0:T(2,128)}, u32[]{:S(2)}) copy-start(f32[2,1024]{1,0:T(2,128)} %param.34) | copy-start | bytes 24580
  807.6 43.5 %copy-start.35 = (f32[2,1024]{1,0:T(2,128)S(1)}, f32[2,1024]{1,0:T(2,128)}, u32[]{:S(2)}) copy-start(f32[2,1024]{1,0:T(2,128)} %param.42) | copy-start | bytes 24580
  807.6 43.5 %copy-start.36 = (f32[2,1024]{1,0:T(2,128)S(1)}, f32[2,1024]{1,0:T(2,128)}, u32[]{:S(2)}) copy-start(f32[2,1024]{1,0:T(2,128)} %param.50) | copy-start | bytes 24580
  807.7 44.2 %copy-start.14 = (f32[4,1024]{1,0:T(4,128)S(1)}, f32[4,1024]{1,0:T(4,128)}, u32[]{:S(2)}) copy-start(f32[4,1024]{1,0:T(4,128)} %param.35) | copy-start | bytes 49156
  807.7 44.1 %copy-start.29 = (f32[4,1024]{1,0:T(4,128)S(1)}, f32[4,1024]{1,0:T(4,128)}, u32[]{:S(2)}) copy-start(f32[4,1024]{1,0:T(4,128)} %param.43) | copy-start | bytes 49156
  807.7 44.1 %copy-start.30 = (f32[4,1024]{1,0:T(4,128)S(1)}, f32[4,1024]{1,0:T(4,128)}, u32[]{:S(2)}) copy-start(f32[4,1024]{1,0:T(4,128)} %param.51) | copy-start | bytes 49156
  849.8 17.5 %copy-start.20 = (f32[2,1024]{1,0:T(2,128)}, f32[2,1024]{1,0:T(2,128)S(1)}, u32[]{:S(2)}) copy-start(f32[2,1024]{1,0:T(2,128)S(1)} %slice.197) | copy-start | bytes 24580
  849.9 17.4 %copy-start.15 = (f32[4,1024]{1,0:T(4,128)}, f32[4,1024]{1,0:T(4,128)S(1)}, u32[]{:S(2)}) copy-start(f32[4,1024]{1,0:T(4,128)S(1)} %slice.199) | copy-start | bytes 49156
  (11 other events, 32.1 us)
Sparse Core Ops, SparseCore 0:
  11.5 72.3 all-gather.15
  87.3 54.8 all-gather.17
  145.6 76.2 all-gather.19
  225.3 76.0 all-gather.21
  472.6 60.3 reduce-scatter.8
  537.2 71.2 reduce-scatter.16
  612.0 71.2 reduce-scatter.20
  687.5 41.1 reduce-scatter.12
  731.1 23.2 reduce-scatter.10
  756.5 26.4 reduce-scatter.18
  785.4 25.7 reduce-scatter.22
  813.3 18.3 reduce-scatter.14
  833.7 24.4 all-gather.27
  860.3 169.4 all-gather.23
  1031.8 167.0 all-gather.25
  1200.9 26.0 all-gather.29
  1228.9 27.8 all-gather.31

commit v2 on v1

v2 whole, which is shorter than its diff:
```python
import math

import jax
import jax.numpy as jnp
from jax import lax
from jax.experimental import pallas as pl
from jax.experimental.pallas import tpu as pltpu
from jax.sharding import PartitionSpec as P

D = 1024
FF = 4096
STEP = 3
BETA_ONE = 0.9
BETA_TWO = 0.999
ADAM_EPS = 1e-08
MATRIX_DECAY = 0.05

HD=64
LOG2E=1.4426950408889634
NORM_EPS = 1e-05
SQRT_HALF = 0.7071067811865476
INV_SQRT_TAU = 0.3989422804014327
NT=(((1,),(1,)),((),()))
NN=(((1,),(0,)),((),()))
TN=(((0,),(0,)),((),()))
BF=jnp.bfloat16
F32=jnp.float32
VLIM=36*2**20
PAIR=2*HD

def dot(a,b,dims):
    return lax.dot_general(a,b,dims,preferred_element_type=jnp.float32)

def normalize(v):
    center=v-jnp.mean(v,axis=-1,keepdims=True)
    inv_std=lax.rsqrt(jnp.mean(center*center,axis=-1,keepdims=True)+NORM_EPS)
    return center*inv_std,inv_std

def norm_back(d_normed,normed,inv_std):
    return inv_std*(d_normed-jnp.mean(d_normed,axis=-1,keepdims=True)-normed*jnp.mean(d_normed*normed,axis=-1,keepdims=True))

def qkv_attn_kernel(x_ref,gain_ref,shift_ref,w_ref,b_ref,act_ref,qkv_ref,out_ref):
    t=pl.program_id(1)
    @pl.when(t==0)
    def _():
        normed,_=normalize(x_ref[0].astype(F32))
        act_ref[0]=(normed*gain_ref[...]+shift_ref[...]).astype(BF)
    qkv_ref[0]=(dot(act_ref[0],w_ref[0],NN)+b_ref[0]).astype(BF)
    lw=out_ref.shape[2]
    seq=x_ref.shape[1]
    low=lax.broadcasted_iota(jnp.int32,(seq,PAIR),1)<HD
    for p in range(lw//PAIR):
        at=p*PAIR
        q=qkv_ref[0,:,at:at+PAIR]
        k=qkv_ref[0,:,lw+at:lw+at+PAIR]
        v=qkv_ref[0,:,2*lw+at:2*lw+at+PAIR]
        outs=[]
        for sel in (low,~low):
            s=dot(jnp.where(sel,q,jnp.zeros_like(q)),k,NT)*(HD**-0.5*LOG2E)
            e=jnp.exp2(s-jnp.max(s,axis=1,keepdims=True))
            l=jnp.sum(e,axis=1,keepdims=True)
            outs.append(dot(e.astype(BF),v,NN)/l)
        out_ref[0,:,at:at+PAIR]=jnp.where(low,outs[0],outs[1]).astype(BF)

def params(name,flops,nbytes,trans=0,work=1000000):
    return dict(name=name,compiler_params=pltpu.CompilerParams(vmem_limit_bytes=VLIM),
        cost_estimate=pl.CostEstimate(flops=int(work),bytes_accessed=1000000,transcendentals=0))

def row(width): return pl.BlockSpec((1,width),lambda *_:(0,0))

def qkv_attn(at,x,gain,shift,w,b,n=1,work=1000000):
    _,seq,d=x.shape
    g=w.shape[0]
    w3=b.shape[1]
    lw=w3//3
    return pl.pallas_call(qkv_attn_kernel,grid=(n,g),
        in_specs=[pl.BlockSpec((1,seq,d),lambda i,t:(at+i,0,0)),row(d),row(d),
            pl.BlockSpec((1,d,w3),lambda i,t:(t,0,0)),pl.BlockSpec((1,1,w3),lambda i,t:(t,0,0))],
        out_specs=[pl.BlockSpec((1,seq,d),lambda i,t:(i,0,0)),pl.BlockSpec((1,seq,w3),lambda i,t:(i,0,t)),pl.BlockSpec((1,seq,lw),lambda i,t:(i,0,t))],
        out_shape=[jax.ShapeDtypeStruct((n,seq,d),BF),jax.ShapeDtypeStruct((n,seq,g*w3),BF),jax.ShapeDtypeStruct((n,seq,g*lw),BF)],
        **params("qkv_attn",2*n*seq*d*g*w3+16*n*seq*seq*g*lw,n*seq*(2*d+g*w3+g*lw)*2,n*g*lw//HD*seq*seq,work))(x,gain,shift,w,b.reshape(g,1,w3))

def mlp_fwd_kernel(x_ref,att_ref,pw_ref,pb_ref,gain_ref,shift_ref,w1_ref,b1_ref,w2_ref,b2_ref,
                   resid_ref,act_ref,hid_ref,slope_ref,out_ref,acc_ref):
    j=pl.program_id(1)
    @pl.when(j==0)
    def _():
        g,_,lw=pw_ref.shape
        for b in range(g):
            cols=slice(b*lw,(b+1)*lw)
            part=x_ref[0,:,cols].astype(F32)+pb_ref[:,cols]
            for k in range(g):
                part=part+dot(att_ref[0,:,k*lw:(k+1)*lw],pw_ref[k,cols,:],NN)
            resid_ref[0,:,cols]=part
        resid=resid_ref[0]
        normed,_=normalize(resid)
        act_ref[0]=(normed*gain_ref[...]+shift_ref[...]).astype(BF)
        acc_ref[...]=resid+b2_ref[...]
    pre=dot(act_ref[0],w1_ref[0],NN)+b1_ref[0]
    cdf=0.5+0.5*lax.erf(pre*SQRT_HALF)
    hid=(pre*cdf).astype(BF)
    hid_ref[0]=hid
    slope_ref[0]=(cdf+pre*jnp.exp2(pre*pre*(-0.5*LOG2E))*INV_SQRT_TAU).astype(BF)
    acc_ref[...]+=dot(hid,w2_ref[0],NN)
    @pl.when(j==pl.num_programs(1)-1)
    def _():
        out_ref[0]=acc_ref[...].astype(BF)

def mlp_fwd(at,x,att,pw,pb,gain,shift,w1,b1,w2,b2,tile=1024,n=1,work=1000000):
    _,seq,d=x.shape
    g,_,fw=w1.shape
    ff=g*fw
    tile=min(tile,fw)
    per=fw//tile
    img=pl.BlockSpec((1,seq,d),lambda i,j:(i,0,0))
    own=pl.BlockSpec((1,seq,d),lambda i,j:(at+i,0,0))
    hidden=pl.BlockSpec((1,seq,tile),lambda i,j:(i,0,j))
    return pl.pallas_call(mlp_fwd_kernel,grid=(n,ff//tile),
        in_specs=[own,img,pl.BlockSpec((g,d,d//g),lambda i,j:(0,0,3)),row(d),row(d),row(d),
            pl.BlockSpec((1,d,tile),lambda i,j:(j//per,0,j%per)),pl.BlockSpec((1,1,tile),lambda i,j:(j,0,0)),
            pl.BlockSpec((1,tile,d),lambda i,j:(j//per,j%per,0)),row(d)],
        out_specs=[img,img,hidden,hidden,img],
        out_shape=[jax.ShapeDtypeStruct((n,seq,d),F32),jax.ShapeDtypeStruct((n,seq,d),BF),jax.ShapeDtypeStruct((n,seq,ff),BF),
            jax.ShapeDtypeStruct((n,seq,ff),BF),jax.ShapeDtypeStruct((n,seq,d),BF)],
        scratch_shapes=[pltpu.VMEM((seq,d),F32)],
        **params("mlp_fwd",2*n*seq*d*(d+2*ff),n*seq*(5*d+2*ff)*2+ff*d*4,2*n*seq*ff,work))(x,att,pw,pb,gain,shift,w1,b1.reshape(ff//tile,1,tile),w2,b2)

def mlp_bwd_kernel(cot_ref,slope_ref,w2_ref,w1_ref,resid_ref,gain_ref,pw_ref,
                   dpre_ref,db1_ref,dres_ref,dresb_ref,datt_ref,sums_ref,acc_ref):
    j=pl.program_id(1)
    dpre=dot(cot_ref[0],w2_ref[0],NT)*slope_ref[0].astype(F32)
    db1_ref[0,0]=jnp.sum(dpre,axis=0,keepdims=True)
    dpre_b=dpre.astype(BF)
    dpre_ref[0]=dpre_b
    part=dot(dpre_b,w1_ref[0],NT)
    @pl.when(j==0)
    def _():
        acc_ref[...]=part
    @pl.when(j>0)
    def _():
        acc_ref[...]+=part
    @pl.when(j==pl.num_programs(1)-1)
    def _():
        dact=acc_ref[...]
        normed,inv_std=normalize(resid_ref[0])
        dy=cot_ref[0].astype(F32)
        dres=dy+norm_back(dact*gain_ref[...],normed,inv_std)
        dres_ref[0]=dres
        dresb=dres.astype(BF)
        dresb_ref[0]=dresb
        g,_,lw=pw_ref.shape
        for k in range(g):
            part=0.0
            for b in range(g):
                cols=slice(b*lw,(b+1)*lw)
                part=part+dot(dresb[:,cols],pw_ref[k,cols,:],NT)
            datt_ref[0,:,k*lw:(k+1)*lw]=part.astype(BF)
        sums_ref[0,0:1]=jnp.sum(dact*normed,axis=0,keepdims=True)
        sums_ref[0,1:2]=jnp.sum(dact,axis=0,keepdims=True)
        sums_ref[0,2:3]=jnp.sum(dres,axis=0,keepdims=True)
        sums_ref[0,3:4]=jnp.sum(dy,axis=0,keepdims=True)

def mlp_bwd(at,cot,slope,w2,w1,resid,gain,pw,tile=1024):
    n,seq,d=1,*cot.shape[1:]
    g,_,fw=w1.shape
    ff=g*fw
    tile=min(tile,fw)
    per=fw//tile
    img=pl.BlockSpec((1,seq,d),lambda i,j:(i,0,0))
    own=pl.BlockSpec((1,seq,d),lambda i,j:(at,0,0))
    hidden=pl.BlockSpec((1,seq,tile),lambda i,j:(i,0,j))
    return pl.pallas_call(mlp_bwd_kernel,grid=(n,ff//tile),
        in_specs=[own,hidden,pl.BlockSpec((1,tile,d),lambda i,j:(j//per,j%per,0)),pl.BlockSpec((1,d,tile),lambda i,j:(j//per,0,j%per)),
            img,row(d),pl.BlockSpec((g,d,d//g),lambda i,j:(0,0,3))],
        out_specs=[hidden,pl.BlockSpec((1,1,1,tile),lambda i,j:(i,j,0,0)),img,img,img,pl.BlockSpec((1,4,d),lambda i,j:(i,0,0))],
        out_shape=[jax.ShapeDtypeStruct((n,seq,ff),BF),jax.ShapeDtypeStruct((n,ff//tile,1,tile),F32),jax.ShapeDtypeStruct((n,seq,d),F32),
            jax.ShapeDtypeStruct((n,seq,d),BF),jax.ShapeDtypeStruct((n,seq,d),BF),jax.ShapeDtypeStruct((n,4,d),F32)],
        scratch_shapes=[pltpu.VMEM((seq,d),F32)],
        **params("mlp_bwd",2*n*seq*d*(d+2*ff),n*seq*(6*d+2*ff)*2+ff*d*4))(cot,slope,w2,w1,resid,gain,pw)

def attn_bwd_kernel(qkv_ref,do_ref,w_ref,x_ref,dres_ref,gain_ref,dqkv_ref,qvsum_ref,gt_ref,sums_ref,acc_ref):
    t=pl.program_id(1)
    lw=do_ref.shape[2]
    seq=x_ref.shape[1]
    low=lax.broadcasted_iota(jnp.int32,(seq,PAIR),1)<HD
    for p in range(lw//PAIR):
        at=p*PAIR
        q=qkv_ref[0,:,at:at+PAIR]
        k=qkv_ref[0,:,lw+at:lw+at+PAIR]
        v=qkv_ref[0,:,2*lw+at:2*lw+at+PAIR]
        do=do_ref[0,:,at:at+PAIR]
        dqs=[];dks=[];dvs=[]
        for sel in (low,~low):
            km=jnp.where(sel,k,jnp.zeros_like(k))
            vm=jnp.where(sel,v,jnp.zeros_like(v))
            st=dot(km,q,NT)*(HD**-0.5*LOG2E)
            e=jnp.exp2(st-jnp.max(st,axis=0,keepdims=True))
            pt=e*(1.0/jnp.sum(e,axis=0,keepdims=True))
            dp=dot(vm,do,NT)
            delta=jnp.sum(pt*dp,axis=0,keepdims=True)
            ds=(pt*((dp-delta)*HD**-0.5)).astype(BF)
            dvs.append(dot(pt.astype(BF),do,NN))
            dks.append(dot(ds,q,NN))
            dqs.append(dot(ds,k,TN))
        dq=jnp.where(low,dqs[0],dqs[1]); dk=jnp.where(low,dks[0],dks[1]); dv=jnp.where(low,dvs[0],dvs[1])
        dqkv_ref[0,:,at:at+PAIR]=dq.astype(BF)
        dqkv_ref[0,:,lw+at:lw+at+PAIR]=dk.astype(BF)
        dqkv_ref[0,:,2*lw+at:2*lw+at+PAIR]=dv.astype(BF)
        qvsum_ref[0,0,0:1,at:at+PAIR]=jnp.sum(dq,axis=0,keepdims=True)
        qvsum_ref[0,0,1:2,at:at+PAIR]=jnp.sum(dv,axis=0,keepdims=True)
    part=dot(dqkv_ref[0],w_ref[0],NT)
    @pl.when(t==0)
    def _():
        acc_ref[...]=part
    @pl.when(t>0)
    def _():
        acc_ref[...]+=part
    @pl.when(t==pl.num_programs(1)-1)
    def _():
        dact=acc_ref[...]
        normed,inv_std=normalize(x_ref[0].astype(F32))
        gt_ref[0]=(dres_ref[0]+norm_back(dact*gain_ref[...],normed,inv_std)).astype(BF)
        sums_ref[0,0:1]=jnp.sum(dact*normed,axis=0,keepdims=True)
        sums_ref[0,1:2]=jnp.sum(dact,axis=0,keepdims=True)

def attn_bwd(at,qkv,do,w,x,dres,gain):
    n,seq,d=1,*x.shape[1:]
    g=w.shape[0]
    w3=qkv.shape[2]//g
    lw=w3//3
    img=pl.BlockSpec((1,seq,d),lambda i,t:(i,0,0))
    return pl.pallas_call(attn_bwd_kernel,grid=(n,g),
        in_specs=[pl.BlockSpec((1,seq,w3),lambda i,t:(i,0,t)),pl.BlockSpec((1,seq,lw),lambda i,t:(i,0,t)),
            pl.BlockSpec((1,d,w3),lambda i,t:(t,0,0)),pl.BlockSpec((1,seq,d),lambda i,t:(at,0,0)),img,row(d)],
        out_specs=[pl.BlockSpec((1,seq,w3),lambda i,t:(i,0,t)),pl.BlockSpec((1,1,2,lw),lambda i,t:(i,t,0,0)),img,pl.BlockSpec((1,2,d),lambda i,t:(i,0,0))],
        out_shape=[jax.ShapeDtypeStruct((n,seq,g*w3),BF),jax.ShapeDtypeStruct((n,g,2,lw),F32),jax.ShapeDtypeStruct((n,seq,d),BF),jax.ShapeDtypeStruct((n,2,d),F32)],
        scratch_shapes=[pltpu.VMEM((seq,d),F32)],
        **params("attn_bwd",2*n*seq*d*g*w3+40*n*seq*seq*g*lw,n*seq*(2*g*w3+g*lw+4*d)*2+g*w3*d*2,n*g*lw//HD*seq*seq))(qkv,do,w,x,dres,gain)


def cut(total,out_ref):
    out_ref[...]=total.astype(BF).reshape(out_ref.shape)

def image_sum(refs):
    n=len(refs)//2
    return sum(dot(l[0],r[0],TN) for l,r in zip(refs[:n],refs[n:]))

def grad_kernel(*refs):
    cut(image_sum(refs[:-1]),refs[-1])

def grad_fc1_kernel(*refs):
    out_ref=refs[-1]
    half=len(refs)//2
    n_dp,_,rows,width=out_ref.shape
    fw=refs[half-1].shape[2]
    lw=width-fw
    out_ref[:,0,:,:fw]=image_sum(refs[:half]).astype(BF).reshape(n_dp,rows,fw)
    proj=image_sum(refs[half:-1]).astype(BF)
    per=lw//rows
    for b in range(n_dp//per):
        out_ref[b*per:(b+1)*per,0,:,fw:]=proj[:,b*lw:(b+1)*lw].reshape(per,rows,lw)

def shard_grads(kernel,name,n_dp,g,rows,width,specs,ops):
    return pl.pallas_call(kernel,
        grid=(g,),in_specs=specs,out_specs=pl.BlockSpec((n_dp,1,rows//n_dp,width),lambda k:(0,k,0,0)),
        out_shape=jax.ShapeDtypeStruct((n_dp,g,rows//n_dp,width),BF),
        **params(name,0,0))(*ops)

def whole(ops): return [pl.BlockSpec((1,*a.shape[1:]),lambda k:(0,0,0)) for a in ops]

def both(a): return [pl.BlockSpec((1,*a.shape[1:]),lambda k,i=i:(i,0,0)) for i in range(a.shape[0])]

def part(ops,g): return [pl.BlockSpec((1,a.shape[1],a.shape[2]//g),lambda k:(0,0,k)) for a in ops]

def grad_fc2(hid,cot,n_dp,g):
    ff,d=hid[0].shape[2],cot.shape[2]
    return shard_grads(grad_kernel,"grad_fc2",n_dp,g,ff//g,d,part(hid,g)+both(cot),(*hid,*[cot]*len(hid)))

def grad_fc1(act,dpre,att,dres,n_dp,g):
    ff,d=dpre[0].shape[2],act[0].shape[2]
    return shard_grads(grad_fc1_kernel,"grad_fc1",n_dp,g,d,ff//g+d//g,
        whole(act)+part(dpre,g)+part(att,g)+whole(dres),(*act,*dpre,*att,*dres))

def grad_qkv(act,dqkv,n_dp,g):
    w,d=dqkv[0].shape[2],act[0].shape[2]
    return shard_grads(grad_kernel,"grad_qkv",n_dp,g,d,w//g,whole(act)+part(dqkv,g),(*act,*dqkv))

def interleave(rows,out_ref):
    out_ref[...]=jnp.swapaxes(jnp.stack([r.astype(F32) for r in rows],axis=0),0,1).astype(BF)

def weave_kernel(*refs):
    interleave([ref[t] for t in range(refs[0].shape[0]) for ref in refs[:-1]],refs[-1])

def weave(parts,tile=64):
    n_t,seq,d=parts[0].shape
    n=n_t*len(parts)
    out=pl.pallas_call(weave_kernel,grid=(pl.cdiv(seq,tile),),
        in_specs=[pl.BlockSpec((n_t,tile,d),lambda r:(0,r,0))]*len(parts),
        out_specs=pl.BlockSpec((tile,n,d),lambda r:(r,0,0)),
        out_shape=jax.ShapeDtypeStruct((seq,n,d),BF),**params("weave",0,0))(*parts)
    return out.transpose(1,0,2)

def adamw(weight_old, moment_one, moment_two, grad_sum, rate_value, decay_value):
    new_one = BETA_ONE * moment_one + (1.0 - BETA_ONE) * grad_sum
    new_two = BETA_TWO * moment_two + (1.0 - BETA_TWO) * grad_sum * grad_sum
    one_hat = new_one / (1.0 - BETA_ONE**STEP)
    two_hat = new_two / (1.0 - BETA_TWO**STEP)
    new_weight = weight_old - rate_value * (
        one_hat / (jnp.sqrt(two_hat) + ADAM_EPS) + decay_value * weight_old
    )
    return (new_weight, new_one, new_two)


def shift(value, axis, by):
    n = lax.axis_size(axis)
    return lax.ppermute(value, axis, [(i, (i + by) % n) for i in range(n)])


def swap(value, axis, mask):
    n = lax.axis_size(axis)
    return lax.ppermute(value, axis, [(i, i ^ mask) for i in range(n)])


def spread_moves(bufs, c, p, units, target):
    half = units * p // 2
    moves = []
    for flip, buf in enumerate(bufs):
        base = c ^ flip
        for at, slot in enumerate((base, base ^ 2, base ^ 4)):
            first = pl.multiple_of(slot * p, p)
            moves += [(buf.at[pl.ds((at * units + k) * p, p)], target(k, first, p)) for k in range(units)]
        first = pl.multiple_of((base ^ 6) * p, p)
        moves += [(buf.at[pl.ds((3 * units + k) * p, p)], target(k, first, p)) for k in range(units)]
    return moves


def run_copies(moves, sems):
    copies = [pltpu.make_async_copy(src, dst, sems.at[i]) for i, (src, dst) in enumerate(moves)]
    for copy in copies:
        copy.start()
    for copy in copies:
        copy.wait()


def place_kernel(at_ref, own_ref, near_ref, far_ref, out_ref, sems):
    p = near_ref.shape[0] // 12
    moves = spread_moves((near_ref, far_ref), at_ref[0], p, 3, lambda k, first, n: out_ref.at[k + 1, pl.ds(first, n)])
    run_copies([(own_ref, out_ref.at[0])] + moves, sems)


def spread_kernel(at_ref, near_ref, far_ref, out_ref, sems):
    p = near_ref.shape[0] // 4
    run_copies(spread_moves((near_ref, far_ref), at_ref[0], p, 1, lambda k, first, n: out_ref.at[pl.ds(first, n)]), sems)


def dma_call(kernel, name, n, out_shape, ops):
    at = lax.axis_index("dp").reshape(1).astype(jnp.int32)
    return pl.pallas_call(
        kernel,
        in_specs=[pl.BlockSpec(memory_space=pltpu.SMEM)] + [pl.BlockSpec(memory_space=pltpu.VMEM)] * len(ops),
        out_specs=pl.BlockSpec(memory_space=pl.ANY),
        out_shape=out_shape,
        scratch_shapes=[pltpu.SemaphoreType.DMA((n,))],
        **params(name, 0, 0),
    )(at, *ops)


def after(value, *earlier):
    return lax.optimization_barrier((value, *earlier))[0]


def tie(*values):
    return lax.optimization_barrier(values)


def shards(piece):
    return [shift(piece, "tensor", k) for k in range(1, lax.axis_size("tensor"))]


def fetch(mine):
    if lax.axis_size("dp") != 8:
        return mine, mine
    return swap(mine, "dp", 2), swap(mine, "dp", 4)


def fetch_diagonal(xs, ys):
    half = xs.shape[0] // 2
    if lax.axis_size("dp") != 8:
        return xs[:half], ys[half:]
    return swap(xs[:half], "dp", 4), swap(ys[half:], "dp", 2)


def finish(own, mine, xs, ys, da, db, name):
    if lax.axis_size("dp") != 8:
        every = lax.all_gather(mine.reshape(lax.axis_size("tensor") - 1, -1, own.shape[1]), "dp", axis=1, tiled=True)
        return jnp.concatenate([own[None], every], 0)
    near = jnp.concatenate([mine, xs, ys, da, db], 0)
    shape = jax.ShapeDtypeStruct((4, *own.shape), own.dtype)
    return dma_call(place_kernel, name, 25, shape, (own, near, swap(near, "dp", 1)))


def reduce_dp(parts):
    return lax.psum_scatter(parts, "dp", scatter_dimension=0, tiled=False)


def parts_of(value):
    parts = []
    for _ in range(3):
        parts.append(lax.reduce_precision(value, 8, 7))
        value = value - parts[-1]
    return [v.astype(BF) for v in parts]


def sum_chain(value):
    for axis in ("dp", "tensor"):
        mask = 1
        while mask < lax.axis_size(axis):
            value = value + (yield swap(value, axis, mask))
            mask *= 2
    return value


def reduce_chain(part, name):
    n_t = part.shape[0]
    up, down = part[1], part[n_t - 1]
    for step in range(1, n_t):
        up, down = yield (
            lax.ppermute(up, "tensor", [(i, i + 1) for i in range(step)]),
            lax.ppermute(down, "tensor", [(n_t - 1 - i, n_t - 2 - i) for i in range(step)]),
        )
        if step < n_t - 1:
            up = (up.astype(F32) + part[step + 1].astype(F32)).astype(BF)
            down = (down.astype(F32) + part[n_t - 1 - step].astype(F32)).astype(BF)
    mine = (part[0].astype(F32) + up.astype(F32) + down.astype(F32)).astype(BF)
    if lax.axis_size("dp") != 8:
        return lax.all_gather(mine, "dp", axis=0, tiled=True).astype(F32)
    xs, ys = yield fetch(mine)
    da, db = yield fetch_diagonal(xs, ys)
    near = jnp.concatenate([mine, xs, ys, da, db], 0)
    far = yield swap(near, "dp", 1)
    shape = jax.ShapeDtypeStruct((8 * mine.shape[0], mine.shape[1]), mine.dtype)
    return dma_call(spread_kernel, name, 8, shape, (near, far)).astype(F32)


def run_chains(chains, work, made):
    live, results, step = {}, [None] * len(chains), 0
    while step == 0 or live or work or any(begin >= step for begin, _ in chains):
        moved = {}
        for at, (begin, make) in enumerate(chains):
            if begin == step:
                live[at] = make()
                moved[at] = next(live[at])
            elif at in live:
                try:
                    moved[at] = live[at].send(kept[at])
                except StopIteration as end:
                    results[at] = end.value
                    del live[at]
        if work:
            made.append(work.pop(0)(made, results))
            moved, made[-1] = tie(moved, made[-1])
        else:
            moved = tie(moved)[0]
        kept = moved
        step += 1
    return results


def per_device(*args):
    tokens, cotangent = args[0], args[1]
    weights, firsts, seconds = args[2:10], args[10:18], args[18:26]
    qkv_weight, qv_bias, proj_weight, fc1_weight, fc1_bias, fc2_weight, norm_gains, shift_biases = weights
    n_t = lax.axis_size("tensor")
    n_dp = lax.axis_size("dp")
    t_at = lax.axis_index("tensor")
    dp_at = lax.axis_index("dp")
    width = tokens.shape[2]
    own = tokens.shape[0] // n_t
    lw = qkv_weight.shape[2]
    fw = fc1_weight.shape[1]

    def proj_pack(value):
        return value.reshape(lw, n_t, lw).transpose(1, 0, 2).reshape(width, lw)

    def proj_unpack(value):
        return value.reshape(n_t, lw, lw).transpose(1, 0, 2).reshape(lw, width)

    mix = jnp.concatenate([qkv_weight[:, 0], qkv_weight[:, 1], qkv_weight[:, 2], proj_pack(proj_weight)], axis=1)
    p = width // n_dp
    mix = mix.astype(BF)
    biases = jnp.concatenate([qv_bias.reshape(-1), fc1_bias])
    flat = jnp.concatenate(parts_of(biases))
    columns = mix.shape[1]
    extra = 16 * pl.cdiv(flat.size, 16 * columns)
    flat = jnp.pad(flat, (0, extra * columns - flat.size)).reshape(extra, columns)

    def dp_rows(w):
        return lax.dynamic_slice_in_dim(w, dp_at * (w.shape[0] // n_dp), w.shape[0] // n_dp, 0).astype(BF)

    p0, p1, p2 = dp_rows(mix), dp_rows(fc1_weight), dp_rows(fc2_weight)
    z0 = shards(jnp.concatenate([p0, flat], axis=0))
    x = lax.dynamic_slice_in_dim(tokens, t_at * own, own, 0)
    cot = lax.dynamic_slice_in_dim(cotangent, t_at * own, own, 0)
    fc1, fc2 = fc1_weight.astype(BF), fc2_weight.astype(BF)
    z0, x, cot, fc1, fc2, p1, p2 = tie(z0, x, cot, fc1, fc2, p1, p2)
    mine0 = jnp.concatenate([z[:p] for z in z0], 0)
    near0, z1 = fetch(mine0), shards(p1)
    near0, z1, p2 = tie(near0, z1, p2)
    mine1 = jnp.concatenate(z1, 0)
    diag0, near1, z2 = fetch_diagonal(*near0), fetch(mine1), shards(p2)
    diag0, near1, z2 = tie(diag0, near1, z2)
    mine2 = jnp.concatenate(z2, 0)
    w_mix = finish(mix, mine0, *near0, *diag0, name="place_mix")
    diag1, near2 = fetch_diagonal(*near1), fetch(mine2)
    flat = jnp.stack([z[p:].reshape(-1)[: 3 * biases.size].astype(F32).reshape(3, -1) for z in z0])
    bias_rel = jnp.concatenate([biases[None], flat[:, 0] + flat[:, 1] + flat[:, 2]], axis=0)
    qv_rel = bias_rel[:, : 2 * lw].reshape(n_t, 2, lw)
    qkv_bias = jnp.stack([qv_rel[:, 0], jnp.zeros_like(qv_rel[:, 0]), qv_rel[:, 1]], axis=1).reshape(n_t, 3 * lw)
    b1_rel = bias_rel[:, 2 * lw :].reshape(-1)
    gain1, gain2 = norm_gains[0:1], norm_gains[1:2]

    def gather(mine):
        return lax.all_gather(mine[0], "tensor", axis=0, tiled=False)

    act1, qkv, attended = [], [], []
    resid, act2, hidden, slope, out_all = [], [], [], [], []
    for i in range(own):
        made = qkv_attn(i, after(x, *hidden[-1:]), gain1, shift_biases[0:1], w_mix, qkv_bias)
        for kept, value in zip((act1, qkv, attended), made):
            kept.append(value)
        if i == 0:
            diag1, near2, head = tie(diag1, near2, attended[0])
            diag2 = fetch_diagonal(*near2)
            w_fc1 = finish(after(fc1, head), mine1, *near1, *diag1, name="place_fc1")
            w_fc1, diag2 = tie(w_fc1, diag2)
            w_fc2 = finish(fc2, mine2, *near2, *diag2, name="place_fc2")
        *kept, out_own = mlp_fwd(
            i, x, attended[i], w_mix, shift_biases[2:3], gain2, shift_biases[1:2], w_fc1, b1_rel, w_fc2, shift_biases[3:4]
        )
        for made, value in zip((resid, act2, hidden, slope), kept):
            made.append(value)
        out_all.append(gather(out_own))
    g_fc2 = grad_fc2(hidden, cot, n_dp, n_t)
    slope[0] = after(slope[0], g_fc2)
    part_fc2 = reduce_dp(g_fc2)
    d_pre, g_b1, d_resid, d_resid_b, d_att, sums2 = [], [], [], [], [], []
    for i in range(own):
        made = mlp_bwd(i, cot, after(slope[i], *d_pre[-1:]), w_fc2, w_fc1, resid[i], gain2, w_mix)
        for kept, value in zip((d_pre, g_b1, d_resid, d_resid_b, d_att, sums2), made):
            kept.append(value)
    part_fc1 = grad_fc1(act2, d_pre, attended, d_resid_b, n_dp, n_t)
    part_fc1, *d_att = tie(part_fc1, *d_att)
    part_fc1 = reduce_dp(part_fc1)
    d_att[0], out_all[0], part_fc2 = tie(d_att[0], out_all[0], part_fc2)
    gt_all = [None] * own

    def attention_back(i):
        def run(made, results):
            d = after(d_att[i], *(made[-1] if made else ()))
            dq, gq, gt_own, s1 = attn_bwd(i, qkv[i], d, w_mix, x, d_resid[i], gain1)
            gt_all[i] = gather(gt_own)
            return dq, gq, s1

        return run

    def attention_grad(made, results):
        d_qkv = [m[0] for m in made]
        d_qkv[-1], out_all[-1] = tie(d_qkv[-1], out_all[-1])
        return grad_qkv(act1, d_qkv, n_dp, n_t)

    rates = (
        1.2 / math.sqrt(D),
        0.6,
        0.6 / math.sqrt(max(D // 128, 1)),
        0.6 / math.sqrt(D),
        0.3,
        0.6 / math.sqrt(max(FF // 8, 1)),
        3.0,
        3.0,
    )
    decays = (MATRIX_DECAY, 0.0, MATRIX_DECAY, MATRIX_DECAY, 0.0, MATRIX_DECAY, 0.0, 0.0)

    def step(at, grad):
        return adamw(weights[at], firsts[at], seconds[at], grad, rates[at], decays[at])

    order = (t_at + n_t - jnp.arange(n_t)) % n_t

    def vectors():
        _, g_qv, sums1 = (sum(v[1:], v[0]) for v in zip(*made[:own]))
        rel = jnp.concatenate([g_qv.reshape(n_t, -1), sum(g_b1).reshape(n_t, -1)], axis=1)
        rel = jnp.take(rel, order, axis=0)
        return jnp.concatenate([rel.reshape(-1), sums1.reshape(-1), sum(sums2).reshape(-1)])

    def fc2_step(made, results):
        return results[1], step(5, results[1])

    def fc1_step(made, results):
        g_fc1, g_proj = results[2][:, :fw], proj_unpack(results[2][:, fw:])
        return g_fc1, g_proj, step(3, g_fc1), step(2, g_proj)

    def waits_for(i):
        return lambda made, results: gt_all[i]

    def nothing(made, results):
        return ()

    made = []
    chains = [
        (own + 1, lambda: sum_chain(vectors())),
        (0, lambda: reduce_chain(part_fc2, "spread_fc2")),
        (own + 1, lambda: reduce_chain(part_fc1, "spread_fc1")),
        (own + 4, lambda: reduce_chain(reduce_dp(made[own]), "spread_qkv")),
    ]
    work = [attention_back(i) for i in range(own)] + [
        attention_grad,
        lambda made, results: weave(out_all),
        waits_for(0),
        nothing,
        nothing if n_t > 4 else fc2_step,
        nothing,
        nothing,
        nothing if n_t > 4 else fc1_step,
        waits_for(-1),
    ]
    flat, g_fc2, g_fc1, g_qkv = run_chains(chains, work, made)
    output, gt_all[0], gt_all[-1] = made[own + 1], made[own + 2], made[-1]
    if n_t > 4:
        made[own + 4], made[own + 7] = fc2_step(made, (None, g_fc2)), fc1_step(made, (None, None, g_fc1))
    (g_fc2, new_fc2), (g_fc1, g_proj, new_fc1, new_proj) = made[own + 4], made[own + 7]
    rel = 2 * lw + fw
    g_qkv = jnp.stack([g_qkv[:, i * lw : (i + 1) * lw] for i in range(3)], axis=1)
    mine = lax.dynamic_index_in_dim(flat[: n_t * rel].reshape(n_t, rel), t_at, 0, keepdims=False)
    rest = flat[n_t * rel :].reshape(6, width)
    g_gains = jnp.stack([rest[0], rest[2]])
    g_shifts = jnp.stack([rest[1], rest[3], rest[4], rest[5]])
    grads = (g_qkv, mine[: 2 * lw].reshape(2, lw), g_proj, g_fc1, mine[2 * lw :], g_fc2, g_gains, g_shifts)
    updated = [step(at, grad) for at, grad in enumerate(grads)]
    updated[3], updated[5], updated[2] = new_fc1, new_fc2, new_proj
    gt_all[-1], *_ = tie(gt_all[-1], *(u[0] for u in updated))
    grad_tokens = weave(gt_all)
    return (
        output,
        grad_tokens,
        *grads,
        *(u[0] for u in updated),
        *(u[1] for u in updated),
        *(u[2] for u in updated),
    )


def solution(mesh):
    weights = (
        P(None, None, "tensor"),
        P(None, "tensor"),
        P("tensor", None),
        P(None, "tensor"),
        P("tensor"),
        P("tensor", None),
        P(),
        P(),
    )
    images = (P("dp", None, None), P("dp", None, None))
    return jax.shard_map(
        per_device,
        mesh=mesh,
        in_specs=images + weights * 3,
        out_specs=images + weights * 4,
        check_vma=False,
    )
```

time: 1280 us -> 652 us (0.51)
  waiting for transfers between devices: 741 us -> 109 us
  matrix products: 213 us -> 0 us
  Pallas kernels: 75.8 us -> 251 us
  starting transfers between devices: 0.68 us -> 98.8 us
  blocking collectives: 64.9 us -> 0 us
  local copies, waits for them, and re-layouts: 93 us -> 125 us
  other arithmetic: 69.9 us -> 43 us
    all_gather x9 -> x4, waiting for transfers between devices: 514 us -> 0.08 us  [gather(): return lax.all_gather(mine[0], 'tensor', axis=0, tiled=False)]
    reduce_scatter x8 -> x3, waiting for transfers between devices: 226 us -> 0.9 us  [reduce_dp(): return lax.psum_scatter(parts, 'dp', scatter_dimension=0, tiled=False)]
    dot_general x30 -> x0, matrix products: 213 us -> none  [the longest x10 95.2 us: matmul_t(): lax.dot_general(left, right, (((left.ndim - 1,), (1,)), ((), ())), prefer...]
    pallas_call x1 -> x17, Pallas kernels: 24.8 us -> 184 us  [the longest x3 47.4 us: shard_grads(): pl.pallas_call(kernel, grid=(g,), in_specs=specs, out_specs=pl.BlockSpec(...]
    ppermute x0 -> x62, waiting for transfers between devices: none -> 108 us  [the longest x35 38.2 us: swap(): return lax.ppermute(value, axis, [(i, i ^ mask) for i in range(n)])]
    ppermute x0 -> x62, starting transfers between devices: none -> 98.4 us  [the longest x35 35.8 us: swap(): return lax.ppermute(value, axis, [(i, i ^ mask) for i in range(n)])]
    unnamed x139 -> x242, local copies, waits for them, and re-layouts: 53.1 us -> 97.9 us
    psum x1 -> x0, blocking collectives: 39.5 us -> none  [per_device(): vecs = lax.psum(vecs, ('dp', 'tensor'))]
  transfers between devices with their start and end apart: 17 -> 69, of which waited for: 13 -> 21; matrix products, arithmetic and copies ran while one was open for 19% -> 11% of each run, Pallas kernels for 2% -> 35%
where the time goes in v2:
time: 652 us; the launch traced here: 644 us
  Pallas kernels  251 us (38%)
  local copies, waits for them, and re-layouts  125 us (19%)
  waiting for transfers between devices  109 us (17%)
  starting transfers between devices  98.8 us (15%)
  other arithmetic  43 us (7%)
  between operations  17.5 us (3%)
    unnamed x242, local copies, waits for them, and re-layouts  97.9 us
    pallas_call x2, Pallas kernels, attn_bwd(): pl.pallas_call(attn_bwd_kernel, grid=(n, g), in_specs=[pl.BlockSpec((1, s...  66.3 us
    pallas_call x3, Pallas kernels, shard_grads(): pl.pallas_call(kernel, grid=(g,), in_specs=specs, out_specs=pl.BlockSpec(...  47.4 us
    pallas_call x2, Pallas kernels, mlp_bwd(): pl.pallas_call(mlp_bwd_kernel, grid=(n, ff // tile), in_specs=[own, hidde...  40.3 us
    ppermute x35, waiting for transfers between devices, swap(): return lax.ppermute(value, axis, [(i, i ^ mask) for i in range(n)])  38.2 us
    ppermute x35, starting transfers between devices, swap(): return lax.ppermute(value, axis, [(i, i ^ mask) for i in range(n)])  35.8 us
    pallas_call x2, Pallas kernels, mlp_fwd(): pl.pallas_call(mlp_fwd_kernel, grid=(n, ff // tile), in_specs=[own, img,...  34.8 us
    pallas_call x2, Pallas kernels, qkv_attn(): pl.pallas_call(qkv_attn_kernel, grid=(n, g), in_specs=[pl.BlockSpec((1, s...  34.4 us
  transfers between devices with their start and end apart: 69, of which 21 were waited for; matrix products, arithmetic and copies ran while one was open for 11% of the time, Pallas kernels for 35%

profile of v2, /device:TPU:0, one launch (start us, length us, event | category | flops | bytes accessed | tf_op | source)
XLA Modules:
  0.0 643.9 jit_solution(13019504223331933195)
XLA Ops:
  8.1 2.1 convert.27
  13.4 3.0 collective-permute-start
  16.4 2.6 collective-permute-start.1
  20.4 9.4 %constant_dynamic-slice_fusion = (bf16[2,577,1024]{2,0,1:T(2,128)(2,1)S(1)}, bf16[2,577,1024]{2,0,1:T(2,128)(2,1)S(1)}) fusion(bf16[8,577,1024]{2,0,1:T(8,128)(2,1)} %param.27, s32[]{:T(128)S(6)} %select_n.58, bf16[8,577,1024]{2,0,1:T(8,128)(2,1)} %param.26), kind=kLoop, calls=%fused_computation.171 | loop fusion | bytes 9453572 | tf_op jit(solution)/shard_map/dynamic_slice | solution.py:503
  30.5 2.1 copy.88.refs_2_.refs_3_.cot_ref
  43.9 6.8 %collective-permute-start.5 = (bf16[128,1024]{1,0:T(8,128)(2,1)S(1)}, bf16[128,1024]{1,0:T(8,128)(2,1)S(1)}, u32[]{:S(2)}, u32[]{:S(2)}) collective-permute-start(bf16[128,1024]{1,0:T(8,128)(2,1)S(1)} %get-tuple-element.175), channel_id=1, source_target_pairs={{0,1},{1,2},{2,3},{3,0},{4,5},{5,6},{6,7},{7,4},{8,9},{9,10},{10,1... | collective-permute-start | bytes 786440 | tf_op jit(solution)/shard_map/ppermute | solution.py:316
  53.0 6.0 collective-permute-done.5
  59.1 8.9 %collective-permute-done.6 = bf16[128,1024]{1,0:T(8,128)(2,1)S(1)} collective-permute-done((bf16[128,1024]{1,0:T(8,128)(2,1)S(1)}, bf16[128,1024]{1,0:T(8,128)(2,1)S(1)}, u32[]{:S(2)}, u32[]{:S(2)}) %collective-permute-start.6) | collective-permute-done | bytes 262176 | tf_op jit(solution)/shard_map/ppermute | solution.py:316
  71.4 6.1 collective-permute-start.12
  77.4 2.3 collective-permute-start.13
  81.4 5.2 collective-permute-done.12
  88.1 7.2 %collective-permute-done.13 = bf16[128,1024]{1,0:T(8,128)(2,1)} collective-permute-done((bf16[128,1024]{1,0:T(8,128)(2,1)S(1)}, bf16[128,1024]{1,0:T(8,128)(2,1)}, u32[]{:S(2)}, u32[]{:S(2)}) %collective-permute-start.13) | collective-permute-done | bytes 262176 | tf_op jit(solution)/shard_map/ppermute | solution.py:316
  98.9 4.6 collective-permute-done.14
  120.7 4.1 place_mix.1.w_ref.pw_ref
  124.8 17.1 %qkv_attn.2 = (bf16[1,577,1024]{2,1,0:T(8,128)(2,1)S(1)}, bf16[1,577,3072]{2,1,0:T(8,128)(2,1)S(1)}, bf16[1,577,1024]{2,1,0:T(8,128)(2,1)S(1)}) custom-call(bf16[2,577,1024]{2,1,0:T(8,128)(2,1)S(1)} %copy.87.x_ref, f32[1,1024]{1,0:T(1,128)S(1)} %get-tuple-element.404.gain_ref, f32[1,1024]{1,0:T(1,128)S(1)} %get-tuple-element.392.shift_ref, ...), custom_call_target="tpu_custom_call" | custom-call | flops 1000000 | bytes 1000000 | tf_op jit(solution)/shard_map/qkv_attn/pallas_call | solution.py:76
  147.5 3.5 collective-permute-done.20.far_ref
  154.6 2.7 place_fc1.1.w1_ref
  157.3 3.4 copy-done.2
  161.0 5.5 collective-permute-done.23.far_ref
  167.4 3.3 copy-done.3
  170.7 17.2 %mlp_fwd.2 = (f32[1,577,1024]{2,1,0:T(8,128)S(1)}, bf16[1,577,1024]{2,1,0:T(8,128)(2,1)S(1)}, bf16[1,577,4096]{2,1,0:T(8,128)(2,1)S(1)}, bf16[1,577,4096]{2,1,0:T(8,128)(2,1)S(1)}, bf16[1,577,1024]{2,1,0:T(8,128)(2,1)S(1)}) custom-call(bf16[2,577,1024]{2,1,0:T(8,128)(2,1)S(1)} %copy.87.x_ref, bf16[1,577,1024]{2,1,0:T(8,128)(2,1)S(1)} %get-tuple-element.185.att_ref.refs_4_, ...), custom_call_target="tpu_custom_call" | custom-call | flops 1000000 | bytes 1000000 | tf_op jit(solution)/shard_map/mlp_fwd/pallas_call | solution.py:118
  187.9 2.2 copy-done.11
  190.1 2.2 copy-done.15
  195.8 3.4 copy-done.1
  199.2 17.2 %qkv_attn.3 = (bf16[1,577,1024]{2,1,0:T(8,128)(2,1)S(1)}, bf16[1,577,3072]{2,1,0:T(8,128)(2,1)S(1)}, bf16[1,577,1024]{2,1,0:T(8,128)(2,1)S(1)}) custom-call(bf16[2,577,1024]{2,1,0:T(8,128)(2,1)S(1)} %copy.87.x_ref, f32[1,1024]{1,0:T(1,128)S(1)} %get-tuple-element.404.gain_ref, f32[1,1024]{1,0:T(1,128)S(1)} %get-tuple-element.392.shift_ref, ...), custom_call_target="tpu_custom_call" | custom-call | flops 1000000 | bytes 1000000 | tf_op jit(solution)/shard_map/qkv_attn/pallas_call | solution.py:76
  219.3 17.7 %mlp_fwd.3 = (f32[1,577,1024]{2,1,0:T(8,128)S(1)}, bf16[1,577,1024]{2,1,0:T(8,128)(2,1)S(1)}, bf16[1,577,4096]{2,1,0:T(8,128)(2,1)S(1)}, bf16[1,577,4096]{2,1,0:T(8,128)(2,1)S(1)}, bf16[1,577,1024]{2,1,0:T(8,128)(2,1)S(1)}) custom-call(bf16[2,577,1024]{2,1,0:T(8,128)(2,1)S(1)} %copy.87.x_ref, bf16[1,577,1024]{2,1,0:T(8,128)(2,1)S(1)} %get-tuple-element.203.att_ref.refs_5_, ...), custom_call_target="tpu_custom_call" | custom-call | flops 1000000 | bytes 1000000 | tf_op jit(solution)/shard_map/mlp_fwd/pallas_call | solution.py:118
  237.0 2.1 copy-done.12
  242.6 15.8 %grad_fc2.1 = bf16[8,4,128,1024]{3,2,1,0:T(8,128)(2,1)} custom-call(bf16[1,577,4096]{2,1,0:T(8,128)(2,1)S(1)} %bitcast.131, bf16[1,577,4096]{2,1,0:T(8,128)(2,1)S(1)} %get-tuple-element.207.refs_1_, bf16[2,577,1024]{2,1,0:T(8,128)(2,1)S(1)} %copy-done.4, bf16[2,577,1024]{2,1,0:T(8,128)(2,1)S(1)} %copy-done.4), custom_call_target="tpu_custom_call" | custom-call | flops 1000000 | bytes 1000000 | tf_op jit(solution)/shard_map/grad_fc2/pallas_call | solution.py:264
  262.6 20.8 %mlp_bwd.2 = (bf16[1,577,4096]{2,1,0:T(8,128)(2,1)S(1)}, f32[1,4,1,1024]{3,2,1,0:T(1,128)S(1)}, f32[1,577,1024]{2,1,0:T(8,128)S(1)}, bf16[1,577,1024]{2,1,0:T(8,...) custom-call(bf16[2,577,1024]{2,1,0:T(8,128)(2,1)S(1)} %copy-done.5, ...), custom_call_target="tpu_custom_call" | custom-call | flops 1000000 | bytes 1000000 | tf_op jit(solution)/shard_map/mlp_bwd/pallas_call | solution.py:172
  285.9 19.5 %mlp_bwd.3 = (bf16[1,577,4096]{2,1,0:T(8,128)(2,1)S(1)}, f32[1,4,1,1024]{3,2,1,0:T(1,128)S(1)}, f32[1,577,1024]{2,1,0:T(8,128)S(1)}, bf16[1,577,1024]{2,1,0:T(8,...) custom-call(bf16[2,577,1024]{2,1,0:T(8,128)(2,1)S(1)} %copy-done.5, ...), custom_call_target="tpu_custom_call" | custom-call | flops 1000000 | bytes 1000000 | tf_op jit(solution)/shard_map/mlp_bwd/pallas_call | solution.py:172
  307.9 20.1 %grad_fc1.1 = bf16[8,4,128,1280]{3,2,1,0:T(8,128)(2,1)} custom-call(bf16[1,577,1024]{2,1,0:T(8,128)(2,1)S(1)} %copy-done.52, bf16[1,577,1024]{2,1,0:T(8,128)(2,1)S(1)} %copy-done.54, bf16[1,577,4096]{2,1,0:T(8,128)(2,1)S(1)} %get-tuple-element.210.refs_2_, bf16[1,577,4096]{2,1,0:T(8,128)(2,1)S(1)} %get-tuple-element.214.refs_3_, ...), custom_call_target="tpu_custom_call" | custom-call | flops 1000000 | bytes 1000000 | tf_op jit(solution)/shard_map/grad_fc1/pallas_call | solution.py:264
  333.9 32.7 %attn_bwd.2 = (bf16[1,577,3072]{2,1,0:T(8,128)(2,1)S(1)}, f32[1,4,2,256]{3,2,1,0:T(2,128)S(1)}, bf16[1,577,1024]{2,1,0:T(8,128)(2,1)S(1)}, f32[1,2,1024]{2,1,0:T(2,128)S(1)}) custom-call(bf16[1,577,3072]{2,1,0:T(8,128)(2,1)S(1)} %copy-done.21, bf16[1,577,1024]{2,1,0:T(8,128)(2,1)S(1)} %copy-done.43, bf16[4,1024,1024]{2,1,0:T(8,128)(2,1)} %copy-done, ...), custom_call_target="tpu_custom_call" | custom-call | flops 1000000 | bytes 1000000 | tf_op jit(solution)/shard_map/attn_bwd/pallas_call | solution.py:232
  369.8 3.6 collective-permute-start.24
  374.1 4.7 collective-permute-done.24
  378.9 4.4 collective-permute-start.26
  384.1 2.4 copy-done.23
  388.5 33.6 %attn_bwd.3 = (bf16[1,577,3072]{2,1,0:T(8,128)(2,1)S(1)}, f32[1,4,2,256]{3,2,1,0:T(2,128)S(1)}, bf16[1,577,1024]{2,1,0:T(8,128)(2,1)}, f32[1,2,1024]{2,1,0:T(2,128)S(1)}) custom-call(bf16[1,577,3072]{2,1,0:T(8,128)(2,1)S(1)} %copy-done.23, bf16[1,577,1024]{2,1,0:T(8,128)(2,1)S(1)} %copy-done.41, bf16[4,1024,1024]{2,1,0:T(8,128)(2,1)} %copy-done, ...), custom_call_target="tpu_custom_call" | custom-call | flops 1000000 | bytes 1000000 | tf_op jit(solution)/shard_map/attn_bwd/pallas_call | solution.py:232
  424.1 4.6 collective-permute-start.29
  436.9 11.5 %grad_qkv.1 = bf16[8,4,128,768]{3,2,1,0:T(8,128)(2,1)S(1)} custom-call(bf16[1,577,1024]{2,1,0:T(8,128)(2,1)S(1)} %copy-done.48, bf16[1,577,1024]{2,1,0:T(8,128)(2,1)S(1)} %copy-done.50, bf16[1,577,3072]{2,1,0:T(8,128)(2,1)S(1)} %copy-done.25, bf16[1,577,3072]{2,1,0:T(8,128)(2,1)S(1)} %copy-done.27), custom_call_target="tpu_custom_call" | custom-call | flops 1000000 | bytes 1000000 | tf_op jit(solution)/shard_map/grad_qkv/pallas_call | solution.py:264
  448.4 2.7 copy-done.6
  453.3 4.8 collective-permute-start.33
  461.8 3.0 copy-done.13
  464.8 3.0 copy-done.14
  467.8 8.1 %weave.2 = bf16[577,8,1024]{2,1,0:T(8,128)(2,1)} custom-call(bf16[4,577,1024]{2,1,0:T(8,128)(2,1)S(1)} %copy-done.13, bf16[4,577,1024]{2,1,0:T(8,128)(2,1)S(1)} %copy-done.14), custom_call_target="tpu_custom_call" | custom-call | flops 1000000 | bytes 1000000 | tf_op jit(solution)/shard_map/weave/pallas_call | solution.py:297
  482.1 8.9 %collective-permute-done.35 = f32[12288]{0:T(1024)S(1)} collective-permute-done((f32[12288]{0:T(1024)S(1)}, f32[12288]{0:T(1024)S(1)}, u32[]{:S(2)}, u32[]{:S(2)}) %collective-permute-start.35) | collective-permute-done | bytes 49184 | tf_op jit(solution)/shard_map/ppermute | solution.py:321
  492.7 4.8 collective-permute-start.42
  500.0 3.0 collective-permute-done.40
  503.0 5.3 collective-permute-done.42
  508.3 12.0 %collective-permute-done.43 = bf16[128,1280]{1,0:T(8,128)(2,1)S(1)} collective-permute-done((bf16[128,1280]{1,0:T(8,128)(2,1)S(1)}, bf16[128,1280]{1,0:T(8,128)(2,1)S(1)}, u32[]{:S(2)}, u32[]{:S(2)}) %collective-permute-start.43) | collective-permute-done | bytes 327712 | tf_op jit(solution)/shard_map/ppermute | solution.py:429
  523.9 4.0 collective-permute-start.44
  534.4 9.3 %multiply_subtract_fusion.1 = (f32[1024,1024]{1,0:T(8,128)}, f32[1024,1024]{1,0:T(8,128)}, f32[1024,1024]{1,0:T(8,128)}) fusion(f32[1024,1024]{1,0:T(8,128)} %param.33, bf16[1024,1024]{1,0:T(8,128)(2,1)S(1)} %spread_fc2.1, f32[1024,1024]{1,0:T(8,128)} %param.41, f32[1024,1024]{1,0:T(8,128)} %param.49), kind=kLoop, calls=%fused_computation.8 | loop fusion | flops 16777216 | bytes 27262976 | tf_op jit(solution)/shard_map/sub | solution.py:308
  543.6 2.5 convert_element_type.268
  549.3 2.5 collective-permute-start.49
  552.7 2.3 collective-permute-start.50
  559.1 12.1 %collective-permute-done.49 = f32[12288]{0:T(1024)S(1)} collective-permute-done((f32[12288]{0:T(1024)S(1)}, f32[12288]{0:T(1024)S(1)}, u32[]{:S(2)}, u32[]{:S(2)}) %collective-permute-start.49) | collective-permute-done | bytes 49184 | tf_op jit(solution)/shard_map/ppermute | solution.py:321
  576.1 7.8 %collective-permute-done.55 = bf16[128,768]{1,0:T(8,128)(2,1)S(1)} collective-permute-done((bf16[128,768]{1,0:T(8,128)(2,1)S(1)}, bf16[128,768]{1,0:T(8,128)(2,1)S(1)}, u32[]{:S(2)}, u32[]{:S(2)}) %collective-permute-start.55) | collective-permute-done | bytes 196640 | tf_op jit(solution)/shard_map/ppermute | solution.py:428
  583.9 7.4 %collective-permute-done.56 = bf16[128,768]{1,0:T(8,128)(2,1)S(1)} collective-permute-done((bf16[128,768]{1,0:T(8,128)(2,1)S(1)}, bf16[128,768]{1,0:T(8,128)(2,1)S(1)}, u32[]{:S(2)}, u32[]{:S(2)}) %collective-permute-start.56) | collective-permute-done | bytes 196640 | tf_op jit(solution)/shard_map/ppermute | solution.py:429
  597.0 5.8 multiply_subtract_fusion
  602.8 2.2 multiply_subtract_fusion.3
  605.2 2.6 slice.344
  609.9 2.7 collective-permute-done.59
  616.3 2.1 spread_qkv.1
  622.3 5.8 multiply_subtract_fusion.2
  628.1 8.2 %weave.3 = bf16[577,8,1024]{2,1,0:T(8,128)(2,1)} custom-call(bf16[4,577,1024]{2,1,0:T(8,128)(2,1)S(1)} %bitcast.127, bf16[4,577,1024]{2,1,0:T(8,128)(2,1)S(1)} %bitcast.129), custom_call_target="tpu_custom_call" | custom-call | flops 1000000 | bytes 1000000 | tf_op jit(solution)/shard_map/weave/pallas_call | solution.py:297
  (452 shorter events, 151.8 us)
Async XLA Ops:
  8.0 320.1 %all-gather.5.cloned.1.call-start = ((), (), s32[]{:S(2)}) async-start(), calls=%async_computation.3 | async-start | bytes 5980160 | tf_op jit(solution)/shard_map/all_gather | solution.py:523
  13.4 24.8 %collective-permute-start = (bf16[144,1024]{1,0:T(8,128)(2,1)}, bf16[144,1024]{1,0:T(8,128)(2,1)S(1)}, u32[]{:S(2)}, u32[]{:S(2)}) collective-permute-start(bf16[144,1024]{1,0:T(8,128)(2,1)} %pad_maximum_fusion.3), channel_id=1, source_target_pairs={{0,1},{1,2},{2,3},{3,0},{4,5},{5,6},{6,7},{7,4},{8,9},{9,10},{10,1... | collective-permute-start | bytes 884744 | tf_op jit(solution)/shard_map/ppermute | solution.py:316
  16.4 22.0 %collective-permute-start.1 = (bf16[144,1024]{1,0:T(8,128)(2,1)}, bf16[144,1024]{1,0:T(8,128)(2,1)S(1)}, u32[]{:S(2)}, u32[]{:S(2)}) collective-permute-start(bf16[144,1024]{1,0:T(8,128)(2,1)} %pad_maximum_fusion.3), channel_id=1, source_target_pairs={{0,2},{1,3},{2,0},{3,1},{4,6},{5,7},{6,4},{7,5},{8,10},{9,11},{10,... | collective-permute-start | bytes 884744 | tf_op jit(solution)/shard_map/ppermute | solution.py:316
  19.0 19.4 %collective-permute-start.2 = (bf16[144,1024]{1,0:T(8,128)(2,1)}, bf16[144,1024]{1,0:T(8,128)(2,1)S(1)}, u32[]{:S(2)}, u32[]{:S(2)}) collective-permute-start(bf16[144,1024]{1,0:T(8,128)(2,1)} %pad_maximum_fusion.3), channel_id=1, source_target_pairs={{0,3},{1,0},{2,1},{3,2},{4,7},{5,4},{6,5},{7,6},{8,11},{9,8},{10,9... | collective-permute-start | bytes 884744 | tf_op jit(solution)/shard_map/ppermute | solution.py:316
  40.8 27.1 %collective-permute-start.3 = (bf16[384,1024]{1,0:T(8,128)(2,1)S(1)}, bf16[384,1024]{1,0:T(8,128)(2,1)S(1)}, u32[]{:S(2)}, u32[]{:S(2)}) collective-permute-start(bf16[384,1024]{1,0:T(8,128)(2,1)S(1)} %pad_maximum_fusion.2), channel_id=1, source_target_pairs={{0,8},{4,12},{8,0},{12,4},{16,24},{20,28},{24,16},{28,20},{1,9},{5... | collective-permute-start | bytes 2359304 | tf_op jit(solution)/shard_map/ppermute | solution.py:321
  42.4 25.6 %collective-permute-start.4 = (bf16[384,1024]{1,0:T(8,128)(2,1)S(1)}, bf16[384,1024]{1,0:T(8,128)(2,1)S(1)}, u32[]{:S(2)}, u32[]{:S(2)}) collective-permute-start(bf16[384,1024]{1,0:T(8,128)(2,1)S(1)} %pad_maximum_fusion.2), channel_id=1, source_target_pairs={{0,16},{4,20},{8,24},{12,28},{16,0},{20,4},{24,8},{28,12},{1,17},{... | collective-permute-start | bytes 2359304 | tf_op jit(solution)/shard_map/ppermute | solution.py:321
  43.9 15.1 %collective-permute-start.5 = (bf16[128,1024]{1,0:T(8,128)(2,1)S(1)}, bf16[128,1024]{1,0:T(8,128)(2,1)S(1)}, u32[]{:S(2)}, u32[]{:S(2)}) collective-permute-start(bf16[128,1024]{1,0:T(8,128)(2,1)S(1)} %get-tuple-element.175), channel_id=1, source_target_pairs={{0,1},{1,2},{2,3},{3,0},{4,5},{5,6},{6,7},{7,4},{8,9},{9,10},{10,1... | collective-permute-start | bytes 786440 | tf_op jit(solution)/shard_map/ppermute | solution.py:316
  50.7 17.3 %collective-permute-start.6 = (bf16[128,1024]{1,0:T(8,128)(2,1)S(1)}, bf16[128,1024]{1,0:T(8,128)(2,1)S(1)}, u32[]{:S(2)}, u32[]{:S(2)}) collective-permute-start(bf16[128,1024]{1,0:T(8,128)(2,1)S(1)} %get-tuple-element.175), channel_id=1, source_target_pairs={{0,2},{1,3},{2,0},{3,1},{4,6},{5,7},{6,4},{7,5},{8,10},{9,11},{10,... | collective-permute-start | bytes 786440 | tf_op jit(solution)/shard_map/ppermute | solution.py:316
  52.3 15.7 %collective-permute-start.7 = (bf16[128,1024]{1,0:T(8,128)(2,1)S(1)}, bf16[128,1024]{1,0:T(8,128)(2,1)S(1)}, u32[]{:S(2)}, u32[]{:S(2)}) collective-permute-start(bf16[128,1024]{1,0:T(8,128)(2,1)S(1)} %get-tuple-element.175), channel_id=1, source_target_pairs={{0,3},{1,0},{2,1},{3,2},{4,7},{5,4},{6,5},{7,6},{8,11},{9,8},{10,9... | collective-permute-start | bytes 786440 | tf_op jit(solution)/shard_map/ppermute | solution.py:316
  70.3 33.3 %collective-permute-start.10 = (bf16[384,1024]{1,0:T(8,128)(2,1)S(1)}, bf16[384,1024]{1,0:T(8,128)(2,1)S(1)}, u32[]{:S(2)}, u32[]{:S(2)}) collective-permute-start(bf16[384,1024]{1,0:T(8,128)(2,1)S(1)} %get-tuple-element.378), channel_id=1, source_target_pairs={{0,8},{4,12},{8,0},{12,4},{16,24},{20,28},{24,16},{28,20},{1,9},{5... | collective-permute-start | bytes 2359304 | tf_op jit(solution)/shard_map/ppermute | solution.py:321
  70.9 32.7 %collective-permute-start.11 = (bf16[384,1024]{1,0:T(8,128)(2,1)S(1)}, bf16[384,1024]{1,0:T(8,128)(2,1)S(1)}, u32[]{:S(2)}, u32[]{:S(2)}) collective-permute-start(bf16[384,1024]{1,0:T(8,128)(2,1)S(1)} %get-tuple-element.378), channel_id=1, source_target_pairs={{0,16},{4,20},{8,24},{12,28},{16,0},{20,4},{24,8},{28,12},{1,17},{... | collective-permute-start | bytes 2359304 | tf_op jit(solution)/shard_map/ppermute | solution.py:321
  71.4 15.3 %collective-permute-start.12 = (bf16[128,1024]{1,0:T(8,128)(2,1)S(1)}, bf16[128,1024]{1,0:T(8,128)(2,1)}, u32[]{:S(2)}, u32[]{:S(2)}) collective-permute-start(bf16[128,1024]{1,0:T(8,128)(2,1)S(1)} %get-tuple-element.182), channel_id=1, source_target_pairs={{0,1},{1,2},{2,3},{3,0},{4,5},{5,6},{6,7},{7,4},{8,9},{9,10},{10,1... | collective-permute-start | bytes 786440 | tf_op jit(solution)/shard_map/ppermute | solution.py:316
  77.4 17.9 %collective-permute-start.13 = (bf16[128,1024]{1,0:T(8,128)(2,1)S(1)}, bf16[128,1024]{1,0:T(8,128)(2,1)}, u32[]{:S(2)}, u32[]{:S(2)}) collective-permute-start(bf16[128,1024]{1,0:T(8,128)(2,1)S(1)} %get-tuple-element.182), channel_id=1, source_target_pairs={{0,2},{1,3},{2,0},{3,1},{4,6},{5,7},{6,4},{7,5},{8,10},{9,11},{10,... | collective-permute-start | bytes 786440 | tf_op jit(solution)/shard_map/ppermute | solution.py:316
  79.8 23.7 %collective-permute-start.8 = (bf16[192,1024]{1,0:T(8,128)(2,1)S(1)}, bf16[192,1024]{1,0:T(8,128)(2,1)S(1)}, u32[]{:S(2)}, u32[]{:S(2)}) collective-permute-start(bf16[192,1024]{1,0:T(8,128)(2,1)S(1)} %slice.260), channel_id=1, source_target_pairs={{0,16},{4,20},{8,24},{12,28},{16,0},{20,4},{24,8},{28,12},{1,17},{... | collective-permute-start | bytes 1179656 | tf_op jit(solution)/shard_map/ppermute | solution.py:321
  86.6 16.9 %collective-permute-start.9 = (bf16[192,1024]{1,0:T(8,128)(2,1)S(1)}, bf16[192,1024]{1,0:T(8,128)(2,1)S(1)}, u32[]{:S(2)}, u32[]{:S(2)}) collective-permute-start(bf16[192,1024]{1,0:T(8,128)(2,1)S(1)} %slice.261), channel_id=1, source_target_pairs={{0,8},{4,12},{8,0},{12,4},{16,24},{20,28},{24,16},{28,20},{1,9},{5... | collective-permute-start | bytes 1179656 | tf_op jit(solution)/shard_map/ppermute | solution.py:321
  95.3 8.2 %collective-permute-start.14 = (bf16[128,1024]{1,0:T(8,128)(2,1)S(1)}, bf16[128,1024]{1,0:T(8,128)(2,1)S(1)}, u32[]{:S(2)}, u32[]{:S(2)}) collective-permute-start(bf16[128,1024]{1,0:T(8,128)(2,1)S(1)} %get-tuple-element.182), channel_id=1, source_target_pairs={{0,3},{1,0},{2,1},{3,2},{4,7},{5,4},{6,5},{7,6},{8,11},{9,8},{10,9... | collective-permute-start | bytes 786440 | tf_op jit(solution)/shard_map/ppermute | solution.py:316
  105.2 15.4 %collective-permute-start.15 = (bf16[1536,1024]{1,0:T(8,128)(2,1)}, bf16[1536,1024]{1,0:T(8,128)(2,1)}, u32[]{:S(2)}, u32[]{:S(2)}) collective-permute-start(bf16[1536,1024]{1,0:T(8,128)(2,1)} %constant_dynamic-update-slice_fusion.4.near_ref), channel_id=1, source_target_pairs={{0,4},{4,0},{8,12},{12,8},{16,20},{20,16},{24,28},{28,24},{1,5},{5... | collective-permute-start | bytes 9437192 | tf_op jit(solution)/shard_map/ppermute | solution.py:321
  113.8 29.8 %collective-permute-start.18 = (bf16[384,1024]{1,0:T(8,128)(2,1)}, bf16[384,1024]{1,0:T(8,128)(2,1)S(1)}, u32[]{:S(2)}, u32[]{:S(2)}) collective-permute-start(bf16[384,1024]{1,0:T(8,128)(2,1)} %get-tuple-element.372), channel_id=1, source_target_pairs={{0,8},{4,12},{8,0},{12,4},{16,24},{20,28},{24,16},{28,20},{1,9},{5... | collective-permute-start | bytes 2359304 | tf_op jit(solution)/shard_map/ppermute | solution.py:321
  115.3 28.3 %collective-permute-start.19 = (bf16[384,1024]{1,0:T(8,128)(2,1)}, bf16[384,1024]{1,0:T(8,128)(2,1)S(1)}, u32[]{:S(2)}, u32[]{:S(2)}) collective-permute-start(bf16[384,1024]{1,0:T(8,128)(2,1)} %get-tuple-element.372), channel_id=1, source_target_pairs={{0,16},{4,20},{8,24},{12,28},{16,0},{20,4},{24,8},{28,12},{1,17},{... | collective-permute-start | bytes 2359304 | tf_op jit(solution)/shard_map/ppermute | solution.py:321
  116.8 26.7 %collective-permute-start.16 = (bf16[192,1024]{1,0:T(8,128)(2,1)S(1)}, bf16[192,1024]{1,0:T(8,128)(2,1)S(1)}, u32[]{:S(2)}, u32[]{:S(2)}) collective-permute-start(bf16[192,1024]{1,0:T(8,128)(2,1)S(1)} %slice.277), channel_id=1, source_target_pairs={{0,16},{4,20},{8,24},{12,28},{16,0},{20,4},{24,8},{28,12},{1,17},{... | collective-permute-start | bytes 1179656 | tf_op jit(solution)/shard_map/ppermute | solution.py:321
  118.2 25.4 %collective-permute-start.17 = (bf16[192,1024]{1,0:T(8,128)(2,1)}, bf16[192,1024]{1,0:T(8,128)(2,1)S(1)}, u32[]{:S(2)}, u32[]{:S(2)}) collective-permute-start(bf16[192,1024]{1,0:T(8,128)(2,1)} %slice.278), channel_id=1, source_target_pairs={{0,8},{4,12},{8,0},{12,4},{16,24},{20,28},{24,16},{28,20},{1,9},{5... | collective-permute-start | bytes 1179656 | tf_op jit(solution)/shard_map/ppermute | solution.py:321
  145.2 5.9 collective-permute-start.20
  145.2 15.5 %collective-permute-start.21 = (bf16[192,1024]{1,0:T(8,128)(2,1)S(1)}, bf16[192,1024]{1,0:T(8,128)(2,1)S(1)}, u32[]{:S(2)}, u32[]{:S(2)}) collective-permute-start(bf16[192,1024]{1,0:T(8,128)(2,1)S(1)} %slice.279), channel_id=1, source_target_pairs={{0,16},{4,20},{8,24},{12,28},{16,0},{20,4},{24,8},{28,12},{1,17},{... | collective-permute-start | bytes 1179656 | tf_op jit(solution)/shard_map/ppermute | solution.py:321
  146.8 13.9 %collective-permute-start.22 = (bf16[192,1024]{1,0:T(8,128)(2,1)S(1)}, bf16[192,1024]{1,0:T(8,128)(2,1)S(1)}, u32[]{:S(2)}, u32[]{:S(2)}) collective-permute-start(bf16[192,1024]{1,0:T(8,128)(2,1)S(1)} %slice.280), channel_id=1, source_target_pairs={{0,8},{4,12},{8,0},{12,4},{16,24},{20,28},{24,16},{28,20},{1,9},{5... | collective-permute-start | bytes 1179656 | tf_op jit(solution)/shard_map/ppermute | solution.py:321
  160.8 5.7 collective-permute-start.23
  195.8 133.2 %reduce-scatter.4.cloned.1.call-start = ((), (), s32[]{:S(2)}) async-start(), calls=%async_computation.4 | async-start | bytes 9437184 | tf_op jit(solution)/shard_map/reduce_scatter | solution.py:403
  258.5 171.7 %all-gather.7.cloned.1.call-start = ((), (), s32[]{:S(2)}) async-start(), calls=%async_computation.5 | async-start | bytes 5980160 | tf_op jit(solution)/shard_map/all_gather | solution.py:523
  259.2 193.0 %reduce-scatter.6.cloned.1.call-start = ((), (), s32[]{:S(2)}) async-start(), calls=%async_computation.6 | async-start | bytes 11796480 | tf_op jit(solution)/shard_map/reduce_scatter | solution.py:403
  328.0 163.0 %all-gather.9.cloned.1.call-start = ((), (), s32[]{:S(2)}) async-start(), calls=%async_computation.7 | async-start | bytes 5980160 | tf_op jit(solution)/shard_map/all_gather | solution.py:523
  369.5 161.2 %reduce-scatter.8.cloned.1.call-start = ((), (), s32[]{:S(2)}) async-start(), calls=%async_computation.8 | async-start | bytes 7077888 | tf_op jit(solution)/shard_map/reduce_scatter | solution.py:403
  369.8 9.0 %collective-permute-start.24 = (bf16[128,1024]{1,0:T(8,128)(2,1)S(1)}, bf16[128,1024]{1,0:T(8,128)(2,1)S(1)}, u32[]{:S(2)}, u32[]{:S(2)}) collective-permute-start(bf16[128,1024]{1,0:T(8,128)(2,1)S(1)} %get-tuple-element.358), channel_id=1, source_target_pairs={{0,1},{4,5},{8,9},{12,13},{16,17},{20,21},{24,25},{28,29}} | collective-permute-start | bytes 786440 | tf_op jit(solution)/shard_map/ppermute | solution.py:428
  378.9 44.9 %collective-permute-start.26 = (bf16[128,1024]{1,0:T(8,128)(2,1)S(1)}, bf16[128,1024]{1,0:T(8,128)(2,1)S(1)}, u32[]{:S(2)}, u32[]{:S(2)}) collective-permute-start(bf16[128,1024]{1,0:T(8,128)(2,1)S(1)} %get-tuple-element.356), channel_id=1, source_target_pairs={{0,1},{1,2},{4,5},{5,6},{8,9},{9,10},{12,13},{13,14},{16,17},{17,1... | collective-permute-start | bytes 786440 | tf_op jit(solution)/shard_map/ppermute | solution.py:428
  383.4 40.5 %collective-permute-start.27 = (bf16[128,1024]{1,0:T(8,128)(2,1)S(1)}, bf16[128,1024]{1,0:T(8,128)(2,1)S(1)}, u32[]{:S(2)}, u32[]{:S(2)}) collective-permute-start(bf16[128,1024]{1,0:T(8,128)(2,1)S(1)} %get-tuple-element.355), channel_id=1, source_target_pairs={{3,2},{2,1},{7,6},{6,5},{11,10},{10,9},{15,14},{14,13},{19,18},{18... | collective-permute-start | bytes 786440 | tf_op jit(solution)/shard_map/ppermute | solution.py:429
  424.1 27.0 %collective-permute-start.29 = (bf16[128,1024]{1,0:T(8,128)(2,1)S(1)}, bf16[128,1024]{1,0:T(8,128)(2,1)S(1)}, u32[]{:S(2)}, u32[]{:S(2)}) collective-permute-start(bf16[128,1024]{1,0:T(8,128)(2,1)S(1)} %get-tuple-element.354), channel_id=1, source_target_pairs={{0,1},{1,2},{2,3},{4,5},{5,6},{6,7},{8,9},{9,10},{10,11},{12,13},{... | collective-permute-start | bytes 786440 | tf_op jit(solution)/shard_map/ppermute | solution.py:428
  428.7 22.6 %collective-permute-start.30 = (bf16[128,1024]{1,0:T(8,128)(2,1)S(1)}, bf16[128,1024]{1,0:T(8,128)(2,1)S(1)}, u32[]{:S(2)}, u32[]{:S(2)}) collective-permute-start(bf16[128,1024]{1,0:T(8,128)(2,1)S(1)} %get-tuple-element.353), channel_id=1, source_target_pairs={{3,2},{2,1},{1,0},{7,6},{6,5},{5,4},{11,10},{10,9},{9,8},{15,14},{... | collective-permute-start | bytes 786440 | tf_op jit(solution)/shard_map/ppermute | solution.py:429
  451.3 158.6 %all-gather.11.cloned.1.call-start = ((), (), s32[]{:S(2)}) async-start(), calls=%async_computation.9 | async-start | bytes 5980160 | tf_op jit(solution)/shard_map/all_gather | solution.py:523
  453.3 22.6 %collective-permute-start.33 = (bf16[128,1280]{1,0:T(8,128)(2,1)S(1)}, bf16[128,1280]{1,0:T(8,128)(2,1)S(1)}, u32[]{:S(2)}, u32[]{:S(2)}) collective-permute-start(bf16[128,1280]{1,0:T(8,128)(2,1)S(1)} %get-tuple-element.352), channel_id=1, source_target_pairs={{0,1},{4,5},{8,9},{12,13},{16,17},{20,21},{24,25},{28,29}} | collective-permute-start | bytes 983048 | tf_op jit(solution)/shard_map/ppermute | solution.py:428
  458.1 17.9 %collective-permute-start.34 = (bf16[128,1280]{1,0:T(8,128)(2,1)S(1)}, bf16[128,1280]{1,0:T(8,128)(2,1)S(1)}, u32[]{:S(2)}, u32[]{:S(2)}) collective-permute-start(bf16[128,1280]{1,0:T(8,128)(2,1)S(1)} %get-tuple-element.351), channel_id=1, source_target_pairs={{3,2},{7,6},{11,10},{15,14},{19,18},{23,22},{27,26},{31,30}} | collective-permute-start | bytes 983048 | tf_op jit(solution)/shard_map/ppermute | solution.py:429
  459.0 17.0 %collective-permute-start.31 = (bf16[128,1024]{1,0:T(8,128)(2,1)S(1)}, bf16[128,1024]{1,0:T(8,128)(2,1)S(1)}, u32[]{:S(2)}, u32[]{:S(2)}) collective-permute-start(bf16[128,1024]{1,0:T(8,128)(2,1)S(1)} %get-tuple-element.340), channel_id=1, source_target_pairs={{0,8},{4,12},{8,0},{12,4},{16,24},{20,28},{24,16},{28,20},{1,9},{5... | collective-permute-start | bytes 786440 | tf_op jit(solution)/shard_map/ppermute | solution.py:321
  460.4 15.6 %collective-permute-start.32 = (bf16[128,1024]{1,0:T(8,128)(2,1)S(1)}, bf16[128,1024]{1,0:T(8,128)(2,1)S(1)}, u32[]{:S(2)}, u32[]{:S(2)}) collective-permute-start(bf16[128,1024]{1,0:T(8,128)(2,1)S(1)} %get-tuple-element.340), channel_id=1, source_target_pairs={{0,16},{4,20},{8,24},{12,28},{16,0},{20,4},{24,8},{28,12},{1,17},{... | collective-permute-start | bytes 786440 | tf_op jit(solution)/shard_map/ppermute | solution.py:321
  461.8 14.2 %collective-permute-start.28 = (f32[12288]{0:T(1024)S(1)}, f32[12288]{0:T(1024)S(1)}, u32[]{:S(2)}, u32[]{:S(2)}) collective-permute-start(f32[12288]{0:T(1024)S(1)} %bitcast_dynamic-update-slice_fusion), channel_id=1, source_target_pairs={{0,4},{4,0},{8,12},{12,8},{16,20},{20,16},{24,28},{28,24},{1,5},{5... | collective-permute-start | bytes 147464 | tf_op jit(solution)/shard_map/ppermute | solution.py:321
  477.2 13.9 %collective-permute-start.38 = (bf16[128,1280]{1,0:T(8,128)(2,1)S(1)}, bf16[128,1280]{1,0:T(8,128)(2,1)S(1)}, u32[]{:S(2)}, u32[]{:S(2)}) collective-permute-start(bf16[128,1280]{1,0:T(8,128)(2,1)S(1)} %get-tuple-element.350), channel_id=1, source_target_pairs={{0,1},{1,2},{4,5},{5,6},{8,9},{9,10},{12,13},{13,14},{16,17},{17,1... | collective-permute-start | bytes 983048 | tf_op jit(solution)/shard_map/ppermute | solution.py:428
  478.5 12.6 %collective-permute-start.39 = (bf16[128,1280]{1,0:T(8,128)(2,1)S(1)}, bf16[128,1280]{1,0:T(8,128)(2,1)S(1)}, u32[]{:S(2)}, u32[]{:S(2)}) collective-permute-start(bf16[128,1280]{1,0:T(8,128)(2,1)S(1)} %get-tuple-element.349), channel_id=1, source_target_pairs={{3,2},{2,1},{7,6},{6,5},{11,10},{10,9},{15,14},{14,13},{19,18},{18... | collective-permute-start | bytes 983048 | tf_op jit(solution)/shard_map/ppermute | solution.py:429
  479.2 11.8 %collective-permute-start.36 = (bf16[64,1024]{1,0:T(8,128)(2,1)S(1)}, bf16[64,1024]{1,0:T(8,128)(2,1)S(1)}, u32[]{:S(2)}, u32[]{:S(2)}) collective-permute-start(bf16[64,1024]{1,0:T(8,128)(2,1)S(1)} %slice.289), channel_id=1, source_target_pairs={{0,16},{4,20},{8,24},{12,28},{16,0},{20,4},{24,8},{28,12},{1,17},{... | collective-permute-start | bytes 393224 | tf_op jit(solution)/shard_map/ppermute | solution.py:321
  479.9 11.1 %collective-permute-start.37 = (bf16[64,1024]{1,0:T(8,128)(2,1)S(1)}, bf16[64,1024]{1,0:T(8,128)(2,1)S(1)}, u32[]{:S(2)}, u32[]{:S(2)}) collective-permute-start(bf16[64,1024]{1,0:T(8,128)(2,1)S(1)} %slice.290), channel_id=1, source_target_pairs={{0,8},{4,12},{8,0},{12,4},{16,24},{20,28},{24,16},{28,20},{1,9},{5... | collective-permute-start | bytes 393224 | tf_op jit(solution)/shard_map/ppermute | solution.py:321
  481.7 9.3 %collective-permute-start.35 = (f32[12288]{0:T(1024)S(1)}, f32[12288]{0:T(1024)S(1)}, u32[]{:S(2)}, u32[]{:S(2)}) collective-permute-start(f32[12288]{0:T(1024)S(1)} %add.279), channel_id=1, source_target_pairs={{0,8},{4,12},{8,0},{12,4},{16,24},{20,28},{24,16},{28,20},{1,9},{5... | collective-permute-start | bytes 147464 | tf_op jit(solution)/shard_map/ppermute | solution.py:321
  491.1 29.1 %collective-permute-start.41 = (bf16[512,1024]{1,0:T(8,128)(2,1)S(1)}, bf16[512,1024]{1,0:T(8,128)(2,1)S(1)}, u32[]{:S(2)}, u32[]{:S(2)}) collective-permute-start(bf16[512,1024]{1,0:T(8,128)(2,1)S(1)} %constant_dynamic-update-slice_fusion.29.near_ref), channel_id=1, source_target_pairs={{0,4},{4,0},{8,12},{12,8},{16,20},{20,16},{24,28},{28,24},{1,5},{5... | collective-permute-start | bytes 3145736 | tf_op jit(solution)/shard_map/ppermute | solution.py:321
  492.7 15.5 %collective-permute-start.42 = (bf16[128,1280]{1,0:T(8,128)(2,1)S(1)}, bf16[128,1280]{1,0:T(8,128)(2,1)S(1)}, u32[]{:S(2)}, u32[]{:S(2)}) collective-permute-start(bf16[128,1280]{1,0:T(8,128)(2,1)S(1)} %get-tuple-element.348), channel_id=1, source_target_pairs={{0,1},{1,2},{2,3},{4,5},{5,6},{6,7},{8,9},{9,10},{10,11},{12,13},{... | collective-permute-start | bytes 983048 | tf_op jit(solution)/shard_map/ppermute | solution.py:428
  497.5 22.7 %collective-permute-start.43 = (bf16[128,1280]{1,0:T(8,128)(2,1)S(1)}, bf16[128,1280]{1,0:T(8,128)(2,1)S(1)}, u32[]{:S(2)}, u32[]{:S(2)}) collective-permute-start(bf16[128,1280]{1,0:T(8,128)(2,1)S(1)} %get-tuple-element.347), channel_id=1, source_target_pairs={{3,2},{2,1},{1,0},{7,6},{6,5},{5,4},{11,10},{10,9},{9,8},{15,14},{... | collective-permute-start | bytes 983048 | tf_op jit(solution)/shard_map/ppermute | solution.py:429
  523.1 23.1 %collective-permute-start.45 = (bf16[128,1280]{1,0:T(8,128)(2,1)}, bf16[128,1280]{1,0:T(8,128)(2,1)}, u32[]{:S(2)}, u32[]{:S(2)}) collective-permute-start(bf16[128,1280]{1,0:T(8,128)(2,1)} %get-tuple-element.338), channel_id=1, source_target_pairs={{0,8},{4,12},{8,0},{12,4},{16,24},{20,28},{24,16},{28,20},{1,9},{5... | collective-permute-start | bytes 983048 | tf_op jit(solution)/shard_map/ppermute | solution.py:321
  523.9 22.2 %collective-permute-start.46 = (bf16[128,1280]{1,0:T(8,128)(2,1)}, bf16[128,1280]{1,0:T(8,128)(2,1)}, u32[]{:S(2)}, u32[]{:S(2)}) collective-permute-start(bf16[128,1280]{1,0:T(8,128)(2,1)} %get-tuple-element.338), channel_id=1, source_target_pairs={{0,16},{4,20},{8,24},{12,28},{16,0},{20,4},{24,8},{28,12},{1,17},{... | collective-permute-start | bytes 983048 | tf_op jit(solution)/shard_map/ppermute | solution.py:321
  523.9 22.2 %collective-permute-start.44 = (f32[12288]{0:T(1024)S(1)}, f32[12288]{0:T(1024)S(1)}, u32[]{:S(2)}, u32[]{:S(2)}) collective-permute-start(f32[12288]{0:T(1024)S(1)} %add.287), channel_id=1, source_target_pairs={{0,1},{1,0},{2,3},{3,2},{4,5},{5,4},{6,7},{7,6},{8,9},{9,8},{10,11... | collective-permute-start | bytes 147464 | tf_op jit(solution)/shard_map/ppermute | solution.py:321
  531.7 14.4 %collective-permute-start.47 = (bf16[128,768]{1,0:T(8,128)(2,1)S(1)}, bf16[128,768]{1,0:T(8,128)(2,1)S(1)}, u32[]{:S(2)}, u32[]{:S(2)}) collective-permute-start(bf16[128,768]{1,0:T(8,128)(2,1)S(1)} %get-tuple-element.364), channel_id=1, source_target_pairs={{0,1},{4,5},{8,9},{12,13},{16,17},{20,21},{24,25},{28,29}} | collective-permute-start | bytes 589832 | tf_op jit(solution)/shard_map/ppermute | solution.py:428
  533.7 12.5 %collective-permute-start.48 = (bf16[128,768]{1,0:T(8,128)(2,1)S(1)}, bf16[128,768]{1,0:T(8,128)(2,1)S(1)}, u32[]{:S(2)}, u32[]{:S(2)}) collective-permute-start(bf16[128,768]{1,0:T(8,128)(2,1)S(1)} %get-tuple-element.363), channel_id=1, source_target_pairs={{3,2},{7,6},{11,10},{15,14},{19,18},{23,22},{27,26},{31,30}} | collective-permute-start | bytes 589832 | tf_op jit(solution)/shard_map/ppermute | solution.py:429
  547.3 23.9 %collective-permute-start.52 = (bf16[128,768]{1,0:T(8,128)(2,1)S(1)}, bf16[128,768]{1,0:T(8,128)(2,1)S(1)}, u32[]{:S(2)}, u32[]{:S(2)}) collective-permute-start(bf16[128,768]{1,0:T(8,128)(2,1)S(1)} %get-tuple-element.362), channel_id=1, source_target_pairs={{0,1},{1,2},{4,5},{5,6},{8,9},{9,10},{12,13},{13,14},{16,17},{17,1... | collective-permute-start | bytes 589832 | tf_op jit(solution)/shard_map/ppermute | solution.py:428
  548.6 22.6 %collective-permute-start.53 = (bf16[128,768]{1,0:T(8,128)(2,1)S(1)}, bf16[128,768]{1,0:T(8,128)(2,1)S(1)}, u32[]{:S(2)}, u32[]{:S(2)}) collective-permute-start(bf16[128,768]{1,0:T(8,128)(2,1)S(1)} %get-tuple-element.361), channel_id=1, source_target_pairs={{3,2},{2,1},{7,6},{6,5},{11,10},{10,9},{15,14},{14,13},{19,18},{18... | collective-permute-start | bytes 589832 | tf_op jit(solution)/shard_map/ppermute | solution.py:429
  549.3 21.9 %collective-permute-start.49 = (f32[12288]{0:T(1024)S(1)}, f32[12288]{0:T(1024)S(1)}, u32[]{:S(2)}, u32[]{:S(2)}) collective-permute-start(f32[12288]{0:T(1024)S(1)} %add.292), channel_id=1, source_target_pairs={{0,2},{1,3},{2,0},{3,1},{4,6},{5,7},{6,4},{7,5},{8,10},{9,11},{10,... | collective-permute-start | bytes 147464 | tf_op jit(solution)/shard_map/ppermute | solution.py:321
  552.7 18.5 %collective-permute-start.50 = (bf16[64,1280]{1,0:T(8,128)(2,1)S(1)}, bf16[64,1280]{1,0:T(8,128)(2,1)S(1)}, u32[]{:S(2)}, u32[]{:S(2)}) collective-permute-start(bf16[64,1280]{1,0:T(8,128)(2,1)S(1)} %slice.296), channel_id=1, source_target_pairs={{0,16},{4,20},{8,24},{12,28},{16,0},{20,4},{24,8},{28,12},{1,17},{... | collective-permute-start | bytes 491528 | tf_op jit(solution)/shard_map/ppermute | solution.py:321
  555.9 15.2 %collective-permute-start.51 = (bf16[64,1280]{1,0:T(8,128)(2,1)S(1)}, bf16[64,1280]{1,0:T(8,128)(2,1)S(1)}, u32[]{:S(2)}, u32[]{:S(2)}) collective-permute-start(bf16[64,1280]{1,0:T(8,128)(2,1)S(1)} %slice.297), channel_id=1, source_target_pairs={{0,8},{4,12},{8,0},{12,4},{16,24},{20,28},{24,16},{28,20},{1,9},{5... | collective-permute-start | bytes 491528 | tf_op jit(solution)/shard_map/ppermute | solution.py:321
  571.9 19.3 %collective-permute-start.54 = (bf16[512,1280]{1,0:T(8,128)(2,1)S(1)}, bf16[512,1280]{1,0:T(8,128)(2,1)S(1)}, u32[]{:S(2)}, u32[]{:S(2)}) collective-permute-start(bf16[512,1280]{1,0:T(8,128)(2,1)S(1)} %constant_dynamic-update-slice_fusion.34.near_ref), channel_id=1, source_target_pairs={{0,4},{4,0},{8,12},{12,8},{16,20},{20,16},{24,28},{28,24},{1,5},{5... | collective-permute-start | bytes 3932168 | tf_op jit(solution)/shard_map/ppermute | solution.py:321
  573.2 10.7 %collective-permute-start.55 = (bf16[128,768]{1,0:T(8,128)(2,1)S(1)}, bf16[128,768]{1,0:T(8,128)(2,1)S(1)}, u32[]{:S(2)}, u32[]{:S(2)}) collective-permute-start(bf16[128,768]{1,0:T(8,128)(2,1)S(1)} %get-tuple-element.360), channel_id=1, source_target_pairs={{0,1},{1,2},{2,3},{4,5},{5,6},{6,7},{8,9},{9,10},{10,11},{12,13},{... | collective-permute-start | bytes 589832 | tf_op jit(solution)/shard_map/ppermute | solution.py:428
  574.5 16.7 %collective-permute-start.56 = (bf16[128,768]{1,0:T(8,128)(2,1)S(1)}, bf16[128,768]{1,0:T(8,128)(2,1)S(1)}, u32[]{:S(2)}, u32[]{:S(2)}) collective-permute-start(bf16[128,768]{1,0:T(8,128)(2,1)S(1)} %get-tuple-element.359), channel_id=1, source_target_pairs={{3,2},{2,1},{1,0},{7,6},{6,5},{5,4},{11,10},{10,9},{9,8},{15,14},{... | collective-permute-start | bytes 589832 | tf_op jit(solution)/shard_map/ppermute | solution.py:429
  592.8 14.9 %collective-permute-start.57 = (bf16[128,768]{1,0:T(8,128)(2,1)S(1)}, bf16[128,768]{1,0:T(8,128)(2,1)S(1)}, u32[]{:S(2)}, u32[]{:S(2)}) collective-permute-start(bf16[128,768]{1,0:T(8,128)(2,1)S(1)} %get-tuple-element.327), channel_id=1, source_target_pairs={{0,8},{4,12},{8,0},{12,4},{16,24},{20,28},{24,16},{28,20},{1,9},{5... | collective-permute-start | bytes 589832 | tf_op jit(solution)/shard_map/ppermute | solution.py:321
  594.1 13.7 %collective-permute-start.58 = (bf16[128,768]{1,0:T(8,128)(2,1)S(1)}, bf16[128,768]{1,0:T(8,128)(2,1)S(1)}, u32[]{:S(2)}, u32[]{:S(2)}) collective-permute-start(bf16[128,768]{1,0:T(8,128)(2,1)S(1)} %get-tuple-element.327), channel_id=1, source_target_pairs={{0,16},{4,20},{8,24},{12,28},{16,0},{20,4},{24,8},{28,12},{1,17},{... | collective-permute-start | bytes 589832 | tf_op jit(solution)/shard_map/ppermute | solution.py:321
  (108 other events, 907.6 us)
Sparse Core Ops, SparseCore 0:
  195.9 89.5 all-gather.4
  287.7 88.9 all-gather.6
  378.8 99.1 all-gather.8
  491.3 105.5 all-gather.10
Sparse Core Ops, SparseCore 1:
  258.6 70.4 reduce-scatter.3
  332.7 81.3 reduce-scatter.5
  451.4 66.9 reduce-scatter.7

commit v3 on v2

--- a/solution.py
+++ b/solution.py
@@ -62,8 +62,8 @@
             outs.append(dot(e.astype(BF),v,NN)/l)
         out_ref[0,:,at:at+PAIR]=jnp.where(low,outs[0],outs[1]).astype(BF)
 
-def params(name,flops,nbytes,trans=0,work=1000000):
-    return dict(name=name,compiler_params=pltpu.CompilerParams(vmem_limit_bytes=VLIM),
+def params(name,flops,nbytes,trans=0,work=1000000,limit=VLIM):
+    return dict(name=name,compiler_params=pltpu.CompilerParams(vmem_limit_bytes=limit),
         cost_estimate=pl.CostEstimate(flops=int(work),bytes_accessed=1000000,transcendentals=0))
 
 def row(width): return pl.BlockSpec((1,width),lambda *_:(0,0))
@@ -123,7 +123,7 @@
         out_shape=[jax.ShapeDtypeStruct((n,seq,d),F32),jax.ShapeDtypeStruct((n,seq,d),BF),jax.ShapeDtypeStruct((n,seq,ff),BF),
             jax.ShapeDtypeStruct((n,seq,ff),BF),jax.ShapeDtypeStruct((n,seq,d),BF)],
         scratch_shapes=[pltpu.VMEM((seq,d),F32)],
-        **params("mlp_fwd",2*n*seq*d*(d+2*ff),n*seq*(5*d+2*ff)*2+ff*d*4,2*n*seq*ff,work))(x,att,pw,pb,gain,shift,w1,b1.reshape(ff//tile,1,tile),w2,b2)
+        **params("mlp_fwd",2*n*seq*d*(d+2*ff),n*seq*(5*d+2*ff)*2+ff*d*4,2*n*seq*ff,work,52*2**20))(x,att,pw,pb,gain,shift,w1,b1.reshape(ff//tile,1,tile),w2,b2)
 
 def mlp_bwd_kernel(cot_ref,slope_ref,w2_ref,w1_ref,resid_ref,gain_ref,pw_ref,
                    dpre_ref,db1_ref,dres_ref,dresb_ref,datt_ref,sums_ref,acc_ref):
@@ -412,7 +412,7 @@
 
 
 def sum_chain(value):
-    for axis in ("dp", "tensor"):
+    for axis in ("tensor", "dp"):
         mask = 1
         while mask < lax.axis_size(axis):
             value = value + (yield swap(value, axis, mask))
@@ -497,7 +497,10 @@
     def dp_rows(w):
         return lax.dynamic_slice_in_dim(w, dp_at * (w.shape[0] // n_dp), w.shape[0] // n_dp, 0).astype(BF)
 
-    p0, p1, p2 = dp_rows(mix), dp_rows(fc1_weight), dp_rows(fc2_weight)
+    rows = dp_rows(qkv_weight)
+    proj_rows = lax.dynamic_slice(proj_weight, (dp_at * p % lw, dp_at * p // lw * lw), (p, lw)).astype(BF)
+    p0 = jnp.concatenate([rows[:, 0], rows[:, 1], rows[:, 2], proj_rows], axis=1)
+    p1, p2 = dp_rows(fc1_weight), dp_rows(fc2_weight)
     z0 = shards(jnp.concatenate([p0, flat], axis=0))
     x = lax.dynamic_slice_in_dim(tokens, t_at * own, own, 0)
     cot = lax.dynamic_slice_in_dim(cotangent, t_at * own, own, 0)
@@ -557,6 +560,8 @@
     def attention_back(i):
         def run(made, results):
             d = after(d_att[i], *(made[-1] if made else ()))
+            if i == own - 1:
+                d, out_all[i] = tie(d, out_all[i])
             dq, gq, gt_own, s1 = attn_bwd(i, qkv[i], d, w_mix, x, d_resid[i], gain1)
             gt_all[i] = gather(gt_own)
             return dq, gq, s1
@@ -564,9 +569,7 @@
         return run
 
     def attention_grad(made, results):
-        d_qkv = [m[0] for m in made]
-        d_qkv[-1], out_all[-1] = tie(d_qkv[-1], out_all[-1])
-        return grad_qkv(act1, d_qkv, n_dp, n_t)
+        return grad_qkv(act1, [m[0] for m in made], n_dp, n_t)
 
     rates = (
         1.2 / math.sqrt(D),
@@ -607,26 +610,26 @@
     made = []
     chains = [
         (own + 1, lambda: sum_chain(vectors())),
-        (0, lambda: reduce_chain(part_fc2, "spread_fc2")),
+        (own, lambda: reduce_chain(part_fc2, "spread_fc2")),
         (own + 1, lambda: reduce_chain(part_fc1, "spread_fc1")),
-        (own + 4, lambda: reduce_chain(reduce_dp(made[own]), "spread_qkv")),
+        (own + 3, lambda: reduce_chain(reduce_dp(made[own]), "spread_qkv")),
     ]
     work = [attention_back(i) for i in range(own)] + [
         attention_grad,
         lambda made, results: weave(out_all),
         waits_for(0),
         nothing,
-        nothing if n_t > 4 else fc2_step,
         nothing,
         nothing,
+        nothing if n_t > 4 else fc2_step,
         nothing if n_t > 4 else fc1_step,
         waits_for(-1),
     ]
     flat, g_fc2, g_fc1, g_qkv = run_chains(chains, work, made)
-    output, gt_all[0], gt_all[-1] = made[own + 1], made[own + 2], made[-1]
+    output, grad_tokens = made[own + 1], weave(gt_all[:-1] + [made[-1]])
     if n_t > 4:
-        made[own + 4], made[own + 7] = fc2_step(made, (None, g_fc2)), fc1_step(made, (None, None, g_fc1))
-    (g_fc2, new_fc2), (g_fc1, g_proj, new_fc1, new_proj) = made[own + 4], made[own + 7]
+        made[own + 6], made[own + 7] = fc2_step(made, (None, g_fc2)), fc1_step(made, (None, None, g_fc1))
+    (g_fc2, new_fc2), (g_fc1, g_proj, new_fc1, new_proj) = made[own + 6], made[own + 7]
     rel = 2 * lw + fw
     g_qkv = jnp.stack([g_qkv[:, i * lw : (i + 1) * lw] for i in range(3)], axis=1)
     mine = lax.dynamic_index_in_dim(flat[: n_t * rel].reshape(n_t, rel), t_at, 0, keepdims=False)
@@ -636,8 +639,6 @@
     grads = (g_qkv, mine[: 2 * lw].reshape(2, lw), g_proj, g_fc1, mine[2 * lw :], g_fc2, g_gains, g_shifts)
     updated = [step(at, grad) for at, grad in enumerate(grads)]
     updated[3], updated[5], updated[2] = new_fc1, new_fc2, new_proj
-    gt_all[-1], *_ = tie(gt_all[-1], *(u[0] for u in updated))
-    grad_tokens = weave(gt_all)
     return (
         output,
         grad_tokens,

time: 652 us -> 644 us (0.988)
  waiting for transfers between devices: 109 us -> 86.2 us
  starting transfers between devices: 98.8 us -> 115 us
  local copies, waits for them, and re-layouts: 125 us -> 114 us
    ppermute x9, waiting for transfers between devices: 19.6 us -> 1.93 us  [reduce_chain(): lax.ppermute(down, 'tensor', [(n_t - 1 - i, n_t - 2 - i) for i in range(s...]
    unnamed x242 -> x256, local copies, waits for them, and re-layouts: 97.9 us -> 80.8 us
    ppermute x9, starting transfers between devices: 28 us -> 44.3 us  [reduce_chain(): lax.ppermute(up, 'tensor', [(i, i + 1) for i in range(step)])]
    ppermute x9, waiting for transfers between devices: 17.8 us -> 5.22 us  [reduce_chain(): lax.ppermute(up, 'tensor', [(i, i + 1) for i in range(step)])]
    ppermute x35, waiting for transfers between devices: 38.2 us -> 45.6 us  [swap(): return lax.ppermute(value, axis, [(i, i ^ mask) for i in range(n)])]
  transfers between devices with their start and end apart: 69 -> 69, of which waited for: 21 -> 20; matrix products, arithmetic and copies ran while one was open for 11% -> 12% of each run, Pallas kernels for 35% -> 35%
where the time goes in v3:
time: 644 us; the launch traced here: 636 us
  Pallas kernels  257 us (40%)
  starting transfers between devices  115 us (18%)
  local copies, waits for them, and re-layouts  114 us (18%)
  waiting for transfers between devices  86.2 us (13%)
  other arithmetic  46 us (7%)
  between operations  17.5 us (3%)
    unnamed x256, local copies, waits for them, and re-layouts  80.8 us
    pallas_call x2, Pallas kernels, attn_bwd(): pl.pallas_call(attn_bwd_kernel, grid=(n, g), in_specs=[pl.BlockSpec((1, s...  66.6 us
    pallas_call x3, Pallas kernels, shard_grads(): pl.pallas_call(kernel, grid=(g,), in_specs=specs, out_specs=pl.BlockSpec(...  47.2 us
    ppermute x35, waiting for transfers between devices, swap(): return lax.ppermute(value, axis, [(i, i ^ mask) for i in range(n)])  45.6 us
    ppermute x9, starting transfers between devices, reduce_chain(): lax.ppermute(up, 'tensor', [(i, i + 1) for i in range(step)])  44.3 us
    pallas_call x2, Pallas kernels, mlp_bwd(): pl.pallas_call(mlp_bwd_kernel, grid=(n, ff // tile), in_specs=[own, hidde...  40.9 us
    pallas_call x2, Pallas kernels, mlp_fwd(): pl.pallas_call(mlp_fwd_kernel, grid=(n, ff // tile), in_specs=[own, img,...  40.6 us
    ppermute x35, starting transfers between devices, swap(): return lax.ppermute(value, axis, [(i, i ^ mask) for i in range(n)])  35 us
  transfers between devices with their start and end apart: 69, of which 20 were waited for; matrix products, arithmetic and copies ran while one was open for 12% of the time, Pallas kernels for 35%

profile of v3, /device:TPU:0, one launch (start us, length us, event | category | flops | bytes accessed | tf_op | source)
XLA Modules:
  0.0 636.3 jit_solution(7193423978285355428)
XLA Ops:
  12.3 3.0 collective-permute-start
  15.3 2.6 collective-permute-start.1
  19.3 9.4 %constant_dynamic-slice_fusion = (bf16[2,577,1024]{2,0,1:T(2,128)(2,1)S(1)}, bf16[2,577,1024]{2,0,1:T(2,128)(2,1)S(1)}) fusion(bf16[8,577,1024]{2,0,1:T(8,128)(2,1)} %param.27, s32[]{:T(128)S(6)} %select_n.78, bf16[8,577,1024]{2,0,1:T(8,128)(2,1)} %param.26), kind=kLoop, calls=%fused_computation.176 | loop fusion | bytes 9453572 | tf_op jit(solution)/shard_map/dynamic_slice | solution.py:506
  29.4 2.1 copy.88.refs_2_.refs_3_.cot_ref
  43.6 6.0 collective-permute-start.5
  51.9 6.0 collective-permute-done.5
  58.0 8.9 %collective-permute-done.6 = bf16[128,1024]{1,0:T(8,128)(2,1)S(1)} collective-permute-done((bf16[128,1024]{1,0:T(8,128)(2,1)S(1)}, bf16[128,1024]{1,0:T(8,128)(2,1)S(1)}, u32[]{:S(2)}, u32[]{:S(2)}) %collective-permute-start.6) | collective-permute-done | bytes 262176 | tf_op jit(solution)/shard_map/ppermute | solution.py:316
  70.2 6.1 collective-permute-start.12
  76.3 2.3 collective-permute-start.13
  80.3 5.2 collective-permute-done.12
  87.3 6.7 %collective-permute-done.13 = bf16[128,1024]{1,0:T(8,128)(2,1)S(1)} collective-permute-done((bf16[128,1024]{1,0:T(8,128)(2,1)S(1)}, bf16[128,1024]{1,0:T(8,128)(2,1)S(1)}, u32[]{:S(2)}, u32[]{:S(2)}) %collective-permute-start.13) | collective-permute-done | bytes 262176 | tf_op jit(solution)/shard_map/ppermute | solution.py:316
  97.7 4.6 collective-permute-done.14
  121.1 3.8 place_mix.1.w_ref.pw_ref
  124.9 17.1 %qkv_attn.2 = (bf16[1,577,1024]{2,1,0:T(8,128)(2,1)S(1)}, bf16[1,577,3072]{2,1,0:T(8,128)(2,1)S(1)}, bf16[1,577,1024]{2,1,0:T(8,128)(2,1)S(1)}) custom-call(bf16[2,577,1024]{2,1,0:T(8,128)(2,1)S(1)} %copy.87.x_ref, f32[1,1024]{1,0:T(1,128)S(1)} %get-tuple-element.405.gain_ref, f32[1,1024]{1,0:T(1,128)S(1)} %get-tuple-element.393.shift_ref, ...), custom_call_target="tpu_custom_call" | custom-call | flops 1000000 | bytes 1000000 | tf_op jit(solution)/shard_map/qkv_attn/pallas_call | solution.py:76
  147.9 3.5 collective-permute-done.20.far_ref
  151.4 2.7 place_fc1.1.w1_ref
  154.2 3.4 copy-done.2
  158.7 5.6 collective-permute-done.23.far_ref
  165.1 3.3 copy-done.3
  168.4 20.2 %mlp_fwd.2 = (f32[1,577,1024]{2,1,0:T(8,128)}, bf16[1,577,1024]{2,1,0:T(8,128)(2,1)S(1)}, bf16[1,577,4096]{2,1,0:T(8,128)(2,1)}, bf16[1,577,4096]{2,1,0:T(8,128)(2,1)}, bf16[1,577,1024]{2,1,0:T(8,128)(2,1)}) custom-call(bf16[2,577,1024]{2,1,0:T(8,128)(2,1)} %copy-done.4, bf16[1,577,1024]{2,1,0:T(8,128)(2,1)} %copy-done.15, bf16[4,1024,1024]{2,1,0:T(8,128)(2,1)} %copy-done, ...), custom_call_target="tpu_custom_call" | custom-call | flops 1000000 | bytes 1000000 | tf_op jit(solution)/shard_map/mlp_fwd/pallas_call | solution.py:118
  189.8 3.4 copy-done.1
  193.2 17.3 %qkv_attn.3 = (bf16[1,577,1024]{2,1,0:T(8,128)(2,1)S(1)}, bf16[1,577,3072]{2,1,0:T(8,128)(2,1)S(1)}, bf16[1,577,1024]{2,1,0:T(8,128)(2,1)S(1)}) custom-call(bf16[2,577,1024]{2,1,0:T(8,128)(2,1)S(1)} %copy-done.5, f32[1,1024]{1,0:T(1,128)S(1)} %get-tuple-element.405.gain_ref, f32[1,1024]{1,0:T(1,128)S(1)} %get-tuple-element.393.shift_ref, ...), custom_call_target="tpu_custom_call" | custom-call | flops 1000000 | bytes 1000000 | tf_op jit(solution)/shard_map/qkv_attn/pallas_call | solution.py:76
  214.4 20.3 %mlp_fwd.3 = (f32[1,577,1024]{2,1,0:T(8,128)}, bf16[1,577,1024]{2,1,0:T(8,128)(2,1)S(1)}, bf16[1,577,4096]{2,1,0:T(8,128)(2,1)}, bf16[1,577,4096]{2,1,0:T(8,128)(2,1)}, bf16[1,577,1024]{2,1,0:T(8,128)(2,1)}) custom-call(bf16[2,577,1024]{2,1,0:T(8,128)(2,1)} %copy-done.4, bf16[1,577,1024]{2,1,0:T(8,128)(2,1)} %copy-done.17, bf16[4,1024,1024]{2,1,0:T(8,128)(2,1)} %copy-done, ...), custom_call_target="tpu_custom_call" | custom-call | flops 1000000 | bytes 1000000 | tf_op jit(solution)/shard_map/mlp_fwd/pallas_call | solution.py:118
  235.7 2.4 copy-done.14
  238.1 15.8 %grad_fc2.1 = bf16[8,4,128,1024]{3,2,1,0:T(8,128)(2,1)} custom-call(bf16[1,577,4096]{2,1,0:T(8,128)(2,1)S(1)} %bitcast.137, bf16[1,577,4096]{2,1,0:T(8,128)(2,1)S(1)} %copy-done.14, bf16[2,577,1024]{2,1,0:T(8,128)(2,1)S(1)} %copy-done.7, bf16[2,577,1024]{2,1,0:T(8,128)(2,1)S(1)} %copy-done.7), custom_call_target="tpu_custom_call" | custom-call | flops 1000000 | bytes 1000000 | tf_op jit(solution)/shard_map/grad_fc2/pallas_call | solution.py:264
  256.5 21.5 %mlp_bwd.2 = (bf16[1,577,4096]{2,1,0:T(8,128)(2,1)S(1)}, f32[1,4,1,1024]{3,2,1,0:T(1,128)S(1)}, f32[1,577,1024]{2,1,0:T(8,128)S(1)}, bf16[1,577,1024]{2,1,0:T(8,...) custom-call(bf16[2,577,1024]{2,1,0:T(8,128)(2,1)S(1)} %copy-done.7, ...), custom_call_target="tpu_custom_call" | custom-call | flops 1000000 | bytes 1000000 | tf_op jit(solution)/shard_map/mlp_bwd/pallas_call | solution.py:172
  280.4 19.4 %mlp_bwd.3 = (bf16[1,577,4096]{2,1,0:T(8,128)(2,1)S(1)}, f32[1,4,1,1024]{3,2,1,0:T(1,128)S(1)}, f32[1,577,1024]{2,1,0:T(8,128)S(1)}, bf16[1,577,1024]{2,1,0:T(8,...) custom-call(bf16[2,577,1024]{2,1,0:T(8,128)(2,1)S(1)} %copy-done.7, ...), custom_call_target="tpu_custom_call" | custom-call | flops 1000000 | bytes 1000000 | tf_op jit(solution)/shard_map/mlp_bwd/pallas_call | solution.py:172
  302.3 19.8 %grad_fc1.1 = bf16[8,4,128,1280]{3,2,1,0:T(8,128)(2,1)} custom-call(bf16[1,577,1024]{2,1,0:T(8,128)(2,1)S(1)} %copy-done.41, bf16[1,577,1024]{2,1,0:T(8,128)(2,1)S(1)} %copy-done.43, bf16[1,577,4096]{2,1,0:T(8,128)(2,1)S(1)} %get-tuple-element.210.refs_2_, bf16[1,577,4096]{2,1,0:T(8,128)(2,1)S(1)} %get-tuple-element.214.refs_3_, ...), custom_call_target="tpu_custom_call" | custom-call | flops 1000000 | bytes 1000000 | tf_op jit(solution)/shard_map/grad_fc1/pallas_call | solution.py:264
  323.9 2.0 copy-done.20
  328.9 32.7 %attn_bwd.2 = (bf16[1,577,3072]{2,1,0:T(8,128)(2,1)S(1)}, f32[1,4,2,256]{3,2,1,0:T(2,128)S(1)}, bf16[1,577,1024]{2,1,0:T(8,128)(2,1)S(1)}, f32[1,2,1024]{2,1,0:T(2,128)S(1)}) custom-call(bf16[1,577,3072]{2,1,0:T(8,128)(2,1)S(1)} %copy-done.20, bf16[1,577,1024]{2,1,0:T(8,128)(2,1)S(1)} %copy-done.34, bf16[4,1024,1024]{2,1,0:T(8,128)(2,1)} %copy-done, ...), custom_call_target="tpu_custom_call" | custom-call | flops 1000000 | bytes 1000000 | tf_op jit(solution)/shard_map/attn_bwd/pallas_call | solution.py:232
  365.7 3.6 collective-permute-start.25
  370.7 2.4 copy-done.22
  376.1 33.9 %attn_bwd.3 = (bf16[1,577,3072]{2,1,0:T(8,128)(2,1)S(1)}, f32[1,4,2,256]{3,2,1,0:T(2,128)S(1)}, bf16[1,577,1024]{2,1,0:T(8,128)(2,1)}, f32[1,2,1024]{2,1,0:T(2,128)S(1)}) custom-call(bf16[1,577,3072]{2,1,0:T(8,128)(2,1)S(1)} %copy-done.22, bf16[1,577,1024]{2,1,0:T(8,128)(2,1)S(1)} %copy-done.32, bf16[4,1024,1024]{2,1,0:T(8,128)(2,1)} %copy-done, ...), custom_call_target="tpu_custom_call" | custom-call | flops 1000000 | bytes 1000000 | tf_op jit(solution)/shard_map/attn_bwd/pallas_call | solution.py:232
  410.0 11.5 %grad_qkv.1 = bf16[8,4,128,768]{3,2,1,0:T(8,128)(2,1)S(1)} custom-call(bf16[1,577,1024]{2,1,0:T(8,128)(2,1)S(1)} %copy-done.37, bf16[1,577,1024]{2,1,0:T(8,128)(2,1)S(1)} %copy-done.39, bf16[1,577,3072]{2,1,0:T(8,128)(2,1)S(1)} %copy-done.24, bf16[1,577,3072]{2,1,0:T(8,128)(2,1)S(1)} %get-tuple-element.247.refs_3_), custom_call_target="tpu_custom_call" | custom-call | flops 1000000 | bytes 1000000 | tf_op jit(solution)/shard_map/grad_qkv/pallas_call | solution.py:264
  421.5 2.7 copy-done.8
  433.0 3.0 copy-done.12
  436.0 2.8 copy-done.13
  438.7 8.1 %weave.2 = bf16[577,8,1024]{2,1,0:T(8,128)(2,1)} custom-call(bf16[4,577,1024]{2,1,0:T(8,128)(2,1)S(1)} %copy-done.12, bf16[4,577,1024]{2,1,0:T(8,128)(2,1)S(1)} %copy-done.13), custom_call_target="tpu_custom_call" | custom-call | flops 1000000 | bytes 1000000 | tf_op jit(solution)/shard_map/weave/pallas_call | solution.py:297
  446.9 8.9 %collective-permute-done.24 = f32[12288]{0:T(1024)S(1)} collective-permute-done((f32[12288]{0:T(1024)S(1)}, f32[12288]{0:T(1024)S(1)}, u32[]{:S(2)}, u32[]{:S(2)}) %collective-permute-start.24) | collective-permute-done | bytes 49184 | tf_op jit(solution)/shard_map/ppermute | solution.py:321
  455.9 4.4 collective-permute-start.34
  461.9 3.5 collective-permute-start.32
  466.8 4.8 collective-permute-start.31
  471.6 12.4 %collective-permute-done.31 = f32[12288]{0:T(1024)S(1)} collective-permute-done((f32[12288]{0:T(1024)S(1)}, f32[12288]{0:T(1024)S(1)}, u32[]{:S(2)}, u32[]{:S(2)}) %collective-permute-start.31) | collective-permute-done | bytes 49184 | tf_op jit(solution)/shard_map/ppermute | solution.py:321
  490.5 2.1 add_convert_fusion
  492.6 6.3 collective-permute-start.39
  502.9 4.5 collective-permute-start.41
  508.9 3.2 collective-permute-done.41
  520.1 4.4 collective-permute-start.48
  527.8 3.4 collective-permute-done.45
  531.2 2.0 collective-permute-done.48
  535.5 14.7 %collective-permute-start.54 = (bf16[128,768]{1,0:T(8,128)(2,1)S(1)}, bf16[128,768]{1,0:T(8,128)(2,1)S(1)}, u32[]{:S(2)}, u32[]{:S(2)}) collective-permute-start(bf16[128,768]{1,0:T(8,128)(2,1)S(1)} %get-tuple-element.358), channel_id=1, source_target_pairs={{0,1},{1,2},{2,3},{4,5},{5,6},{6,7},{8,9},{9,10},{10,11},{12,13},{... | collective-permute-start | bytes 589832 | tf_op jit(solution)/shard_map/ppermute | solution.py:428
  552.5 2.0 collective-permute-start.50
  556.5 3.4 collective-permute-done.50
  560.9 4.6 collective-permute-done.53
  575.0 2.6 convert_element_type.291
  579.9 7.6 %multiply_subtract_fusion.1 = (f32[1024,1024]{1,0:T(8,128)}, f32[1024,1024]{1,0:T(8,128)}, f32[1024,1024]{1,0:T(8,128)}) fusion(f32[1024,1024]{1,0:T(8,128)S(1)} %copy-done.49, bf16[1024,1024]{1,0:T(8,128)(2,1)S(1)} %spread_fc2.1, f32[1024,1024]{1,0:T(8,128)S(1)} %copy-done.57, f32[1024,1024]{1,0:T(8,128)} %param.49), kind=kLoop, calls=%fused_computation.8 | loop fusion | flops 16777216 | bytes 27262976 | tf_op jit(solution)/shard_map/sub | solution.py:308
  589.0 2.7 slice.359
  591.8 2.1 collective-permute-start.59
  593.9 2.1 collective-permute-start.60
  596.0 2.2 multiply_subtract_fusion.3
  599.5 5.8 multiply_subtract_fusion
  608.9 2.1 spread_qkv.1
  614.7 5.8 multiply_subtract_fusion.2
  620.6 8.2 %weave.3 = bf16[577,8,1024]{2,1,0:T(8,128)(2,1)} custom-call(bf16[4,577,1024]{2,1,0:T(8,128)(2,1)S(1)} %bitcast.133, bf16[4,577,1024]{2,1,0:T(8,128)(2,1)S(1)} %bitcast.135), custom_call_target="tpu_custom_call" | custom-call | flops 1000000 | bytes 1000000 | tf_op jit(solution)/shard_map/weave/pallas_call | solution.py:297
  (468 shorter events, 147.7 us)
Async XLA Ops:
  8.0 314.2 %all-gather.5.cloned.1.call-start = ((), (), s32[]{:S(2)}) async-start(), calls=%async_computation.3 | async-start | bytes 5980160 | tf_op jit(solution)/shard_map/all_gather | solution.py:526
  12.3 25.7 %collective-permute-start = (bf16[144,1024]{1,0:T(8,128)(2,1)}, bf16[144,1024]{1,0:T(8,128)(2,1)S(1)}, u32[]{:S(2)}, u32[]{:S(2)}) collective-permute-start(bf16[144,1024]{1,0:T(8,128)(2,1)} %pad_maximum_fusion.3), channel_id=1, source_target_pairs={{0,1},{1,2},{2,3},{3,0},{4,5},{5,6},{6,7},{7,4},{8,9},{9,10},{10,1... | collective-permute-start | bytes 884744 | tf_op jit(solution)/shard_map/ppermute | solution.py:316
  15.3 22.7 %collective-permute-start.1 = (bf16[144,1024]{1,0:T(8,128)(2,1)}, bf16[144,1024]{1,0:T(8,128)(2,1)S(1)}, u32[]{:S(2)}, u32[]{:S(2)}) collective-permute-start(bf16[144,1024]{1,0:T(8,128)(2,1)} %pad_maximum_fusion.3), channel_id=1, source_target_pairs={{0,2},{1,3},{2,0},{3,1},{4,6},{5,7},{6,4},{7,5},{8,10},{9,11},{10,... | collective-permute-start | bytes 884744 | tf_op jit(solution)/shard_map/ppermute | solution.py:316
  17.9 20.1 %collective-permute-start.2 = (bf16[144,1024]{1,0:T(8,128)(2,1)}, bf16[144,1024]{1,0:T(8,128)(2,1)S(1)}, u32[]{:S(2)}, u32[]{:S(2)}) collective-permute-start(bf16[144,1024]{1,0:T(8,128)(2,1)} %pad_maximum_fusion.3), channel_id=1, source_target_pairs={{0,3},{1,0},{2,1},{3,2},{4,7},{5,4},{6,5},{7,6},{8,11},{9,8},{10,9... | collective-permute-start | bytes 884744 | tf_op jit(solution)/shard_map/ppermute | solution.py:316
  40.5 26.4 %collective-permute-start.3 = (bf16[384,1024]{1,0:T(8,128)(2,1)S(1)}, bf16[384,1024]{1,0:T(8,128)(2,1)S(1)}, u32[]{:S(2)}, u32[]{:S(2)}) collective-permute-start(bf16[384,1024]{1,0:T(8,128)(2,1)S(1)} %pad_maximum_fusion.2), channel_id=1, source_target_pairs={{0,8},{4,12},{8,0},{12,4},{16,24},{20,28},{24,16},{28,20},{1,9},{5... | collective-permute-start | bytes 2359304 | tf_op jit(solution)/shard_map/ppermute | solution.py:321
  42.0 24.8 %collective-permute-start.4 = (bf16[384,1024]{1,0:T(8,128)(2,1)S(1)}, bf16[384,1024]{1,0:T(8,128)(2,1)S(1)}, u32[]{:S(2)}, u32[]{:S(2)}) collective-permute-start(bf16[384,1024]{1,0:T(8,128)(2,1)S(1)} %pad_maximum_fusion.2), channel_id=1, source_target_pairs={{0,16},{4,20},{8,24},{12,28},{16,0},{20,4},{24,8},{28,12},{1,17},{... | collective-permute-start | bytes 2359304 | tf_op jit(solution)/shard_map/ppermute | solution.py:321
  43.6 14.4 %collective-permute-start.5 = (bf16[128,1024]{1,0:T(8,128)(2,1)S(1)}, bf16[128,1024]{1,0:T(8,128)(2,1)S(1)}, u32[]{:S(2)}, u32[]{:S(2)}) collective-permute-start(bf16[128,1024]{1,0:T(8,128)(2,1)S(1)} %get-tuple-element.174), channel_id=1, source_target_pairs={{0,1},{1,2},{2,3},{3,0},{4,5},{5,6},{6,7},{7,4},{8,9},{9,10},{10,1... | collective-permute-start | bytes 786440 | tf_op jit(solution)/shard_map/ppermute | solution.py:316
  49.6 17.3 %collective-permute-start.6 = (bf16[128,1024]{1,0:T(8,128)(2,1)S(1)}, bf16[128,1024]{1,0:T(8,128)(2,1)S(1)}, u32[]{:S(2)}, u32[]{:S(2)}) collective-permute-start(bf16[128,1024]{1,0:T(8,128)(2,1)S(1)} %get-tuple-element.174), channel_id=1, source_target_pairs={{0,2},{1,3},{2,0},{3,1},{4,6},{5,7},{6,4},{7,5},{8,10},{9,11},{10,... | collective-permute-start | bytes 786440 | tf_op jit(solution)/shard_map/ppermute | solution.py:316
  51.2 15.7 %collective-permute-start.7 = (bf16[128,1024]{1,0:T(8,128)(2,1)S(1)}, bf16[128,1024]{1,0:T(8,128)(2,1)S(1)}, u32[]{:S(2)}, u32[]{:S(2)}) collective-permute-start(bf16[128,1024]{1,0:T(8,128)(2,1)S(1)} %get-tuple-element.174), channel_id=1, source_target_pairs={{0,3},{1,0},{2,1},{3,2},{4,7},{5,4},{6,5},{7,6},{8,11},{9,8},{10,9... | collective-permute-start | bytes 786440 | tf_op jit(solution)/shard_map/ppermute | solution.py:316
  69.1 33.1 %collective-permute-start.10 = (bf16[384,1024]{1,0:T(8,128)(2,1)S(1)}, bf16[384,1024]{1,0:T(8,128)(2,1)S(1)}, u32[]{:S(2)}, u32[]{:S(2)}) collective-permute-start(bf16[384,1024]{1,0:T(8,128)(2,1)S(1)} %get-tuple-element.376), channel_id=1, source_target_pairs={{0,8},{4,12},{8,0},{12,4},{16,24},{20,28},{24,16},{28,20},{1,9},{5... | collective-permute-start | bytes 2359304 | tf_op jit(solution)/shard_map/ppermute | solution.py:321
  69.7 32.6 %collective-permute-start.11 = (bf16[384,1024]{1,0:T(8,128)(2,1)S(1)}, bf16[384,1024]{1,0:T(8,128)(2,1)S(1)}, u32[]{:S(2)}, u32[]{:S(2)}) collective-permute-start(bf16[384,1024]{1,0:T(8,128)(2,1)S(1)} %get-tuple-element.376), channel_id=1, source_target_pairs={{0,16},{4,20},{8,24},{12,28},{16,0},{20,4},{24,8},{28,12},{1,17},{... | collective-permute-start | bytes 2359304 | tf_op jit(solution)/shard_map/ppermute | solution.py:321
  70.2 15.3 %collective-permute-start.12 = (bf16[128,1024]{1,0:T(8,128)(2,1)S(1)}, bf16[128,1024]{1,0:T(8,128)(2,1)}, u32[]{:S(2)}, u32[]{:S(2)}) collective-permute-start(bf16[128,1024]{1,0:T(8,128)(2,1)S(1)} %get-tuple-element.181), channel_id=1, source_target_pairs={{0,1},{1,2},{2,3},{3,0},{4,5},{5,6},{6,7},{7,4},{8,9},{9,10},{10,1... | collective-permute-start | bytes 786440 | tf_op jit(solution)/shard_map/ppermute | solution.py:316
  76.3 17.8 %collective-permute-start.13 = (bf16[128,1024]{1,0:T(8,128)(2,1)S(1)}, bf16[128,1024]{1,0:T(8,128)(2,1)S(1)}, u32[]{:S(2)}, u32[]{:S(2)}) collective-permute-start(bf16[128,1024]{1,0:T(8,128)(2,1)S(1)} %get-tuple-element.181), channel_id=1, source_target_pairs={{0,2},{1,3},{2,0},{3,1},{4,6},{5,7},{6,4},{7,5},{8,10},{9,11},{10,... | collective-permute-start | bytes 786440 | tf_op jit(solution)/shard_map/ppermute | solution.py:316
  78.6 23.6 %collective-permute-start.8 = (bf16[192,1024]{1,0:T(8,128)(2,1)S(1)}, bf16[192,1024]{1,0:T(8,128)(2,1)S(1)}, u32[]{:S(2)}, u32[]{:S(2)}) collective-permute-start(bf16[192,1024]{1,0:T(8,128)(2,1)S(1)} %slice.272), channel_id=1, source_target_pairs={{0,16},{4,20},{8,24},{12,28},{16,0},{20,4},{24,8},{28,12},{1,17},{... | collective-permute-start | bytes 1179656 | tf_op jit(solution)/shard_map/ppermute | solution.py:321
  85.5 16.8 %collective-permute-start.9 = (bf16[192,1024]{1,0:T(8,128)(2,1)S(1)}, bf16[192,1024]{1,0:T(8,128)(2,1)S(1)}, u32[]{:S(2)}, u32[]{:S(2)}) collective-permute-start(bf16[192,1024]{1,0:T(8,128)(2,1)S(1)} %slice.273), channel_id=1, source_target_pairs={{0,8},{4,12},{8,0},{12,4},{16,24},{20,28},{24,16},{28,20},{1,9},{5... | collective-permute-start | bytes 1179656 | tf_op jit(solution)/shard_map/ppermute | solution.py:321
  94.0 8.2 %collective-permute-start.14 = (bf16[128,1024]{1,0:T(8,128)(2,1)S(1)}, bf16[128,1024]{1,0:T(8,128)(2,1)S(1)}, u32[]{:S(2)}, u32[]{:S(2)}) collective-permute-start(bf16[128,1024]{1,0:T(8,128)(2,1)S(1)} %get-tuple-element.181), channel_id=1, source_target_pairs={{0,3},{1,0},{2,1},{3,2},{4,7},{5,4},{6,5},{7,6},{8,11},{9,8},{10,9... | collective-permute-start | bytes 786440 | tf_op jit(solution)/shard_map/ppermute | solution.py:316
  104.0 17.1 %collective-permute-start.15 = (bf16[1536,1024]{1,0:T(8,128)(2,1)}, bf16[1536,1024]{1,0:T(8,128)(2,1)}, u32[]{:S(2)}, u32[]{:S(2)}) collective-permute-start(bf16[1536,1024]{1,0:T(8,128)(2,1)} %constant_dynamic-update-slice_fusion.4.near_ref), channel_id=1, source_target_pairs={{0,4},{4,0},{8,12},{12,8},{16,20},{20,16},{24,28},{28,24},{1,5},{5... | collective-permute-start | bytes 9437192 | tf_op jit(solution)/shard_map/ppermute | solution.py:321
  114.2 29.8 %collective-permute-start.18 = (bf16[384,1024]{1,0:T(8,128)(2,1)}, bf16[384,1024]{1,0:T(8,128)(2,1)S(1)}, u32[]{:S(2)}, u32[]{:S(2)}) collective-permute-start(bf16[384,1024]{1,0:T(8,128)(2,1)} %get-tuple-element.370), channel_id=1, source_target_pairs={{0,8},{4,12},{8,0},{12,4},{16,24},{20,28},{24,16},{28,20},{1,9},{5... | collective-permute-start | bytes 2359304 | tf_op jit(solution)/shard_map/ppermute | solution.py:321
  115.6 28.3 %collective-permute-start.19 = (bf16[384,1024]{1,0:T(8,128)(2,1)}, bf16[384,1024]{1,0:T(8,128)(2,1)S(1)}, u32[]{:S(2)}, u32[]{:S(2)}) collective-permute-start(bf16[384,1024]{1,0:T(8,128)(2,1)} %get-tuple-element.370), channel_id=1, source_target_pairs={{0,16},{4,20},{8,24},{12,28},{16,0},{20,4},{24,8},{28,12},{1,17},{... | collective-permute-start | bytes 2359304 | tf_op jit(solution)/shard_map/ppermute | solution.py:321
  117.2 26.7 %collective-permute-start.16 = (bf16[192,1024]{1,0:T(8,128)(2,1)S(1)}, bf16[192,1024]{1,0:T(8,128)(2,1)S(1)}, u32[]{:S(2)}, u32[]{:S(2)}) collective-permute-start(bf16[192,1024]{1,0:T(8,128)(2,1)S(1)} %slice.289), channel_id=1, source_target_pairs={{0,16},{4,20},{8,24},{12,28},{16,0},{20,4},{24,8},{28,12},{1,17},{... | collective-permute-start | bytes 1179656 | tf_op jit(solution)/shard_map/ppermute | solution.py:321
  118.6 25.4 %collective-permute-start.17 = (bf16[192,1024]{1,0:T(8,128)(2,1)}, bf16[192,1024]{1,0:T(8,128)(2,1)S(1)}, u32[]{:S(2)}, u32[]{:S(2)}) collective-permute-start(bf16[192,1024]{1,0:T(8,128)(2,1)} %slice.290), channel_id=1, source_target_pairs={{0,8},{4,12},{8,0},{12,4},{16,24},{20,28},{24,16},{28,20},{1,9},{5... | collective-permute-start | bytes 1179656 | tf_op jit(solution)/shard_map/ppermute | solution.py:321
  145.5 5.9 collective-permute-start.20
  145.6 12.0 %collective-permute-start.21 = (bf16[192,1024]{1,0:T(8,128)(2,1)S(1)}, bf16[192,1024]{1,0:T(8,128)(2,1)S(1)}, u32[]{:S(2)}, u32[]{:S(2)}) collective-permute-start(bf16[192,1024]{1,0:T(8,128)(2,1)S(1)} %slice.291), channel_id=1, source_target_pairs={{0,16},{4,20},{8,24},{12,28},{16,0},{20,4},{24,8},{28,12},{1,17},{... | collective-permute-start | bytes 1179656 | tf_op jit(solution)/shard_map/ppermute | solution.py:321
  147.2 11.3 %collective-permute-start.22 = (bf16[192,1024]{1,0:T(8,128)(2,1)S(1)}, bf16[192,1024]{1,0:T(8,128)(2,1)S(1)}, u32[]{:S(2)}, u32[]{:S(2)}) collective-permute-start(bf16[192,1024]{1,0:T(8,128)(2,1)S(1)} %slice.292), channel_id=1, source_target_pairs={{0,8},{4,12},{8,0},{12,4},{16,24},{20,28},{24,16},{28,20},{1,9},{5... | collective-permute-start | bytes 1179656 | tf_op jit(solution)/shard_map/ppermute | solution.py:321
  158.5 5.7 collective-permute-start.23
  189.8 133.6 %reduce-scatter.4.cloned.1.call-start = ((), (), s32[]{:S(2)}) async-start(), calls=%async_computation.4 | async-start | bytes 9437184 | tf_op jit(solution)/shard_map/reduce_scatter | solution.py:403
  254.0 116.7 %all-gather.7.cloned.1.call-start = ((), (), s32[]{:S(2)}) async-start(), calls=%async_computation.5 | async-start | bytes 5980160 | tf_op jit(solution)/shard_map/all_gather | solution.py:526
  254.7 170.4 %reduce-scatter.6.cloned.1.call-start = ((), (), s32[]{:S(2)}) async-start(), calls=%async_computation.6 | async-start | bytes 11796480 | tf_op jit(solution)/shard_map/reduce_scatter | solution.py:403
  322.2 163.3 %all-gather.9.cloned.1.call-start = ((), (), s32[]{:S(2)}) async-start(), calls=%async_computation.7 | async-start | bytes 5980160 | tf_op jit(solution)/shard_map/all_gather | solution.py:526
  364.4 136.7 %reduce-scatter.8.cloned.1.call-start = ((), (), s32[]{:S(2)}) async-start(), calls=%async_computation.8 | async-start | bytes 7077888 | tf_op jit(solution)/shard_map/reduce_scatter | solution.py:403
  365.7 58.5 %collective-permute-start.25 = (bf16[128,1024]{1,0:T(8,128)(2,1)}, bf16[128,1024]{1,0:T(8,128)(2,1)}, u32[]{:S(2)}, u32[]{:S(2)}) collective-permute-start(bf16[128,1024]{1,0:T(8,128)(2,1)} %get-tuple-element.356), channel_id=1, source_target_pairs={{0,1},{4,5},{8,9},{12,13},{16,17},{20,21},{24,25},{28,29}} | collective-permute-start | bytes 786440 | tf_op jit(solution)/shard_map/ppermute | solution.py:428
  369.3 54.9 %collective-permute-start.26 = (bf16[128,1024]{1,0:T(8,128)(2,1)}, bf16[128,1024]{1,0:T(8,128)(2,1)}, u32[]{:S(2)}, u32[]{:S(2)}) collective-permute-start(bf16[128,1024]{1,0:T(8,128)(2,1)} %get-tuple-element.355), channel_id=1, source_target_pairs={{3,2},{7,6},{11,10},{15,14},{19,18},{23,22},{27,26},{31,30}} | collective-permute-start | bytes 786440 | tf_op jit(solution)/shard_map/ppermute | solution.py:429
  424.2 184.6 %all-gather.11.cloned.1.call-start = ((), (), s32[]{:S(2)}) async-start(), calls=%async_computation.9 | async-start | bytes 5980160 | tf_op jit(solution)/shard_map/all_gather | solution.py:526
  426.3 29.4 %collective-permute-start.29 = (bf16[128,1280]{1,0:T(8,128)(2,1)S(1)}, bf16[128,1280]{1,0:T(8,128)(2,1)S(1)}, u32[]{:S(2)}, u32[]{:S(2)}) collective-permute-start(bf16[128,1280]{1,0:T(8,128)(2,1)S(1)} %get-tuple-element.350), channel_id=1, source_target_pairs={{0,1},{4,5},{8,9},{12,13},{16,17},{20,21},{24,25},{28,29}} | collective-permute-start | bytes 983048 | tf_op jit(solution)/shard_map/ppermute | solution.py:428
  427.8 28.0 %collective-permute-start.30 = (bf16[128,1280]{1,0:T(8,128)(2,1)S(1)}, bf16[128,1280]{1,0:T(8,128)(2,1)S(1)}, u32[]{:S(2)}, u32[]{:S(2)}) collective-permute-start(bf16[128,1280]{1,0:T(8,128)(2,1)S(1)} %get-tuple-element.349), channel_id=1, source_target_pairs={{3,2},{7,6},{11,10},{15,14},{19,18},{23,22},{27,26},{31,30}} | collective-permute-start | bytes 983048 | tf_op jit(solution)/shard_map/ppermute | solution.py:429
  429.7 26.1 %collective-permute-start.27 = (bf16[128,1024]{1,0:T(8,128)(2,1)S(1)}, bf16[128,1024]{1,0:T(8,128)(2,1)S(1)}, u32[]{:S(2)}, u32[]{:S(2)}) collective-permute-start(bf16[128,1024]{1,0:T(8,128)(2,1)S(1)} %get-tuple-element.354), channel_id=1, source_target_pairs={{0,1},{1,2},{4,5},{5,6},{8,9},{9,10},{12,13},{13,14},{16,17},{17,1... | collective-permute-start | bytes 786440 | tf_op jit(solution)/shard_map/ppermute | solution.py:428
  431.0 24.8 %collective-permute-start.28 = (bf16[128,1024]{1,0:T(8,128)(2,1)S(1)}, bf16[128,1024]{1,0:T(8,128)(2,1)S(1)}, u32[]{:S(2)}, u32[]{:S(2)}) collective-permute-start(bf16[128,1024]{1,0:T(8,128)(2,1)S(1)} %get-tuple-element.353), channel_id=1, source_target_pairs={{3,2},{2,1},{7,6},{6,5},{11,10},{10,9},{15,14},{14,13},{19,18},{18... | collective-permute-start | bytes 786440 | tf_op jit(solution)/shard_map/ppermute | solution.py:429
  431.7 24.1 %collective-permute-start.24 = (f32[12288]{0:T(1024)S(1)}, f32[12288]{0:T(1024)S(1)}, u32[]{:S(2)}, u32[]{:S(2)}) collective-permute-start(f32[12288]{0:T(1024)S(1)} %bitcast_dynamic-update-slice_fusion), channel_id=1, source_target_pairs={{0,1},{1,0},{2,3},{3,2},{4,5},{5,4},{6,7},{7,6},{8,9},{9,8},{10,11... | collective-permute-start | bytes 147464 | tf_op jit(solution)/shard_map/ppermute | solution.py:321
  455.9 28.0 %collective-permute-start.34 = (bf16[128,1280]{1,0:T(8,128)(2,1)S(1)}, bf16[128,1280]{1,0:T(8,128)(2,1)S(1)}, u32[]{:S(2)}, u32[]{:S(2)}) collective-permute-start(bf16[128,1280]{1,0:T(8,128)(2,1)S(1)} %get-tuple-element.348), channel_id=1, source_target_pairs={{0,1},{1,2},{4,5},{5,6},{8,9},{9,10},{12,13},{13,14},{16,17},{17,1... | collective-permute-start | bytes 983048 | tf_op jit(solution)/shard_map/ppermute | solution.py:428
  460.3 25.1 %collective-permute-start.35 = (bf16[128,1280]{1,0:T(8,128)(2,1)S(1)}, bf16[128,1280]{1,0:T(8,128)(2,1)}, u32[]{:S(2)}, u32[]{:S(2)}) collective-permute-start(bf16[128,1280]{1,0:T(8,128)(2,1)S(1)} %get-tuple-element.347), channel_id=1, source_target_pairs={{3,2},{2,1},{7,6},{6,5},{11,10},{10,9},{15,14},{14,13},{19,18},{18... | collective-permute-start | bytes 983048 | tf_op jit(solution)/shard_map/ppermute | solution.py:429
  461.9 22.0 %collective-permute-start.32 = (bf16[128,1024]{1,0:T(8,128)(2,1)S(1)}, bf16[128,1024]{1,0:T(8,128)(2,1)S(1)}, u32[]{:S(2)}, u32[]{:S(2)}) collective-permute-start(bf16[128,1024]{1,0:T(8,128)(2,1)S(1)} %get-tuple-element.352), channel_id=1, source_target_pairs={{0,1},{1,2},{2,3},{4,5},{5,6},{6,7},{8,9},{9,10},{10,11},{12,13},{... | collective-permute-start | bytes 786440 | tf_op jit(solution)/shard_map/ppermute | solution.py:428
  465.5 18.5 %collective-permute-start.33 = (bf16[128,1024]{1,0:T(8,128)(2,1)S(1)}, bf16[128,1024]{1,0:T(8,128)(2,1)S(1)}, u32[]{:S(2)}, u32[]{:S(2)}) collective-permute-start(bf16[128,1024]{1,0:T(8,128)(2,1)S(1)} %get-tuple-element.351), channel_id=1, source_target_pairs={{3,2},{2,1},{1,0},{7,6},{6,5},{5,4},{11,10},{10,9},{9,8},{15,14},{... | collective-permute-start | bytes 786440 | tf_op jit(solution)/shard_map/ppermute | solution.py:429
  466.8 17.1 %collective-permute-start.31 = (f32[12288]{0:T(1024)S(1)}, f32[12288]{0:T(1024)S(1)}, u32[]{:S(2)}, u32[]{:S(2)}) collective-permute-start(f32[12288]{0:T(1024)S(1)} %add.289), channel_id=1, source_target_pairs={{0,2},{1,3},{2,0},{3,1},{4,6},{5,7},{6,4},{7,5},{8,10},{9,11},{10,... | collective-permute-start | bytes 147464 | tf_op jit(solution)/shard_map/ppermute | solution.py:321
  487.4 20.1 %collective-permute-start.37 = (bf16[128,1024]{1,0:T(8,128)(2,1)}, bf16[128,1024]{1,0:T(8,128)(2,1)S(1)}, u32[]{:S(2)}, u32[]{:S(2)}) collective-permute-start(bf16[128,1024]{1,0:T(8,128)(2,1)} %get-tuple-element.338), channel_id=1, source_target_pairs={{0,8},{4,12},{8,0},{12,4},{16,24},{20,28},{24,16},{28,20},{1,9},{5... | collective-permute-start | bytes 786440 | tf_op jit(solution)/shard_map/ppermute | solution.py:321
  489.1 19.8 %collective-permute-start.38 = (bf16[128,1024]{1,0:T(8,128)(2,1)}, bf16[128,1024]{1,0:T(8,128)(2,1)S(1)}, u32[]{:S(2)}, u32[]{:S(2)}) collective-permute-start(bf16[128,1024]{1,0:T(8,128)(2,1)} %get-tuple-element.338), channel_id=1, source_target_pairs={{0,16},{4,20},{8,24},{12,28},{16,0},{20,4},{24,8},{28,12},{1,17},{... | collective-permute-start | bytes 786440 | tf_op jit(solution)/shard_map/ppermute | solution.py:321
  492.6 16.3 %collective-permute-start.39 = (bf16[128,1280]{1,0:T(8,128)(2,1)}, bf16[128,1280]{1,0:T(8,128)(2,1)S(1)}, u32[]{:S(2)}, u32[]{:S(2)}) collective-permute-start(bf16[128,1280]{1,0:T(8,128)(2,1)} %get-tuple-element.346), channel_id=1, source_target_pairs={{0,1},{1,2},{2,3},{4,5},{5,6},{6,7},{8,9},{9,10},{10,11},{12,13},{... | collective-permute-start | bytes 983048 | tf_op jit(solution)/shard_map/ppermute | solution.py:428
  498.9 10.0 %collective-permute-start.40 = (bf16[128,1280]{1,0:T(8,128)(2,1)}, bf16[128,1280]{1,0:T(8,128)(2,1)S(1)}, u32[]{:S(2)}, u32[]{:S(2)}) collective-permute-start(bf16[128,1280]{1,0:T(8,128)(2,1)} %get-tuple-element.345), channel_id=1, source_target_pairs={{3,2},{2,1},{1,0},{7,6},{6,5},{5,4},{11,10},{10,9},{9,8},{15,14},{... | collective-permute-start | bytes 983048 | tf_op jit(solution)/shard_map/ppermute | solution.py:429
  502.9 9.2 %collective-permute-start.41 = (bf16[128,768]{1,0:T(8,128)(2,1)S(1)}, bf16[128,768]{1,0:T(8,128)(2,1)S(1)}, u32[]{:S(2)}, u32[]{:S(2)}) collective-permute-start(bf16[128,768]{1,0:T(8,128)(2,1)S(1)} %get-tuple-element.362), channel_id=1, source_target_pairs={{0,1},{4,5},{8,9},{12,13},{16,17},{20,21},{24,25},{28,29}} | collective-permute-start | bytes 589832 | tf_op jit(solution)/shard_map/ppermute | solution.py:428
  513.9 19.2 %collective-permute-start.46 = (bf16[128,1280]{1,0:T(8,128)(2,1)S(1)}, bf16[128,1280]{1,0:T(8,128)(2,1)S(1)}, u32[]{:S(2)}, u32[]{:S(2)}) collective-permute-start(bf16[128,1280]{1,0:T(8,128)(2,1)S(1)} %get-tuple-element.334), channel_id=1, source_target_pairs={{0,8},{4,12},{8,0},{12,4},{16,24},{20,28},{24,16},{28,20},{1,9},{5... | collective-permute-start | bytes 983048 | tf_op jit(solution)/shard_map/ppermute | solution.py:321
  514.5 18.6 %collective-permute-start.47 = (bf16[128,1280]{1,0:T(8,128)(2,1)S(1)}, bf16[128,1280]{1,0:T(8,128)(2,1)S(1)}, u32[]{:S(2)}, u32[]{:S(2)}) collective-permute-start(bf16[128,1280]{1,0:T(8,128)(2,1)S(1)} %get-tuple-element.334), channel_id=1, source_target_pairs={{0,16},{4,20},{8,24},{12,28},{16,0},{20,4},{24,8},{28,12},{1,17},{... | collective-permute-start | bytes 983048 | tf_op jit(solution)/shard_map/ppermute | solution.py:321
  515.1 11.1 %collective-permute-start.44 = (bf16[64,1024]{1,0:T(8,128)(2,1)S(1)}, bf16[64,1024]{1,0:T(8,128)(2,1)S(1)}, u32[]{:S(2)}, u32[]{:S(2)}) collective-permute-start(bf16[64,1024]{1,0:T(8,128)(2,1)S(1)} %slice.305), channel_id=1, source_target_pairs={{0,16},{4,20},{8,24},{12,28},{16,0},{20,4},{24,8},{28,12},{1,17},{... | collective-permute-start | bytes 393224 | tf_op jit(solution)/shard_map/ppermute | solution.py:321
  517.5 7.1 %collective-permute-start.43 = (f32[12288]{0:T(1024)S(1)}, f32[12288]{0:T(1024)S(1)}, u32[]{:S(2)}, u32[]{:S(2)}) collective-permute-start(f32[12288]{0:T(1024)S(1)} %add.299), channel_id=1, source_target_pairs={{0,8},{4,12},{8,0},{12,4},{16,24},{20,28},{24,16},{28,20},{1,9},{5... | collective-permute-start | bytes 147464 | tf_op jit(solution)/shard_map/ppermute | solution.py:321
  520.1 13.0 %collective-permute-start.48 = (bf16[128,768]{1,0:T(8,128)(2,1)S(1)}, bf16[128,768]{1,0:T(8,128)(2,1)S(1)}, u32[]{:S(2)}, u32[]{:S(2)}) collective-permute-start(bf16[128,768]{1,0:T(8,128)(2,1)S(1)} %get-tuple-element.360), channel_id=1, source_target_pairs={{0,1},{1,2},{4,5},{5,6},{8,9},{9,10},{12,13},{13,14},{16,17},{17,1... | collective-permute-start | bytes 589832 | tf_op jit(solution)/shard_map/ppermute | solution.py:428
  524.6 8.6 %collective-permute-start.49 = (bf16[128,768]{1,0:T(8,128)(2,1)S(1)}, bf16[128,768]{1,0:T(8,128)(2,1)S(1)}, u32[]{:S(2)}, u32[]{:S(2)}) collective-permute-start(bf16[128,768]{1,0:T(8,128)(2,1)S(1)} %get-tuple-element.359), channel_id=1, source_target_pairs={{3,2},{2,1},{7,6},{6,5},{11,10},{10,9},{15,14},{14,13},{19,18},{18... | collective-permute-start | bytes 589832 | tf_op jit(solution)/shard_map/ppermute | solution.py:429
  534.1 33.3 %collective-permute-start.51 = (bf16[512,1024]{1,0:T(8,128)(2,1)S(1)}, bf16[512,1024]{1,0:T(8,128)(2,1)S(1)}, u32[]{:S(2)}, u32[]{:S(2)}) collective-permute-start(bf16[512,1024]{1,0:T(8,128)(2,1)S(1)} %constant_dynamic-update-slice_fusion.29.near_ref), channel_id=1, source_target_pairs={{0,4},{4,0},{8,12},{12,8},{16,20},{20,16},{24,28},{28,24},{1,5},{5... | collective-permute-start | bytes 3145736 | tf_op jit(solution)/shard_map/ppermute | solution.py:321
  535.5 30.1 %collective-permute-start.54 = (bf16[128,768]{1,0:T(8,128)(2,1)S(1)}, bf16[128,768]{1,0:T(8,128)(2,1)S(1)}, u32[]{:S(2)}, u32[]{:S(2)}) collective-permute-start(bf16[128,768]{1,0:T(8,128)(2,1)S(1)} %get-tuple-element.358), channel_id=1, source_target_pairs={{0,1},{1,2},{2,3},{4,5},{5,6},{6,7},{8,9},{9,10},{10,11},{12,13},{... | collective-permute-start | bytes 589832 | tf_op jit(solution)/shard_map/ppermute | solution.py:428
  550.2 17.2 %collective-permute-start.55 = (bf16[128,768]{1,0:T(8,128)(2,1)S(1)}, bf16[128,768]{1,0:T(8,128)(2,1)S(1)}, u32[]{:S(2)}, u32[]{:S(2)}) collective-permute-start(bf16[128,768]{1,0:T(8,128)(2,1)S(1)} %get-tuple-element.357), channel_id=1, source_target_pairs={{3,2},{2,1},{1,0},{7,6},{6,5},{5,4},{11,10},{10,9},{9,8},{15,14},{... | collective-permute-start | bytes 589832 | tf_op jit(solution)/shard_map/ppermute | solution.py:429
  552.4 8.5 %collective-permute-start.52 = (bf16[64,1280]{1,0:T(8,128)(2,1)S(1)}, bf16[64,1280]{1,0:T(8,128)(2,1)S(1)}, u32[]{:S(2)}, u32[]{:S(2)}) collective-permute-start(bf16[64,1280]{1,0:T(8,128)(2,1)S(1)} %slice.309), channel_id=1, source_target_pairs={{0,16},{4,20},{8,24},{12,28},{16,0},{20,4},{24,8},{28,12},{1,17},{... | collective-permute-start | bytes 491528 | tf_op jit(solution)/shard_map/ppermute | solution.py:321
  552.5 7.4 %collective-permute-start.50 = (f32[12288]{0:T(1024)S(1)}, f32[12288]{0:T(1024)S(1)}, u32[]{:S(2)}, u32[]{:S(2)}) collective-permute-start(f32[12288]{0:T(1024)S(1)} %add.304), channel_id=1, source_target_pairs={{0,16},{4,20},{8,24},{12,28},{16,0},{20,4},{24,8},{28,12},{1,17},{... | collective-permute-start | bytes 147464 | tf_op jit(solution)/shard_map/ppermute | solution.py:321
  570.1 17.4 %collective-permute-start.57 = (bf16[128,768]{1,0:T(8,128)(2,1)}, bf16[128,768]{1,0:T(8,128)(2,1)S(1)}, u32[]{:S(2)}, u32[]{:S(2)}) collective-permute-start(bf16[128,768]{1,0:T(8,128)(2,1)} %get-tuple-element.336), channel_id=1, source_target_pairs={{0,8},{4,12},{8,0},{12,4},{16,24},{20,28},{24,16},{28,20},{1,9},{5... | collective-permute-start | bytes 589832 | tf_op jit(solution)/shard_map/ppermute | solution.py:321
  570.1 17.4 %collective-permute-start.58 = (bf16[128,768]{1,0:T(8,128)(2,1)}, bf16[128,768]{1,0:T(8,128)(2,1)S(1)}, u32[]{:S(2)}, u32[]{:S(2)}) collective-permute-start(bf16[128,768]{1,0:T(8,128)(2,1)} %get-tuple-element.336), channel_id=1, source_target_pairs={{0,16},{4,20},{8,24},{12,28},{16,0},{20,4},{24,8},{28,12},{1,17},{... | collective-permute-start | bytes 589832 | tf_op jit(solution)/shard_map/ppermute | solution.py:321
  577.6 9.9 %collective-permute-start.56 = (bf16[512,1280]{1,0:T(8,128)(2,1)S(1)}, bf16[512,1280]{1,0:T(8,128)(2,1)S(1)}, u32[]{:S(2)}, u32[]{:S(2)}) collective-permute-start(bf16[512,1280]{1,0:T(8,128)(2,1)S(1)} %constant_dynamic-update-slice_fusion.34.near_ref), channel_id=1, source_target_pairs={{0,4},{4,0},{8,12},{12,8},{16,20},{20,16},{24,28},{28,24},{1,5},{5... | collective-permute-start | bytes 3932168 | tf_op jit(solution)/shard_map/ppermute | solution.py:321
  591.8 13.5 %collective-permute-start.59 = (bf16[64,768]{1,0:T(8,128)(2,1)S(1)}, bf16[64,768]{1,0:T(8,128)(2,1)S(1)}, u32[]{:S(2)}, u32[]{:S(2)}) collective-permute-start(bf16[64,768]{1,0:T(8,128)(2,1)S(1)} %slice.311), channel_id=1, source_target_pairs={{0,16},{4,20},{8,24},{12,28},{16,0},{20,4},{24,8},{28,12},{1,17},{... | collective-permute-start | bytes 294920 | tf_op jit(solution)/shard_map/ppermute | solution.py:321
  593.9 11.4 %collective-permute-start.60 = (bf16[64,768]{1,0:T(8,128)(2,1)S(1)}, bf16[64,768]{1,0:T(8,128)(2,1)S(1)}, u32[]{:S(2)}, u32[]{:S(2)}) collective-permute-start(bf16[64,768]{1,0:T(8,128)(2,1)S(1)} %slice.312), channel_id=1, source_target_pairs={{0,8},{4,12},{8,0},{12,4},{16,24},{20,28},{24,16},{28,20},{1,9},{5... | collective-permute-start | bytes 294920 | tf_op jit(solution)/shard_map/ppermute | solution.py:321
  (115 other events, 1059.0 us)
Sparse Core Ops, SparseCore 0:
  189.9 88.6 all-gather.4
  280.7 88.9 all-gather.6
  371.9 108.7 all-gather.8
  509.0 95.3 all-gather.10
Sparse Core Ops, SparseCore 1:
  254.1 69.3 reduce-scatter.3
  327.2 81.3 reduce-scatter.5
  424.3 60.1 reduce-scatter.7
